TPU v7x, 32 devices: a whole 2x2x4 slice. The times are simulated.
32 devices in a mesh: groups: 2 (over y), chan: 4 (over z), day: 2 (over x), sub: 2 (over core).
Axes of the slice: x: 2, y: 2, z: 4, core: 2. Of those that a mesh axis runs over, the one named last changes fastest.
Arguments:
- spectra: bfloat16 [4, 16, 128, 2, 512], P(('groups', 'day'), 'sub', 'chan'), parts along dimension 0, may hold values from -6 to 6
- tile_offset: int32 [4, 3], P('chan'), may hold values from -1 to 3, as said below
- pair_reach: int32 [4, 3], P('chan'), may hold values from 0 to 128, as said below
Outputs:
- correlations: float32 [8, 3, 32, 32, 256], P(('groups', 'chan'), None, ('day', 'sub')), parts along dimension 0
There are 2 independent parts, one for each index of `groups`. A program takes and returns all parts, laid end to end along the dimension named above; an argument that names none is the same for every part. Nothing has to cross between parts.
Inputs may be any that keep to these rules, and one draw needn't show every extreme that they name: `tile_offset`: in row a the first 1 to 3 slots hold distinct offsets s with a + s < 4, the rest hold -1; row 0 is full and holds 3. `pair_reach`: A slot with offset s holds a value from max(2, (s - 1) * 32 + 2) to (s + 1) * 32; a padding slot holds 0.
All inputs are finite; a program needn't handle non-finite values.
Results may differ from a plain program's by a relative error of at most 0.004.
Values may be sent and summed in bfloat16 or wider, within the bound.
No kernel may reach another device: no remote copies, remote signals or barrier semaphores. Data moves between devices by JAX's collectives and lax.ppermute only.
A program may use at most 128 MiB of HBM per device.

v0:
```python
import math

import jax
import jax.numpy as jnp
from jax import lax
from jax.sharding import PartitionSpec as P

BAND = 32
LAGS = 256


EPSILON = 1e-06


def shifted(value, axis, steps):
    count = lax.axis_size(axis)
    initial, last = (max(0, -steps), min(count, count - steps))
    return lax.ppermute(value, axis, [(source, source + steps) for source in range(initial, last)])


def whiten(spectra_in):
    values = spectra_in.astype(jnp.float32)
    power_sum = values[..., 0, :] ** 2 + values[..., 1, :] ** 2
    power_shape = power_sum.shape
    banded = power_sum.reshape(power_shape[:-1] + (power_shape[-1] // BAND, BAND))
    band_scale = lax.rsqrt(jnp.mean(banded, axis=-1, keepdims=True) + EPSILON)
    band_scale = jnp.broadcast_to(band_scale, banded.shape).reshape(power_shape)
    return (values * band_scale[..., None, :]).astype(jnp.bfloat16)


def lag_table(bin_count, lag_count):
    bin_index = jnp.arange(bin_count, dtype=jnp.float32)
    lag_index = jnp.arange(lag_count, dtype=jnp.float32) - lag_count // 2
    angle_table = math.pi * bin_index[:, None] * lag_index[None, :] / bin_count
    return jnp.concatenate([jnp.cos(angle_table), -jnp.sin(angle_table)], axis=0)


def lag_tile(own_rows, own_turned, partners, offset, reach_now, table, norm_scale):
    partner = lax.dynamic_index_in_dim(partners, jnp.maximum(offset, 0), 0, keepdims=False)
    real_part = jnp.einsum(
        "dwicf,dwjcf->ijf", own_rows, partner, preferred_element_type=jnp.float32
    )
    imag_part = jnp.einsum(
        "dwicf,dwjcf->ijf", own_turned, partner, preferred_element_type=jnp.float32
    )
    row_count, block_width, bin_count = real_part.shape
    joined = jnp.concatenate([real_part, imag_part], axis=2).reshape(
        row_count * block_width, 2 * bin_count
    )
    lagged = jnp.dot(
        joined, table, precision=lax.Precision.HIGHEST, preferred_element_type=jnp.float32
    )
    lagged = lagged.reshape(row_count, block_width, -1) * norm_scale
    row_index = jnp.arange(row_count, dtype=jnp.int32)
    col_index = jnp.arange(block_width, dtype=jnp.int32)
    distance_abs = jnp.abs(offset * block_width + col_index[None, :] - row_index[:, None])
    keep_mask = (offset >= 0) & (distance_abs > 0) & (distance_abs < reach_now)
    return jnp.where(keep_mask[:, :, None], lagged, jnp.float32(0.0))


def on_device(spectra, tile_offset, pair_reach):
    white = whiten(spectra)
    steps_ahead = min(4, lax.axis_size("chan") - 1)
    held_blocks = [white]
    moving = white
    for step_index in range(steps_ahead):
        moving = shifted(moving, "chan", -1)
        held_blocks.append(moving)
    partners = jnp.stack(held_blocks)
    bin_count = white.shape[4]
    tile_count = tile_offset.shape[1]
    total_windows = white.shape[0] * lax.axis_size("day") * white.shape[1] * lax.axis_size("sub")
    norm_scale = 1.0 / math.sqrt(bin_count * total_windows)
    table = lag_table(bin_count, LAGS)
    offsets = tile_offset[0]
    reaches = pair_reach[0]
    own_turned = jnp.stack([white[:, :, :, 1, :], -white[:, :, :, 0, :]], axis=3)
    results = []
    for slot_index in range(tile_count):
        offset = offsets[slot_index]
        reach_now = reaches[slot_index]
        tile_lags = lag_tile(white, own_turned, partners, offset, reach_now, table, norm_scale)
        results.append(tile_lags)
    summed = lax.psum_scatter(
        jnp.stack(results, axis=1), ("day", "sub"), scatter_dimension=0, tiled=True
    )
    return jnp.transpose(summed, (1, 0, 2, 3))[None]


def solution(mesh):
    in_specs = (P(("groups", "day"), "sub", "chan", None, None), P("chan", None), P("chan", None))
    out_specs = P(("groups", "chan"), None, ("day", "sub"), None, None)
    return jax.shard_map(
        on_device, mesh=mesh, in_specs=in_specs, out_specs=out_specs, check_vma=False
    )
```

profile of v0, /device:TPU:0, one launch (start us, length us, event | category | flops | bytes accessed | tf_op | source)
XLA Modules:
  0.0 205.1 jit_solution(5847267953984372399)
XLA Ops:
  6.5 1.2 copy_convert_fusion
  10.6 1.3 collective-permute-start
  18.5 9.0 %collective-permute-done = bf16[1,8,32,2,512]{4,2,3,1,0:T(8,128)(2,1)S(1)} collective-permute-done((bf16[1,8,32,2,512]{4,2,3,1,0:T(8,128)(2,1)S(1)}, bf16[1,8,32,2,512]{4,2,3,1,0:T(8,128)(2,1)S(1)}, u32[]{:S(2)}, u32[]{:S(2)}) %collective-permute-start) | collective-permute-done | bytes 524320 | tf_op jit(solution)/shard_map/ppermute | solution.py:18
  27.5 1.3 collective-permute-start.1
  31.0 11.6 %collective-permute-done.1 = bf16[1,8,32,2,512]{4,2,3,1,0:T(8,128)(2,1)} collective-permute-done((bf16[1,8,32,2,512]{4,2,3,1,0:T(8,128)(2,1)S(1)}, bf16[1,8,32,2,512]{4,2,3,1,0:T(8,128)(2,1)}, u32[]{:S(2)}, u32[]{:S(2)}) %collective-permute-start.1) | collective-permute-done | bytes 524320 | tf_op jit(solution)/shard_map/ppermute | solution.py:18
  42.6 1.5 collective-permute-start.2
  45.9 2.9 %copy.12 = bf16[1,8,32,2,512]{2,1,3,4,0:T(8,128)(2,1)S(1)} copy(bf16[1,8,32,2,512]{4,2,3,1,0:T(8,128)(2,1)} %pad_maximum_fusion.2) | data formatting | bytes 1048576 | tf_op jit(solution)/shard_map/stack | solution.py:77
  48.8 3.8 %copy.11 = bf16[8,32,2,512]{1,0,2,3:T(8,128)(2,1)} copy(bf16[8,32,2,512]{3,1,2,0:T(8,128)(2,1)} %fusion.71) | data formatting | bytes 1048576 | tf_op jit(solution)/shard_map/reshape.14
  52.6 3.1 %fusion.49 = (f32[512,256]{1,0:T(8,128)}, f32[512,256]{1,0:T(8,128)}) fusion(f32[256]{0:T(256)S(1)} %iota_add_fusion, f32[512]{0:T(512)S(1)} %iota_multiply_fusion), kind=kLoop, calls=%fused_computation.48 | loop fusion | flops 393216 | bytes 1051648 | tf_op jit(solution)/shard_map/cos | solution.py:35
  55.8 1.2 collective-permute-done.2
  57.0 1.5 pad_maximum_fusion.1
  59.4 3.7 %copy.10 = bf16[1,1,8,32,2,512]{3,2,4,5,1,0:T(8,128)(2,1)} copy(bf16[1,1,8,32,2,512]{5,3,4,2,1,0:T(8,128)(2,1)} %get-tuple-element.5) | data formatting | bytes 1048576 | tf_op jit(solution)/shard_map/jit(dynamic_index_in_dim)/dynamic_slice | solution.py:39
  63.1 6.5 %convolution_bitcast_fusion.4 = f32[32,32,512]{0,1,2:T(8,128)} fusion(bf16[1,8,32,2,512]{2,1,3,4,0:T(8,128)(2,1)S(1)} %copy.12, bf16[1,1,8,32,2,512]{3,2,4,5,1,0:T(8,128)(2,1)} %copy.10), kind=kOutput, calls=%fused_computation.16 | convolution fusion | flops 16777216 | bytes 3145728 | tf_op jit(solution)/shard_map/dwicf,dwjcf->ijf/dot_general | solution.py:43
  69.6 4.1 %convolution_bitcast_fusion.5 = f32[32,32,512]{0,1,2:T(8,128)} fusion(bf16[8,32,2,512]{1,0,2,3:T(8,128)(2,1)S(1)} %copy-done, bf16[1,1,8,32,2,512]{3,2,4,5,1,0:T(8,128)(2,1)S(1)} %copy-done.4), kind=kOutput, calls=%fused_computation.17 | convolution fusion | flops 16777216 | bytes 3145728 | tf_op jit(solution)/shard_map/dwicf,dwjcf->ijf/dot_general | solution.py:40
  73.7 2.8 %copy.15 = bf16[1,1,8,32,2,512]{3,2,4,5,1,0:T(8,128)(2,1)} copy(bf16[1,1,8,32,2,512]{5,3,4,2,1,0:T(8,128)(2,1)S(1)} %get-tuple-element.7) | data formatting | bytes 1048576 | tf_op jit(solution)/shard_map/jit(dynamic_index_in_dim)/dynamic_slice | solution.py:39
  76.5 6.5 %convolution_bitcast_fusion.2 = f32[32,32,512]{0,1,2:T(8,128)} fusion(bf16[1,1,8,32,2,512]{3,2,4,5,1,0:T(8,128)(2,1)} %copy.15, bf16[1,8,32,2,512]{2,1,3,4,0:T(8,128)(2,1)S(1)} %copy.12), kind=kOutput, calls=%fused_computation.14 | convolution fusion | flops 16777216 | bytes 3145728 | tf_op jit(solution)/shard_map/dwicf,dwjcf->ijf/dot_general | solution.py:43
  83.0 4.1 %convolution_bitcast_fusion.3 = f32[32,32,512]{0,1,2:T(8,128)} fusion(bf16[8,32,2,512]{1,0,2,3:T(8,128)(2,1)S(1)} %copy-done.1, bf16[1,1,8,32,2,512]{3,2,4,5,1,0:T(8,128)(2,1)S(1)} %copy-done.5), kind=kOutput, calls=%fused_computation.15 | convolution fusion | flops 16777216 | bytes 3145728 | tf_op jit(solution)/shard_map/dwicf,dwjcf->ijf/dot_general | solution.py:40
  87.0 2.8 %copy.19 = bf16[1,1,8,32,2,512]{3,2,4,5,1,0:T(8,128)(2,1)} copy(bf16[1,1,8,32,2,512]{5,3,4,2,1,0:T(8,128)(2,1)S(1)} %get-tuple-element.6) | data formatting | bytes 1048576 | tf_op jit(solution)/shard_map/jit(dynamic_index_in_dim)/dynamic_slice | solution.py:39
  89.8 6.5 %convolution_bitcast_fusion = f32[32,32,512]{0,1,2:T(8,128)} fusion(bf16[1,1,8,32,2,512]{3,2,4,5,1,0:T(8,128)(2,1)} %copy.19, bf16[1,8,32,2,512]{2,1,3,4,0:T(8,128)(2,1)S(1)} %copy.12), kind=kOutput, calls=%fused_computation.12 | convolution fusion | flops 16777216 | bytes 3145728 | tf_op jit(solution)/shard_map/dwicf,dwjcf->ijf/dot_general | solution.py:43
  96.3 4.1 %convolution_bitcast_fusion.1 = f32[32,32,512]{0,1,2:T(8,128)} fusion(bf16[8,32,2,512]{1,0,2,3:T(8,128)(2,1)S(1)} %copy-done.2, bf16[1,1,8,32,2,512]{3,2,4,5,1,0:T(8,128)(2,1)S(1)} %copy-done.3), kind=kOutput, calls=%fused_computation.13 | convolution fusion | flops 16777216 | bytes 3145728 | tf_op jit(solution)/shard_map/dwicf,dwjcf->ijf/dot_general | solution.py:40
  100.4 6.6 %copy.14 = f32[32,32,512]{2,1,0:T(8,128)} copy(f32[32,32,512]{0,1,2:T(8,128)} %convolution_bitcast_fusion.4) | data formatting | bytes 4194304 | tf_op jit(solution)/shard_map/dwicf,dwjcf->ijf/transpose | solution.py:43
  107.0 6.6 %copy.13 = f32[32,32,512]{2,1,0:T(8,128)} copy(f32[32,32,512]{0,1,2:T(8,128)} %convolution_bitcast_fusion.5) | data formatting | bytes 4194304 | tf_op jit(solution)/shard_map/dwicf,dwjcf->ijf/transpose | solution.py:40
  113.6 6.7 %copy.18 = f32[32,32,512]{2,1,0:T(8,128)} copy(f32[32,32,512]{0,1,2:T(8,128)} %convolution_bitcast_fusion.2) | data formatting | bytes 4194304 | tf_op jit(solution)/shard_map/dwicf,dwjcf->ijf/transpose | solution.py:43
  120.3 6.6 %copy.17 = f32[32,32,512]{2,1,0:T(8,128)} copy(f32[32,32,512]{0,1,2:T(8,128)} %convolution_bitcast_fusion.3) | data formatting | bytes 4194304 | tf_op jit(solution)/shard_map/dwicf,dwjcf->ijf/transpose | solution.py:40
  126.8 5.8 %copy.22 = f32[32,32,512]{2,1,0:T(8,128)S(1)} copy(f32[32,32,512]{0,1,2:T(8,128)} %convolution_bitcast_fusion) | data formatting | bytes 4194304 | tf_op jit(solution)/shard_map/dwicf,dwjcf->ijf/transpose | solution.py:43
  132.7 6.8 %copy.21 = f32[32,32,512]{2,1,0:T(8,128)} copy(f32[32,32,512]{0,1,2:T(8,128)} %convolution_bitcast_fusion.1) | data formatting | bytes 4194304 | tf_op jit(solution)/shard_map/dwicf,dwjcf->ijf/transpose | solution.py:40
  139.5 5.7 %fusion.33 = f32[32,1,32,256]{3,2,0,1:T(8,128)S(1)} fusion(f32[32,32,512]{2,1,0:T(8,128)} %copy.14, f32[32,32,512]{2,1,0:T(8,128)} %copy.13, f32[512,256]{1,0:T(8,128)S(1)} %copy-done.11, f32[512,256]{1,0:T(8,128)S(1)} %copy-done.10, pred[32,32]{1,0:T(8,128)(4,1)S(1)} %fusion.57), kind=kOutput, calls=%fused_computation.33 | convolution fusion | flops 3223060480 | bytes 6292480 | tf_op jit(solution)/shard_map/dot_general | solution.py:50
  145.2 3.4 %fusion.39 = f32[32,1,32,256]{3,2,0,1:T(8,128)S(1)} fusion(f32[32,32,512]{2,1,0:T(8,128)S(1)} %copy-done.8, f32[32,32,512]{2,1,0:T(8,128)S(1)} %copy-done.9, f32[512,256]{1,0:T(8,128)S(1)} %copy-done.11, f32[512,256]{1,0:T(8,128)S(1)} %copy-done.10, pred[32,32]{1,0:T(8,128)(4,1)S(1)} %fusion.59), kind=kOutput, calls=%fused_computation.35 | convolution fusion | flops 3223060480 | bytes 6292480 | tf_op jit(solution)/shard_map/dot_general | solution.py:50
  148.7 3.4 %fusion.45 = f32[32,1,32,256]{3,2,0,1:T(8,128)S(1)} fusion(f32[32,32,512]{2,1,0:T(8,128)S(1)} %copy.22, f32[32,32,512]{2,1,0:T(8,128)S(1)} %copy-done.7, f32[512,256]{1,0:T(8,128)S(1)} %copy-done.11, f32[512,256]{1,0:T(8,128)S(1)} %copy-done.10, pred[32,32]{1,0:T(8,128)(4,1)S(1)} %fusion.61), kind=kOutput, calls=%fused_computation.37 | convolution fusion | flops 3223060480 | bytes 6292480 | tf_op jit(solution)/shard_map/dot_general | solution.py:50
  152.7 3.5 %copy.31 = f32[4,8,96,256]{3,1,2,0:T(8,128)} copy(f32[4,8,96,256]{3,2,1,0:T(8,128)S(1)} %bitcast.106) | data formatting | bytes 6291456
  156.2 39.7 %reduce-scatter.5.cloned.1.call-done = f32[8,24576]{1,0:T(8,128)} async-done(((f32[32,24576]{1,0:T(8,128)}), f32[8,24576]{1,0:T(8,128)}) %reduce-scatter.5.cloned.1.call-update) | async-done | bytes 786448
  196.0 1.4 copy.32
  (59 shorter events, 10.5 us)
Async XLA Ops:
  6.5 189.4 %reduce-scatter.5.cloned.1.call-start = ((), (), s32[]{:S(2)}) async-start(), calls=%async_computation.1 | async-start | bytes 3932160
  9.0 1.5 copy-start.6
  9.6 2.4 %copy-start.14 = (s32[1,3]{1,0:T(1,128)S(1)}, s32[1,3]{1,0:T(1,128)}, u32[]{:S(2)}) copy-start(s32[1,3]{1,0:T(1,128)} %param.4) | copy-start | bytes 40
  9.7 5.4 %copy-start.15 = (s32[1,3]{1,0:T(1,128)S(1)}, s32[1,3]{1,0:T(1,128)}, u32[]{:S(2)}) copy-start(s32[1,3]{1,0:T(1,128)} %param.5) | copy-start | bytes 40
  10.6 16.8 %collective-permute-start = (bf16[1,8,32,2,512]{4,2,3,1,0:T(8,128)(2,1)S(1)}, bf16[1,8,32,2,512]{4,2,3,1,0:T(8,128)(2,1)S(1)}, u32[]{:S(2)}, u32[]{:S(2)}) collective-permute-start(bf16[1,8,32,2,512]{4,2,3,1,0:T(8,128)(2,1)S(1)} %multiply_convert_fusion), channel_id=1, source_target_pairs={{4,0},{8,4},{12,8},{5,1},{9,5},{13,9},{6,2},{10,6},{14,10},{7,3},{... | collective-permute-start | bytes 1572872 | tf_op jit(solution)/shard_map/ppermute | solution.py:18
  27.5 17.9 %copy-start.12 = (bf16[1,8,32,2,512]{4,2,3,1,0:T(8,128)(2,1)}, bf16[1,8,32,2,512]{4,2,3,1,0:T(8,128)(2,1)S(1)}, u32[]{:S(2)}) copy-start(bf16[1,8,32,2,512]{4,2,3,1,0:T(8,128)(2,1)S(1)} %collective-permute-done) | copy-start | bytes 1572868
  27.5 15.1 %collective-permute-start.1 = (bf16[1,8,32,2,512]{4,2,3,1,0:T(8,128)(2,1)S(1)}, bf16[1,8,32,2,512]{4,2,3,1,0:T(8,128)(2,1)}, u32[]{:S(2)}, u32[]{:S(2)}) collective-permute-start(bf16[1,8,32,2,512]{4,2,3,1,0:T(8,128)(2,1)S(1)} %collective-permute-done), channel_id=1, source_target_pairs={{4,0},{8,4},{12,8},{5,1},{9,5},{13,9},{6,2},{10,6},{14,10},{7,3},{... | collective-permute-start | bytes 1572872 | tf_op jit(solution)/shard_map/ppermute | solution.py:18
  42.6 14.4 %collective-permute-start.2 = (bf16[1,8,32,2,512]{4,2,3,1,0:T(8,128)(2,1)}, bf16[1,8,32,2,512]{4,2,3,1,0:T(8,128)(2,1)}, u32[]{:S(2)}, u32[]{:S(2)}) collective-permute-start(bf16[1,8,32,2,512]{4,2,3,1,0:T(8,128)(2,1)} %collective-permute-done.1), channel_id=1, source_target_pairs={{4,0},{8,4},{12,8},{5,1},{9,5},{13,9},{6,2},{10,6},{14,10},{7,3},{... | collective-permute-start | bytes 1572872 | tf_op jit(solution)/shard_map/ppermute | solution.py:18
  52.6 4.4 %copy-start.13 = (bf16[1,8,32,2,512]{4,2,3,1,0:T(8,128)(2,1)S(1)}, bf16[1,8,32,2,512]{4,2,3,1,0:T(8,128)(2,1)}, u32[]{:S(2)}) copy-start(bf16[1,8,32,2,512]{4,2,3,1,0:T(8,128)(2,1)} %copy-done.12) | copy-start | bytes 1572868
  63.1 6.5 %copy-start = (bf16[8,32,2,512]{1,0,2,3:T(8,128)(2,1)S(1)}, bf16[8,32,2,512]{1,0,2,3:T(8,128)(2,1)}, u32[]{:S(2)}) copy-start(bf16[8,32,2,512]{1,0,2,3:T(8,128)(2,1)} %copy.11) | copy-start | bytes 1572868
  63.1 6.5 %copy-start.4 = (bf16[1,1,8,32,2,512]{3,2,4,5,1,0:T(8,128)(2,1)S(1)}, bf16[1,1,8,32,2,512]{3,2,4,5,1,0:T(8,128)(2,1)}, u32[]{:S(2)}) copy-start(bf16[1,1,8,32,2,512]{3,2,4,5,1,0:T(8,128)(2,1)} %copy.10) | copy-start | bytes 1572868
  76.5 6.5 %copy-start.1 = (bf16[8,32,2,512]{1,0,2,3:T(8,128)(2,1)S(1)}, bf16[8,32,2,512]{1,0,2,3:T(8,128)(2,1)}, u32[]{:S(2)}) copy-start(bf16[8,32,2,512]{1,0,2,3:T(8,128)(2,1)} %copy.11) | copy-start | bytes 1572868
  76.5 6.5 %copy-start.5 = (bf16[1,1,8,32,2,512]{3,2,4,5,1,0:T(8,128)(2,1)S(1)}, bf16[1,1,8,32,2,512]{3,2,4,5,1,0:T(8,128)(2,1)}, u32[]{:S(2)}) copy-start(bf16[1,1,8,32,2,512]{3,2,4,5,1,0:T(8,128)(2,1)} %copy.15) | copy-start | bytes 1572868
  89.8 6.5 %copy-start.2 = (bf16[8,32,2,512]{1,0,2,3:T(8,128)(2,1)S(1)}, bf16[8,32,2,512]{1,0,2,3:T(8,128)(2,1)}, u32[]{:S(2)}) copy-start(bf16[8,32,2,512]{1,0,2,3:T(8,128)(2,1)} %copy.11) | copy-start | bytes 1572868
  89.8 6.5 %copy-start.3 = (bf16[1,1,8,32,2,512]{3,2,4,5,1,0:T(8,128)(2,1)S(1)}, bf16[1,1,8,32,2,512]{3,2,4,5,1,0:T(8,128)(2,1)}, u32[]{:S(2)}) copy-start(bf16[1,1,8,32,2,512]{3,2,4,5,1,0:T(8,128)(2,1)} %copy.19) | copy-start | bytes 1572868
  132.6 6.8 %copy-start.10 = (f32[512,256]{1,0:T(8,128)S(1)}, f32[512,256]{1,0:T(8,128)}, u32[]{:S(2)}) copy-start(f32[512,256]{1,0:T(8,128)} %get-tuple-element.10) | copy-start | bytes 1572868
  132.7 6.8 %copy-start.11 = (f32[512,256]{1,0:T(8,128)S(1)}, f32[512,256]{1,0:T(8,128)}, u32[]{:S(2)}) copy-start(f32[512,256]{1,0:T(8,128)} %get-tuple-element.11) | copy-start | bytes 1572868
  139.4 5.7 %copy-start.8 = (f32[32,32,512]{2,1,0:T(8,128)S(1)}, f32[32,32,512]{2,1,0:T(8,128)}, u32[]{:S(2)}) copy-start(f32[32,32,512]{2,1,0:T(8,128)} %copy.18) | copy-start | bytes 6291460
  139.4 5.8 %copy-start.9 = (f32[32,32,512]{2,1,0:T(8,128)S(1)}, f32[32,32,512]{2,1,0:T(8,128)}, u32[]{:S(2)}) copy-start(f32[32,32,512]{2,1,0:T(8,128)} %copy.17) | copy-start | bytes 6291460
  145.2 3.5 %copy-start.7 = (f32[32,32,512]{2,1,0:T(8,128)S(1)}, f32[32,32,512]{2,1,0:T(8,128)}, u32[]{:S(2)}) copy-start(f32[32,32,512]{2,1,0:T(8,128)} %copy.21) | copy-start | bytes 6291460
Sparse Core Ops, SparseCore 0:
  156.4 39.5 reduce-scatter.4
where the time goes:
time: 206 us; the launch traced here: 205 us
  local copies, waits for them, and re-layouts  65.5 us (32%)
  waiting for transfers between devices  61.5 us (30%)
  matrix products  44.2 us (21%)
  between operations  19.3 us (9%)
  other arithmetic  10.6 us (5%)
  starting transfers between devices  4.04 us (2%)
    unnamed x2, waiting for transfers between devices  39.7 us
    ppermute x3, waiting for transfers between devices, shifted(): lax.ppermute(value, axis, [(source, source + steps) for source in range(i...  21.8 us
    transpose x3, local copies, waits for them, and re-layouts, lag_tile(): jnp.einsum('dwicf,dwjcf->ijf', own_rows, partner, preferred_element_type=...  20 us
    dot_general x3, matrix products, lag_tile(): jnp.einsum('dwicf,dwjcf->ijf', own_turned, partner, preferred_element_typ...  19.4 us
    transpose x3, local copies, waits for them, and re-layouts, lag_tile(): jnp.einsum('dwicf,dwjcf->ijf', own_turned, partner, preferred_element_typ...  19.1 us
    dot_general x3, matrix products, lag_tile(): jnp.dot(joined, table, precision=lax.Precision.HIGHEST, preferred_element...  12.6 us
    dot_general x3, matrix products, lag_tile(): jnp.einsum('dwicf,dwjcf->ijf', own_rows, partner, preferred_element_type=...  12.2 us
    dynamic_slice x4, local copies, waits for them, and re-layouts, lag_tile(): lax.dynamic_index_in_dim(partners, jnp.maximum(offset, 0), 0, keepdims=Fa...  10.3 us
  transfers between devices with their start and end apart: 4, of which 4 were waited for; matrix products, arithmetic and copies ran while one was open for 7% of the time, Pallas kernels for 0%

commit v1 on v0

v1 whole, which is shorter than its diff:
```python
import functools
import math

import jax
import jax.numpy as jnp
import ml_dtypes
import numpy as np
from jax import lax
from jax.experimental import pallas as pl
from jax.experimental.pallas import tpu as pltpu
from jax.sharding import PartitionSpec as P

BAND = 32
LAGS = 256
MAX_STEPS = 4
EPSILON = 1e-06
LANES = 128
ROWS = 16
OWN = 4
VMEM_LIMIT = 40 << 20


def lag_table(bin_count):
    bins = np.arange(bin_count, dtype=np.float64)[:, None]
    lags = np.arange(LAGS, dtype=np.float64)[None, :] - LAGS // 2
    angle = np.pi * bins * lags / bin_count
    table = np.concatenate([np.cos(angle), -np.sin(angle)], axis=0).astype(np.float32)
    return table.astype(ml_dtypes.bfloat16)


def whiten_into(source, target, as_row):
    source_ref, begin = source
    _, windows, channels, bins = source_ref.shape
    width = 2 * LANES
    row = lax.broadcasted_iota(jnp.int32, (width, width), 0) // BAND
    col = lax.broadcasted_iota(jnp.int32, (width, width), 1) // BAND
    mean_matrix = jnp.where(row == col, 1.0 / BAND, 0.0).astype(jnp.bfloat16)
    for at in range(0, bins, width):
        lanes = pl.ds(at, width)
        real = source_ref[0, :, :, lanes].astype(jnp.float32).reshape(windows * channels, width)
        imag = source_ref[1, :, :, lanes].astype(jnp.float32).reshape(windows * channels, width)
        rest = real * real + imag * imag
        mean = jnp.zeros_like(rest)
        for _ in range(3):
            piece = rest.astype(jnp.bfloat16)
            mean += jnp.dot(piece, mean_matrix, preferred_element_type=jnp.float32)
            rest = rest - piece.astype(jnp.float32)
        scale = lax.rsqrt(mean + EPSILON)
        real = (real * scale).astype(jnp.bfloat16).astype(jnp.float32)
        imag = (imag * scale).astype(jnp.bfloat16).astype(jnp.float32)
        if as_row:
            factors = (real + imag, real, imag)
        else:
            factors = (real, -(real + imag), real - imag)
        for k, factor in enumerate(factors):
            target[k, :, pl.ds(begin, channels), lanes] = factor.reshape(windows, channels, width)


def tile_kernel(part_count, can_swap, scalars, own, *refs):
    parts = refs[:part_count]
    table, keep, send, rows, cols, cross = refs[part_count:]
    _, windows, row_count, bins = own.shape
    col_count = cols.shape[2]
    owners, share = keep.shape[0], keep.shape[1]
    begins = [sum(p.shape[2] for p in parts[:k]) for k in range(part_count)]

    def straight():
        whiten_into((own, 0), rows, True)
        for part, begin in zip(parts, begins):
            whiten_into((part, begin), cols, False)

    def swapped():
        whiten_into((own, 0), cols, False)
        for part, begin in zip(parts, begins):
            whiten_into((part, begin), rows, True)

    if can_swap:
        pl.when(scalars[1] == 0)(straight)
        pl.when(scalars[1] != 0)(swapped)
    else:
        straight()

    groups = col_count // ROWS

    def body(step, carry):
        row_at = pl.multiple_of((step // groups) * 8, 8)
        col_at = pl.multiple_of((step % groups) * ROWS, ROWS)
        for at in range(0, bins, LANES):
            lanes = pl.ds(at, LANES)
            for first in range(0, 8, OWN):
                sums = [[None] * 3 for _ in range(OWN)]
                for w in range(windows):
                    for k in range(3):
                        right = cols[k, w, pl.ds(col_at, ROWS), lanes]
                        left = rows.at[k, w, pl.ds(row_at, 8), lanes]
                        for i in range(OWN):
                            product = right * left[pl.ds(first + i, 1)]
                            sums[i][k] = product if w == 0 else sums[i][k] + product
                for i in range(OWN):
                    k1, k2, k3 = sums[i]
                    at_row = (row_at + first + i) * col_count + col_at
                    place = pl.ds(pl.multiple_of(at_row, ROWS), ROWS)
                    cross[place, pl.ds(at, LANES)] = (k1 - k3).astype(jnp.bfloat16)
                    cross[place, pl.ds(bins + at, LANES)] = (k1 + k2).astype(jnp.bfloat16)
        return carry

    lax.fori_loop(0, (row_count // 8) * groups, body, 0)
    for owner in range(owners):
        lags = jnp.dot(
            cross[pl.ds(owner * 2 * share, 2 * share)], table[...], preferred_element_type=jnp.float32
        )
        low, high = lags[:share], lags[share:]

        @pl.when(scalars[0] == 0)
        def _():
            keep[owner] = low
            send[owner] = high.astype(send.dtype)

        @pl.when(scalars[0] != 0)
        def _():
            keep[owner] = high
            send[owner] = low.astype(send.dtype)


def lag_tile(scalars, own, parts, table, owners, can_swap):
    _, windows, row_count, bins = own.shape
    col_count = sum(part.shape[2] for part in parts)
    share = row_count * col_count // (2 * owners)
    vmem = pl.BlockSpec(memory_space=pltpu.VMEM)
    return pl.pallas_call(
        functools.partial(tile_kernel, len(parts), can_swap),
        out_shape=(
            jax.ShapeDtypeStruct((owners, share, LAGS), jnp.float32),
            jax.ShapeDtypeStruct((owners, share, LAGS), jnp.bfloat16),
        ),
        in_specs=[pl.BlockSpec(memory_space=pltpu.SMEM)] + [vmem] * (len(parts) + 2),
        out_specs=(vmem, vmem),
        scratch_shapes=[
            pltpu.VMEM((3, windows, row_count, bins), jnp.float32),
            pltpu.VMEM((3, windows, col_count, bins), jnp.float32),
            pltpu.VMEM((row_count * col_count, 2 * bins), jnp.bfloat16),
        ],
        compiler_params=pltpu.CompilerParams(vmem_limit_bytes=VMEM_LIMIT),
        cost_estimate=pl.CostEstimate(
            flops=5 * 10**6 * row_count * col_count, bytes_accessed=2 << 20, transcendentals=0
        ),
    )(scalars, own, *parts, table)


def final_kernel(shapes, norm_scale, scalars, *refs):
    out = refs[-1]
    row_count, width = out.shape[1], out.shape[2]
    slot = pl.program_id(0)
    slots = pl.num_programs(0)
    offset, reach = scalars[slot], scalars[slots + slot]
    row_begin = scalars[2 * slots] * row_count
    out[...] = jnp.zeros_like(out)
    at = 0
    for step, parts in enumerate(shapes):
        begin = 0
        for term_count, columns in parts:
            terms = refs[at : at + term_count]
            at += term_count

            @pl.when(offset == step)
            def _(terms=terms, begin=begin, columns=columns, step=step):
                value = functools.reduce(
                    lambda x, y: x + y, [t[0].astype(jnp.float32) for t in terms]
                )
                value = value.reshape(row_count, columns, LAGS)
                row = lax.broadcasted_iota(jnp.int32, value.shape, 0) + row_begin
                col = lax.broadcasted_iota(jnp.int32, value.shape, 1) + begin
                distance = jnp.abs(step * width + col - row)
                kept = (distance > 0) & (distance < reach)
                out[0, :, pl.ds(begin, columns), :] = jnp.where(kept, value * norm_scale, 0.0)

            begin += columns


def assemble(scalars, values, slots, row_count, width, norm_scale):
    shapes = [[(len(terms), columns) for columns, terms in parts] for parts in values]
    operands = [term for parts in values for _, terms in parts for term in terms]

    def spec(term):
        if term.shape[0] == 1:
            return pl.BlockSpec((1,) + term.shape[1:], lambda t, sc: (0, 0, 0))
        return pl.BlockSpec((1,) + term.shape[1:], lambda t, sc: (sc[2 * slots + 1], 0, 0))

    return pl.pallas_call(
        functools.partial(final_kernel, shapes, norm_scale),
        out_shape=jax.ShapeDtypeStruct((slots, row_count, width, LAGS), jnp.float32),
        grid_spec=pltpu.PrefetchScalarGridSpec(
            num_scalar_prefetch=1,
            grid=(slots,),
            in_specs=[spec(term) for term in operands],
            out_specs=pl.BlockSpec((1, row_count, width, LAGS), lambda t, sc: (t, 0, 0, 0)),
        ),
        compiler_params=pltpu.CompilerParams(vmem_limit_bytes=VMEM_LIMIT),
    )(scalars, *operands)


def on_device(spectra, tile_offset, pair_reach):
    blocks = lax.axis_size("chan")
    days, cores = lax.axis_size("day"), lax.axis_size("sub")
    steps = min(MAX_STEPS, blocks - 1)
    wraps = blocks >= 3 and steps == blocks - 1
    local_days, local_windows, width, _, bins = spectra.shape
    norm_scale = 1.0 / math.sqrt(bins * local_days * days * local_windows * cores)
    row_count = width // (days * cores)
    slots = tile_offset.shape[1]
    day, core, block = lax.axis_index("day"), lax.axis_index("sub"), lax.axis_index("chan")
    table = jnp.asarray(lag_table(bins))

    own = jnp.transpose(spectra, (3, 0, 1, 2, 4)).reshape(2, -1, width, bins)
    half = width // 2
    halves = [own[:, :, :half], own[:, :, half:]]

    is_last = (block == blocks - 1).astype(jnp.int32) if wraps else jnp.int32(0)
    scalars = jnp.stack([core, is_last]).astype(jnp.int32)

    def over_cores(value):
        return lax.ppermute(value, "sub", [(k, (k + 1) % cores) for k in range(cores)])

    def reduce_tile(parts, can_swap=False):
        keep, send = lag_tile(scalars, own, parts, table, days, can_swap)
        got = over_cores(send)
        terms = [keep, got]
        for shift in range(1, days):
            to = (day + shift) % days
            piece = lax.dynamic_index_in_dim(keep, to, 0) + lax.dynamic_index_in_dim(got, to, 0).astype(
                jnp.float32
            )
            terms.append(
                lax.ppermute(
                    piece.astype(jnp.bfloat16), "day", [(k, (k + shift) % days) for k in range(days)]
                )
            )
        return terms

    def total(terms):
        return functools.reduce(
            lambda x, y: x + y,
            [
                (lax.dynamic_index_in_dim(t, day, 0) if t.shape[0] > 1 else t).astype(jnp.float32)
                for t in terms
            ],
        )

    values = [[(width, [total(reduce_tile(halves))])]]
    moving = halves
    wrapped = None
    for step in range(1, steps + 1):
        if wraps and step == steps:
            back = lax.ppermute(wrapped.astype(jnp.bfloat16), "chan", [(blocks - 1, 0)])
            values.append([(width, [back])])
            break
        pairs = [(a + 1, a) for a in range(blocks - step)]
        if wraps and step == 1:
            pairs.append((0, blocks - 1))
        moving = [lax.ppermute(part, "chan", pairs) for part in moving]
        if step == 1:
            wrapped = total(reduce_tile(moving, can_swap=wraps))
            values.append([(width, [wrapped])])
        else:
            values.append([(half, reduce_tile([part])) for part in moving])

    place = jnp.stack([day * cores + core, day]).astype(jnp.int32)
    last_scalars = jnp.concatenate([tile_offset[0], pair_reach[0], place])
    return assemble(last_scalars, values, slots, row_count, width, norm_scale)[None]


def solution(mesh):
    in_specs = (P(("groups", "day"), "sub", "chan", None, None), P("chan", None), P("chan", None))
    out_specs = P(("groups", "chan"), None, ("day", "sub"), None, None)
    return jax.shard_map(
        on_device, mesh=mesh, in_specs=in_specs, out_specs=out_specs, check_vma=False
    )
```

time: 206 us -> 59 us (0.29)
  local copies, waits for them, and re-layouts: 65.5 us -> 2.73 us
  matrix products: 44.2 us -> 0 us
  waiting for transfers between devices: 61.5 us -> 17.6 us
  Pallas kernels: 0 us -> 22.4 us
  between operations: 19.3 us -> 0.15 us
  starting transfers between devices: 4.04 us -> 15.5 us
  other arithmetic: 10.6 us -> 0.34 us
    dot_general x9 -> x0, matrix products: 44.2 us -> none  [the longest x3 19.4 us: lag_tile(): jnp.einsum('dwicf,dwjcf->ijf', own_turned, partner, preferred_element_typ...]
    unnamed x2 -> x0, waiting for transfers between devices: 39.7 us -> none
    transpose x6 -> x0, local copies, waits for them, and re-layouts: 39.1 us -> none  [the longest x3 20 us: lag_tile(): jnp.einsum('dwicf,dwjcf->ijf', own_rows, partner, preferred_element_type=...]
    pallas_call x0 -> x5, Pallas kernels: none -> 22.4 us  [the longest x4 20.3 us: lag_tile(): pl.pallas_call(functools.partial(tile_kernel, len(parts), can_swap), out_...]
    ppermute x3 -> x13, starting transfers between devices: 4.03 us -> 15.5 us  [the longest x4 7.68 us: on_device(): moving = [lax.ppermute(part, 'chan', pairs) for part in moving]]
    dynamic_slice x4 -> x0, local copies, waits for them, and re-layouts: 10.3 us -> none  [lag_tile(): lax.dynamic_index_in_dim(partners, jnp.maximum(offset, 0), 0, keepdims=Fa...]
    another operation x2 -> x0, local copies, waits for them, and re-layouts: 6.65 us -> none
    ppermute x3 -> x13, waiting for transfers between devices: 21.8 us -> 17.6 us  [the longest x4 7.71 us: on_device(): moving = [lax.ppermute(part, 'chan', pairs) for part in moving]]
  transfers between devices with their start and end apart: 4 -> 13, of which waited for: 4 -> 5; matrix products, arithmetic and copies ran while one was open for 7% -> 0% of each run, Pallas kernels for 0% -> 24%
where the time goes in v1:
time: 59 us; the launch traced here: 58.7 us
  Pallas kernels  22.4 us (38%)
  waiting for transfers between devices  17.6 us (30%)
  starting transfers between devices  15.5 us (26%)
  local copies, waits for them, and re-layouts  2.73 us (5%)
    pallas_call x4, Pallas kernels, lag_tile(): pl.pallas_call(functools.partial(tile_kernel, len(parts), can_swap), out_...  20.3 us
    ppermute x4, waiting for transfers between devices, on_device(): moving = [lax.ppermute(part, 'chan', pairs) for part in moving]  7.71 us
    ppermute x4, starting transfers between devices, on_device(): moving = [lax.ppermute(part, 'chan', pairs) for part in moving]  7.68 us
    ppermute x1, waiting for transfers between devices, on_device(): back = lax.ppermute(wrapped.astype(jnp.bfloat16), 'chan', [(blocks - 1, 0)])  6.33 us
    ppermute x4, starting transfers between devices, reduce_tile(): lax.ppermute(piece.astype(jnp.bfloat16), 'day', [(k, (k + shift) % days)...  5.27 us
    ppermute x4, waiting for transfers between devices, reduce_tile(): lax.ppermute(piece.astype(jnp.bfloat16), 'day', [(k, (k + shift) % days)...  3.57 us
    unnamed x7, local copies, waits for them, and re-layouts  2.7 us
    pallas_call x1, Pallas kernels, assemble(): pl.pallas_call(functools.partial(final_kernel, shapes, norm_scale), out_s...  2.12 us
  transfers between devices with their start and end apart: 13, of which 5 were waited for; matrix products, arithmetic and copies ran while one was open for 0% of the time, Pallas kernels for 24%

profile of v1, /device:TPU:0, one launch (start us, length us, event | category | flops | bytes accessed | tf_op | source)
XLA Modules:
  0.0 58.7 jit_solution(11778067679415420248)
XLA Ops:
  0.0 1.1 %copy.7 = bf16[1,8,32,2,512]{4,2,1,3,0:T(8,128)(2,1)S(1)} copy(bf16[1,8,32,2,512]{4,3,2,1,0:T(2,128)(2,1)} %param.4) | data formatting | bytes 1048576 | tf_op args[0]
  1.1 0.0 copy-start
  1.2 0.1 pad_add_fusion.1.scalars
  1.3 0.9 %copy-done = bf16[1024,256]{1,0:T(8,128)(2,1)S(1)} copy-done((bf16[1024,256]{1,0:T(8,128)(2,1)S(1)}, bf16[1024,256]{1,0:T(8,128)(2,1)}, u32[]{:S(2)}) %copy-start) | copy-done | bytes 524312
  2.2 6.4 %shard_map.46 = (f32[2,256,256]{2,1,0:T(8,128)S(1)}, bf16[2,256,256]{2,1,0:T(8,128)(2,1)S(1)}) custom-call(s32[2]{0:T(128)S(1)} %pad_add_fusion.1.scalars, bf16[2,8,32,512]{3,2,1,0:T(8,128)(2,1)S(1)} %bitcast.13, bf16[2,8,16,512]{3,2,1,0:T(8,128)(2,1)S(1)} %get-tuple-element.24.refs_0_, bf16[2,8,16,512]{3,2,1,0:T(8,128)(2,1)S(1)} %get-tuple-element.23.refs_1_, ...), custom_call_target="tpu_custom_call" | custom-call | flops 5120000000 | bytes 2097152 | tf_op jit(solution)/shard_map/pallas_call | solution.py:130
  8.5 0.5 collective-permute-start
  9.0 4.7 %collective-permute-start.2 = (bf16[2,8,16,512]{3,2,1,0:T(8,128)(2,1)S(1)}, bf16[2,8,16,512]{3,2,1,0:T(8,128)(2,1)S(1)}, u32[]{:S(2)}, u32[]{:S(2)}) collective-permute-start(bf16[2,8,16,512]{3,2,1,0:T(8,128)(2,1)S(1)} %get-tuple-element.24.refs_0_), channel_id=1, source_target_pairs={{4,0},{8,4},{12,8},{0,12},{5,1},{9,5},{13,9},{1,13},{6,2},{10,6},{... | collective-permute-start | bytes 786440 | tf_op jit(solution)/shard_map/ppermute | solution.py:260
  13.7 0.5 collective-permute-start.3
  14.2 0.7 %copy-done.1 = s32[1,3]{1,0:T(1,128)S(1)} copy-done((s32[1,3]{1,0:T(1,128)S(1)}, s32[1,3]{1,0:T(1,128)}, u32[]{:S(2)}) %copy-start.1) | copy-done | bytes 36
  14.8 0.0 copy-done.2
  14.8 0.1 pad_add_fusion.scalars
  14.9 0.0 collective-permute-done
  15.0 1.6 %collective-permute-start.1 = (bf16[1,256,256]{2,1,0:T(8,128)(2,1)S(1)}, bf16[1,256,256]{2,1,0:T(8,128)(2,1)S(1)}, u32[]{:S(2)}, u32[]{:S(2)}) collective-permute-start(bf16[1,256,256]{2,1,0:T(8,128)(2,1)S(1)} %add_convert_fusion.1), channel_id=1, source_target_pairs={{0,2},{2,0},{1,3},{3,1},{4,6},{6,4},{5,7},{7,5},{8,10},{10,8},{9,1... | collective-permute-start | bytes 393224 | tf_op jit(solution)/shard_map/ppermute | solution.py:234
  16.5 3.8 %collective-permute-done.2.refs_0_ = bf16[2,8,16,512]{3,2,1,0:T(8,128)(2,1)S(1)} collective-permute-done((bf16[2,8,16,512]{3,2,1,0:T(8,128)(2,1)S(1)}, bf16[2,8,16,512]{3,2,1,0:T(8,128)(2,1)S(1)}, u32[]{:S(2)}, u32[]{:S(2)}) %collective-permute-start.2) | collective-permute-done | bytes 262176 | tf_op jit(solution)/shard_map/ppermute | solution.py:260
  20.3 1.3 %collective-permute-start.6 = (bf16[2,8,16,512]{3,2,1,0:T(8,128)(2,1)S(1)}, bf16[2,8,16,512]{3,2,1,0:T(8,128)(2,1)S(1)}, u32[]{:S(2)}, u32[]{:S(2)}) collective-permute-start(bf16[2,8,16,512]{3,2,1,0:T(8,128)(2,1)S(1)} %collective-permute-done.2.refs_0_), channel_id=1, source_target_pairs={{4,0},{8,4},{5,1},{9,5},{6,2},{10,6},{7,3},{11,7},{20,16},{24,20},... | collective-permute-start | bytes 786440 | tf_op jit(solution)/shard_map/ppermute | solution.py:260
  21.6 3.9 %collective-permute-done.3.refs_1_ = bf16[2,8,16,512]{3,2,1,0:T(8,128)(2,1)S(1)} collective-permute-done((bf16[2,8,16,512]{3,2,1,0:T(8,128)(2,1)S(1)}, bf16[2,8,16,512]{3,2,1,0:T(8,128)(2,1)S(1)}, u32[]{:S(2)}, u32[]{:S(2)}) %collective-permute-start.3) | collective-permute-done | bytes 262176 | tf_op jit(solution)/shard_map/ppermute | solution.py:260
  25.5 1.3 %collective-permute-start.9 = (bf16[2,8,16,512]{3,2,1,0:T(8,128)(2,1)S(1)}, bf16[2,8,16,512]{3,2,1,0:T(8,128)(2,1)S(1)}, u32[]{:S(2)}, u32[]{:S(2)}) collective-permute-start(bf16[2,8,16,512]{3,2,1,0:T(8,128)(2,1)S(1)} %collective-permute-done.3.refs_1_), channel_id=1, source_target_pairs={{4,0},{8,4},{5,1},{9,5},{6,2},{10,6},{7,3},{11,7},{20,16},{24,20},... | collective-permute-start | bytes 786440 | tf_op jit(solution)/shard_map/ppermute | solution.py:260
  26.8 6.4 %shard_map.47 = (f32[2,256,256]{2,1,0:T(8,128)S(1)}, bf16[2,256,256]{2,1,0:T(8,128)(2,1)S(1)}) custom-call(s32[2]{0:T(128)S(1)} %pad_add_fusion.1.scalars, bf16[2,8,32,512]{3,2,1,0:T(8,128)(2,1)S(1)} %bitcast.14, bf16[2,8,16,512]{3,2,1,0:T(8,128)(2,1)S(1)} %collective-permute-done.2.refs_0_, bf16[2,8,16,512]{3,2,1,0:T(8,128)(2,1)S(1)} %collective-permute-done.3.refs_1_, ...), custom_call_target="tpu_custom_call" | custom-call | flops 5120000000 | bytes 2097152 | tf_op jit(solution)/shard_map/pallas_call | solution.py:130
  33.2 0.1 collective-permute-start.4
  33.3 3.8 %shard_map.48 = (f32[2,128,256]{2,1,0:T(8,128)S(1)}, bf16[2,128,256]{2,1,0:T(8,128)(2,1)S(1)}) custom-call(s32[2]{0:T(128)S(1)} %pad_add_fusion.1.scalars, bf16[2,8,32,512]{3,2,1,0:T(8,128)(2,1)S(1)} %bitcast.15, bf16[2,8,16,512]{3,2,1,0:T(8,128)(2,1)S(1)} %collective-permute-done.6.refs_0_, bf16[1024,256]{1,0:T(8,128)(2,1)S(1)} %copy-done), custom_call_target="tpu_custom_call" | custom-call | flops 2560000000 | bytes 2097152 | tf_op jit(solution)/shard_map/pallas_call | solution.py:130
  37.0 0.6 collective-permute-start.7
  37.6 3.8 %shard_map.49 = (f32[2,128,256]{2,1,0:T(8,128)S(1)}, bf16[2,128,256]{2,1,0:T(8,128)(2,1)S(1)}) custom-call(s32[2]{0:T(128)S(1)} %pad_add_fusion.1.scalars, bf16[2,8,32,512]{3,2,1,0:T(8,128)(2,1)S(1)} %bitcast.16, bf16[2,8,16,512]{3,2,1,0:T(8,128)(2,1)S(1)} %collective-permute-done.9.refs_0_, bf16[1024,256]{1,0:T(8,128)(2,1)S(1)} %copy-done), custom_call_target="tpu_custom_call" | custom-call | flops 2560000000 | bytes 2097152 | tf_op jit(solution)/shard_map/pallas_call | solution.py:130
  41.4 0.1 collective-permute-start.10
  41.5 0.0 collective-permute-done.4
  41.5 1.6 %collective-permute-start.5 = (bf16[1,256,256]{2,1,0:T(8,128)(2,1)S(1)}, bf16[1,256,256]{2,1,0:T(8,128)(2,1)S(1)}, u32[]{:S(2)}, u32[]{:S(2)}) collective-permute-start(bf16[1,256,256]{2,1,0:T(8,128)(2,1)S(1)} %add_convert_fusion), channel_id=1, source_target_pairs={{0,2},{2,0},{1,3},{3,1},{4,6},{6,4},{5,7},{7,5},{8,10},{10,8},{9,1... | collective-permute-start | bytes 393224 | tf_op jit(solution)/shard_map/ppermute | solution.py:234
  43.1 0.6 %collective-permute-start.8 = (bf16[1,128,256]{2,1,0:T(8,128)(2,1)S(1)}, bf16[1,128,256]{2,1,0:T(8,128)(2,1)S(1)}, u32[]{:S(2)}, u32[]{:S(2)}) collective-permute-start(bf16[1,128,256]{2,1,0:T(8,128)(2,1)S(1)} %add_convert_fusion.3), channel_id=1, source_target_pairs={{0,2},{2,0},{1,3},{3,1},{4,6},{6,4},{5,7},{7,5},{8,10},{10,8},{9,1... | collective-permute-start | bytes 196616 | tf_op jit(solution)/shard_map/ppermute | solution.py:234
  43.7 1.6 %collective-permute-start.11 = (bf16[1,128,256]{2,1,0:T(8,128)(2,1)S(1)}, bf16[1,128,256]{2,1,0:T(8,128)(2,1)S(1)}, u32[]{:S(2)}, u32[]{:S(2)}) collective-permute-start(bf16[1,128,256]{2,1,0:T(8,128)(2,1)S(1)} %add_convert_fusion.2), channel_id=1, source_target_pairs={{0,2},{2,0},{1,3},{3,1},{4,6},{6,4},{5,7},{7,5},{8,10},{10,8},{9,1... | collective-permute-start | bytes 196616 | tf_op jit(solution)/shard_map/ppermute | solution.py:234
  45.3 2.6 %collective-permute-done.5 = bf16[1,256,256]{2,1,0:T(8,128)(2,1)S(1)} collective-permute-done((bf16[1,256,256]{2,1,0:T(8,128)(2,1)S(1)}, bf16[1,256,256]{2,1,0:T(8,128)(2,1)S(1)}, u32[]{:S(2)}, u32[]{:S(2)}) %collective-permute-start.5) | collective-permute-done | bytes 131104 | tf_op jit(solution)/shard_map/ppermute | solution.py:234
  47.9 1.3 %collective-permute-start.12 = (bf16[1,256,256]{2,1,0:T(8,128)(2,1)S(1)}, bf16[1,256,256]{2,1,0:T(8,128)(2,1)S(1)}, u32[]{:S(2)}, u32[]{:S(2)}) collective-permute-start(bf16[1,256,256]{2,1,0:T(8,128)(2,1)S(1)} %get-tuple-element.21), channel_id=1, source_target_pairs={{12,0},{13,1},{14,2},{15,3},{28,16},{29,17},{30,18},{31,19}} | collective-permute-start | bytes 393224 | tf_op jit(solution)/shard_map/ppermute | solution.py:254
  49.3 1.0 %collective-permute-done.11.refs_7_ = bf16[1,128,256]{2,1,0:T(8,128)(2,1)S(1)} collective-permute-done((bf16[1,128,256]{2,1,0:T(8,128)(2,1)S(1)}, bf16[1,128,256]{2,1,0:T(8,128)(2,1)S(1)}, u32[]{:S(2)}, u32[]{:S(2)}) %collective-permute-start.11) | collective-permute-done | bytes 65568 | tf_op jit(solution)/shard_map/ppermute | solution.py:234
  50.3 6.3 %collective-permute-done.12.refs_8_ = bf16[1,256,256]{2,1,0:T(8,128)(2,1)S(1)} collective-permute-done((bf16[1,256,256]{2,1,0:T(8,128)(2,1)S(1)}, bf16[1,256,256]{2,1,0:T(8,128)(2,1)S(1)}, u32[]{:S(2)}, u32[]{:S(2)}) %collective-permute-start.12) | collective-permute-done | bytes 131104 | tf_op jit(solution)/shard_map/ppermute | solution.py:254
  56.6 2.1 %shard_map.50 = f32[3,8,32,256]{3,2,1,0:T(8,128)} custom-call(s32[8]{0:T(128)S(1)} %pad_add_fusion.scalars, f32[1,256,256]{2,1,0:T(8,128)S(1)} %convert_add_fusion.1.refs_0_, f32[1,256,256]{2,1,0:T(8,128)S(1)} %get-tuple-element.22.refs_1_, f32[2,128,256]{2,1,0:T(8,128)S(1)} %get-tuple-element.17.refs_2_, ...), custom_call_target="tpu_custom_call" | custom-call | tf_op jit(solution)/shard_map/pallas_call | solution.py:189
  (15 shorter events, 0.2 us)
Async XLA Ops:
  1.1 1.0 %copy-start = (bf16[1024,256]{1,0:T(8,128)(2,1)S(1)}, bf16[1024,256]{1,0:T(8,128)(2,1)}, u32[]{:S(2)}) copy-start(bf16[1024,256]{1,0:T(8,128)(2,1)} %constant.67.clone.refs_2_.refs_1_) | copy-start | bytes 1572868
  8.5 6.4 %collective-permute-start = (bf16[2,256,256]{2,1,0:T(8,128)(2,1)S(1)}, bf16[2,256,256]{2,1,0:T(8,128)(2,1)S(1)}, u32[]{:S(2)}, u32[]{:S(2)}) collective-permute-start(bf16[2,256,256]{2,1,0:T(8,128)(2,1)S(1)} %get-tuple-element.14), channel_id=1, source_target_pairs={{0,1},{1,0},{2,3},{3,2},{4,5},{5,4},{6,7},{7,6},{8,9},{9,8},{10,11... | collective-permute-start | bytes 786440 | tf_op jit(solution)/shard_map/ppermute | solution.py:222
  9.0 11.3 %collective-permute-start.2 = (bf16[2,8,16,512]{3,2,1,0:T(8,128)(2,1)S(1)}, bf16[2,8,16,512]{3,2,1,0:T(8,128)(2,1)S(1)}, u32[]{:S(2)}, u32[]{:S(2)}) collective-permute-start(bf16[2,8,16,512]{3,2,1,0:T(8,128)(2,1)S(1)} %get-tuple-element.24.refs_0_), channel_id=1, source_target_pairs={{4,0},{8,4},{12,8},{0,12},{5,1},{9,5},{13,9},{1,13},{6,2},{10,6},{... | collective-permute-start | bytes 786440 | tf_op jit(solution)/shard_map/ppermute | solution.py:260
  13.7 11.8 %collective-permute-start.3 = (bf16[2,8,16,512]{3,2,1,0:T(8,128)(2,1)S(1)}, bf16[2,8,16,512]{3,2,1,0:T(8,128)(2,1)S(1)}, u32[]{:S(2)}, u32[]{:S(2)}) collective-permute-start(bf16[2,8,16,512]{3,2,1,0:T(8,128)(2,1)S(1)} %get-tuple-element.23.refs_1_), channel_id=1, source_target_pairs={{4,0},{8,4},{12,8},{0,12},{5,1},{9,5},{13,9},{1,13},{6,2},{10,6},{... | collective-permute-start | bytes 786440 | tf_op jit(solution)/shard_map/ppermute | solution.py:260
  14.2 0.7 %copy-start.1 = (s32[1,3]{1,0:T(1,128)S(1)}, s32[1,3]{1,0:T(1,128)}, u32[]{:S(2)}) copy-start(s32[1,3]{1,0:T(1,128)} %param.6) | copy-start | bytes 40
  14.2 0.7 %copy-start.2 = (s32[1,3]{1,0:T(1,128)S(1)}, s32[1,3]{1,0:T(1,128)}, u32[]{:S(2)}) copy-start(s32[1,3]{1,0:T(1,128)} %param.5) | copy-start | bytes 40
  15.0 34.3 %collective-permute-start.1 = (bf16[1,256,256]{2,1,0:T(8,128)(2,1)S(1)}, bf16[1,256,256]{2,1,0:T(8,128)(2,1)S(1)}, u32[]{:S(2)}, u32[]{:S(2)}) collective-permute-start(bf16[1,256,256]{2,1,0:T(8,128)(2,1)S(1)} %add_convert_fusion.1), channel_id=1, source_target_pairs={{0,2},{2,0},{1,3},{3,1},{4,6},{6,4},{5,7},{7,5},{8,10},{10,8},{9,1... | collective-permute-start | bytes 393224 | tf_op jit(solution)/shard_map/ppermute | solution.py:234
  20.3 12.9 %collective-permute-start.6 = (bf16[2,8,16,512]{3,2,1,0:T(8,128)(2,1)S(1)}, bf16[2,8,16,512]{3,2,1,0:T(8,128)(2,1)S(1)}, u32[]{:S(2)}, u32[]{:S(2)}) collective-permute-start(bf16[2,8,16,512]{3,2,1,0:T(8,128)(2,1)S(1)} %collective-permute-done.2.refs_0_), channel_id=1, source_target_pairs={{4,0},{8,4},{5,1},{9,5},{6,2},{10,6},{7,3},{11,7},{20,16},{24,20},... | collective-permute-start | bytes 786440 | tf_op jit(solution)/shard_map/ppermute | solution.py:260
  25.5 12.1 %collective-permute-start.9 = (bf16[2,8,16,512]{3,2,1,0:T(8,128)(2,1)S(1)}, bf16[2,8,16,512]{3,2,1,0:T(8,128)(2,1)S(1)}, u32[]{:S(2)}, u32[]{:S(2)}) collective-permute-start(bf16[2,8,16,512]{3,2,1,0:T(8,128)(2,1)S(1)} %collective-permute-done.3.refs_1_), channel_id=1, source_target_pairs={{4,0},{8,4},{5,1},{9,5},{6,2},{10,6},{7,3},{11,7},{20,16},{24,20},... | collective-permute-start | bytes 786440 | tf_op jit(solution)/shard_map/ppermute | solution.py:260
  33.2 8.3 %collective-permute-start.4 = (bf16[2,256,256]{2,1,0:T(8,128)(2,1)S(1)}, bf16[2,256,256]{2,1,0:T(8,128)(2,1)S(1)}, u32[]{:S(2)}, u32[]{:S(2)}) collective-permute-start(bf16[2,256,256]{2,1,0:T(8,128)(2,1)S(1)} %get-tuple-element.16), channel_id=1, source_target_pairs={{0,1},{1,0},{2,3},{3,2},{4,5},{5,4},{6,7},{7,6},{8,9},{9,8},{10,11... | collective-permute-start | bytes 786440 | tf_op jit(solution)/shard_map/ppermute | solution.py:222
  37.0 6.0 %collective-permute-start.7 = (bf16[2,128,256]{2,1,0:T(8,128)(2,1)S(1)}, bf16[2,128,256]{2,1,0:T(8,128)(2,1)S(1)}, u32[]{:S(2)}, u32[]{:S(2)}) collective-permute-start(bf16[2,128,256]{2,1,0:T(8,128)(2,1)S(1)} %get-tuple-element.18), channel_id=1, source_target_pairs={{0,1},{1,0},{2,3},{3,2},{4,5},{5,4},{6,7},{7,6},{8,9},{9,8},{10,11... | collective-permute-start | bytes 393224 | tf_op jit(solution)/shard_map/ppermute | solution.py:222
  41.4 2.3 %collective-permute-start.10 = (bf16[2,128,256]{2,1,0:T(8,128)(2,1)S(1)}, bf16[2,128,256]{2,1,0:T(8,128)(2,1)S(1)}, u32[]{:S(2)}, u32[]{:S(2)}) collective-permute-start(bf16[2,128,256]{2,1,0:T(8,128)(2,1)S(1)} %get-tuple-element.20), channel_id=1, source_target_pairs={{0,1},{1,0},{2,3},{3,2},{4,5},{5,4},{6,7},{7,6},{8,9},{9,8},{10,11... | collective-permute-start | bytes 393224 | tf_op jit(solution)/shard_map/ppermute | solution.py:222
  41.5 6.4 %collective-permute-start.5 = (bf16[1,256,256]{2,1,0:T(8,128)(2,1)S(1)}, bf16[1,256,256]{2,1,0:T(8,128)(2,1)S(1)}, u32[]{:S(2)}, u32[]{:S(2)}) collective-permute-start(bf16[1,256,256]{2,1,0:T(8,128)(2,1)S(1)} %add_convert_fusion), channel_id=1, source_target_pairs={{0,2},{2,0},{1,3},{3,1},{4,6},{6,4},{5,7},{7,5},{8,10},{10,8},{9,1... | collective-permute-start | bytes 393224 | tf_op jit(solution)/shard_map/ppermute | solution.py:234
  43.1 6.2 %collective-permute-start.8 = (bf16[1,128,256]{2,1,0:T(8,128)(2,1)S(1)}, bf16[1,128,256]{2,1,0:T(8,128)(2,1)S(1)}, u32[]{:S(2)}, u32[]{:S(2)}) collective-permute-start(bf16[1,128,256]{2,1,0:T(8,128)(2,1)S(1)} %add_convert_fusion.3), channel_id=1, source_target_pairs={{0,2},{2,0},{1,3},{3,1},{4,6},{6,4},{5,7},{7,5},{8,10},{10,8},{9,1... | collective-permute-start | bytes 196616 | tf_op jit(solution)/shard_map/ppermute | solution.py:234
  43.7 6.5 %collective-permute-start.11 = (bf16[1,128,256]{2,1,0:T(8,128)(2,1)S(1)}, bf16[1,128,256]{2,1,0:T(8,128)(2,1)S(1)}, u32[]{:S(2)}, u32[]{:S(2)}) collective-permute-start(bf16[1,128,256]{2,1,0:T(8,128)(2,1)S(1)} %add_convert_fusion.2), channel_id=1, source_target_pairs={{0,2},{2,0},{1,3},{3,1},{4,6},{6,4},{5,7},{7,5},{8,10},{10,8},{9,1... | collective-permute-start | bytes 196616 | tf_op jit(solution)/shard_map/ppermute | solution.py:234
  47.9 8.7 %collective-permute-start.12 = (bf16[1,256,256]{2,1,0:T(8,128)(2,1)S(1)}, bf16[1,256,256]{2,1,0:T(8,128)(2,1)S(1)}, u32[]{:S(2)}, u32[]{:S(2)}) collective-permute-start(bf16[1,256,256]{2,1,0:T(8,128)(2,1)S(1)} %get-tuple-element.21), channel_id=1, source_target_pairs={{12,0},{13,1},{14,2},{15,3},{28,16},{29,17},{30,18},{31,19}} | collective-permute-start | bytes 393224 | tf_op jit(solution)/shard_map/ppermute | solution.py:254

commit v2 on v1

v2 whole, which is shorter than its diff:
```python
import functools
import math

import jax
import jax.numpy as jnp
import ml_dtypes
import numpy as np
from jax import lax
from jax.experimental import pallas as pl
from jax.experimental.pallas import tpu as pltpu
from jax.sharding import PartitionSpec as P

BAND = 32
LAGS = 256
MAX_STEPS = 4
EPSILON = 1e-06
LANES = 128
ROWS = 16
OWN = 4
VMEM_LIMIT = 40 << 20


def lag_table(bin_count):
    bins = np.arange(bin_count, dtype=np.float64)[:, None]
    lags = np.arange(LAGS, dtype=np.float64)[None, :] - LAGS // 2
    angle = np.pi * bins * lags / bin_count
    table = np.concatenate([np.cos(angle), -np.sin(angle)], axis=0).astype(np.float32)
    return table.astype(ml_dtypes.bfloat16)


def whiten(source):
    _, windows, channels, bins = source.shape
    width = 2 * LANES
    row = lax.broadcasted_iota(jnp.int32, (width, width), 0) // BAND
    col = lax.broadcasted_iota(jnp.int32, (width, width), 1) // BAND
    mean_matrix = jnp.where(row == col, 1.0 / BAND, 0.0).astype(jnp.bfloat16)
    for at in range(0, bins, width):
        lanes = pl.ds(at, width)
        real = source[0, :, :, lanes].astype(jnp.float32).reshape(windows * channels, width)
        imag = source[1, :, :, lanes].astype(jnp.float32).reshape(windows * channels, width)
        rest = real * real + imag * imag
        mean = jnp.zeros_like(rest)
        for _ in range(3):
            piece = rest.astype(jnp.bfloat16)
            mean += jnp.dot(piece, mean_matrix, preferred_element_type=jnp.float32)
            rest = rest - piece.astype(jnp.float32)
        scale = lax.rsqrt(mean + EPSILON)
        shape = (windows, channels, width)
        yield (
            lanes,
            (real * scale).astype(jnp.bfloat16).astype(jnp.float32).reshape(shape),
            (imag * scale).astype(jnp.bfloat16).astype(jnp.float32).reshape(shape),
        )


def row_factors(real, imag):
    return real + imag, real, imag


def col_factors(real, imag):
    return real, -(real + imag), real - imag


def store_factors(source, target, begin, factors):
    for lanes, real, imag in whiten(source):
        for k, value in enumerate(factors(real, imag)):
            target[k, :, pl.ds(begin, source.shape[2]), lanes] = value


def cross_tile(rows, cols, cross):
    _, windows, row_count, bins = rows.shape
    col_count = cols.shape[2]
    groups = col_count // ROWS

    def body(step, carry):
        row_at = pl.multiple_of((step // groups) * 8, 8)
        col_at = pl.multiple_of((step % groups) * ROWS, ROWS)
        for at in range(0, bins, LANES):
            lanes = pl.ds(at, LANES)
            for first in range(0, 8, OWN):
                sums = [[None] * 3 for _ in range(OWN)]
                for w in range(windows):
                    for k in range(3):
                        right = cols[k, w, pl.ds(col_at, ROWS), lanes]
                        left = rows.at[k, w, pl.ds(row_at, 8), lanes]
                        for i in range(OWN):
                            product = right * left[pl.ds(first + i, 1)]
                            sums[i][k] = product if w == 0 else sums[i][k] + product
                for i in range(OWN):
                    k1, k2, k3 = sums[i]
                    at_row = (row_at + first + i) * col_count + col_at
                    place = pl.ds(pl.multiple_of(at_row, ROWS), ROWS)
                    cross[place, pl.ds(at, LANES)] = (k1 - k3).astype(jnp.bfloat16)
                    cross[place, pl.ds(bins + at, LANES)] = (k1 + k2).astype(jnp.bfloat16)
        return carry

    lax.fori_loop(0, (row_count // 8) * groups, body, 0)


def lag_sums(scalars, cross, table, keep, sends):
    owners, share = keep.shape[0], keep.shape[1]
    core, day = scalars[0], scalars[1]
    for shift in range(owners):
        owner = lax.rem(day + shift, owners)
        place = pl.ds(pl.multiple_of(owner * (2 * share), 2 * share), 2 * share)
        lags = jnp.dot(cross[place], table[...], preferred_element_type=jnp.float32)
        low, high = lags[:share], lags[share:]
        send = sends[shift]

        @pl.when(core == 0)
        def _():
            keep[shift] = low
            send[0] = high.astype(send.dtype)

        @pl.when(core != 0)
        def _():
            keep[shift] = high
            send[0] = low.astype(send.dtype)


def begins_of(parts):
    return [sum(p.shape[2] for p in parts[:k]) for k in range(len(parts))]


def own_kernel(part_count, scalars, table, *refs):
    parts = refs[:part_count]
    keep, *sends, rows, cols, cross = refs[part_count:]
    for part, begin in zip(parts, begins_of(parts)):
        for lanes, real, imag in whiten(part):
            for k in range(3):
                rows[k, :, pl.ds(begin, part.shape[2]), lanes] = row_factors(real, imag)[k]
                cols[k, :, pl.ds(begin, part.shape[2]), lanes] = col_factors(real, imag)[k]
    cross_tile(rows, cols, cross)
    lag_sums(scalars, cross, table, keep, sends)


def partner_kernel(part_count, after_count, can_swap, scalars, own_rows, table, *refs):
    parts = refs[:part_count]
    keep, *sends = refs[part_count + after_count : -2 - can_swap]
    cols, cross = refs[-2 - can_swap :][:2]
    begins = begins_of(parts)

    def straight():
        for part, begin in zip(parts, begins):
            store_factors(part, cols, begin, col_factors)
        cross_tile(own_rows, cols, cross)

    def swapped():
        rows = refs[-1]
        for at in range(0, cols.shape[3], LANES):
            lanes = pl.ds(at, LANES)
            real, imag = own_rows[1, :, :, lanes], own_rows[2, :, :, lanes]
            for k, value in enumerate(col_factors(real, imag)):
                cols[k, :, :, lanes] = value
        for part, begin in zip(parts, begins):
            store_factors(part, rows, begin, row_factors)
        cross_tile(rows, cols, cross)

    if can_swap:
        pl.when(scalars[2] == 0)(straight)
        pl.when(scalars[2] != 0)(swapped)
    else:
        straight()
    lag_sums(scalars, cross, table, keep, sends)


VMEM = pl.BlockSpec(memory_space=pltpu.VMEM)
SMEM = pl.BlockSpec(memory_space=pltpu.SMEM)
ANY = pl.BlockSpec(memory_space=pl.ANY)
FREE = pl.CostEstimate(flops=0, bytes_accessed=0, transcendentals=0)
PARAMS = pltpu.CompilerParams(vmem_limit_bytes=VMEM_LIMIT)


def sums_shapes(owners, pairs):
    share = pairs // (2 * owners)
    return [jax.ShapeDtypeStruct((owners, share, LAGS), jnp.float32)] + [
        jax.ShapeDtypeStruct((1, share, LAGS), jnp.bfloat16)
    ] * owners


def own_tile(scalars, parts, table, owners):
    _, windows, _, bins = parts[0].shape
    width = sum(part.shape[2] for part in parts)
    factors = (3, windows, width, bins)
    keep, *sends, rows = pl.pallas_call(
        functools.partial(own_kernel, len(parts)),
        out_shape=sums_shapes(owners, width * width) + [jax.ShapeDtypeStruct(factors, jnp.float32)],
        in_specs=[SMEM] + [VMEM] * (1 + len(parts)),
        out_specs=[VMEM] * (owners + 2),
        scratch_shapes=[
            pltpu.VMEM(factors, jnp.float32),
            pltpu.VMEM((width * width, 2 * bins), jnp.bfloat16),
        ],
        compiler_params=PARAMS,
        cost_estimate=FREE,
    )(scalars, table, *parts)
    return keep, sends, rows


def partner_tile(scalars, own_rows, parts, table, owners, can_swap, after):
    _, windows, width, bins = own_rows.shape
    col_count = sum(part.shape[2] for part in parts)
    keep, *sends = pl.pallas_call(
        functools.partial(partner_kernel, len(parts), len(after), can_swap),
        out_shape=sums_shapes(owners, width * col_count),
        in_specs=[SMEM] + [VMEM] * (2 + len(parts)) + [ANY] * len(after),
        out_specs=[VMEM] * (owners + 1),
        scratch_shapes=[
            pltpu.VMEM((3, windows, col_count, bins), jnp.float32),
            pltpu.VMEM((width * col_count, 2 * bins), jnp.bfloat16),
        ]
        + [pltpu.VMEM((3, windows, width, bins), jnp.float32)] * can_swap,
        compiler_params=PARAMS,
        cost_estimate=FREE,
    )(scalars, own_rows, table, *parts, *after)
    return keep, sends


def add_kernel(term_count, *refs):
    total = functools.reduce(
        lambda x, y: x + y, [t[...].astype(jnp.float32) for t in refs[:term_count]]
    )
    for out in refs[term_count:]:
        out[...] = total.astype(out.dtype)


def add_terms(terms, dtypes):
    shape = (1,) + terms[0][0].shape[1:]
    return pl.pallas_call(
        functools.partial(add_kernel, len(terms)),
        out_shape=[jax.ShapeDtypeStruct(shape, dtype) for dtype in dtypes],
        grid=(1,),
        in_specs=[pl.BlockSpec(shape, lambda t, k=k: (k, 0, 0)) for _, k in terms],
        out_specs=[pl.BlockSpec(shape, lambda t: (0, 0, 0)) for _ in dtypes],
        compiler_params=PARAMS,
        cost_estimate=FREE,
    )(*[array for array, _ in terms])


def masked(value, step, begin, row_begin, reach, width, norm_scale):
    row = lax.broadcasted_iota(jnp.int32, value.shape, 0) + row_begin
    col = lax.broadcasted_iota(jnp.int32, value.shape, 1) + begin
    distance = jnp.abs(step * width + col - row)
    return jnp.where((distance > 0) & (distance < reach), value * norm_scale, 0.0)


def add_up(terms, row_count, columns):
    value = functools.reduce(lambda x, y: x + y, [t[0].astype(jnp.float32) for t in terms])
    return value.reshape(row_count, columns, LAGS)


def early_kernel(norm_scale, scalars, *refs):
    terms, out = refs[:-1], refs[-1]
    _, row_count, width, _ = out.shape
    slots = pl.num_programs(0)
    slot = pl.program_id(0)
    out[...] = jnp.zeros_like(out)

    @pl.when(scalars[slot] == 0)
    def _():
        value = add_up(terms, row_count, width)
        row_begin = scalars[2 * slots] * row_count
        out[0] = masked(value, 0, 0, row_begin, scalars[slots + slot], width, norm_scale)


def late_kernel(shapes, slots, norm_scale, scalars, *refs):
    out, tiles, sems = refs[-3:]
    _, row_count, width, _ = out.shape
    row_begin = scalars[2 * slots] * row_count
    at = 0
    copies = []
    for place, (step, parts) in enumerate(shapes):
        slot, found = jnp.int32(0), jnp.int32(0)
        for k in range(slots):
            here = (scalars[k] == step).astype(jnp.int32)
            slot, found = slot + k * here, found + here
        reach = scalars[slots + slot]
        copy = pltpu.make_async_copy(tiles.at[place], out.at[slot], sems.at[place])
        listed = []
        begin = 0
        for term_count, columns in parts:
            listed.append((refs[at : at + term_count], begin, columns))
            at += term_count
            begin += columns

        @pl.when(found > 0)
        def _(listed=listed, step=step, reach=reach, place=place, copy=copy):
            for terms, begin, columns in listed:
                value = add_up(terms, row_count, columns)
                tiles[place, :, pl.ds(begin, columns), :] = masked(
                    value, step, begin, row_begin, reach, width, norm_scale
                )
            copy.start()

        copies.append((found, copy))
    for found, copy in copies:
        pl.when(found > 0)(copy.wait)


def owner_spec(term):
    return pl.BlockSpec((1,) + term.shape[1:], lambda t, sc: (0, 0, 0))


def write_early(scalars, terms, slots, row_count, width, norm_scale):
    return pl.pallas_call(
        functools.partial(early_kernel, norm_scale),
        out_shape=jax.ShapeDtypeStruct((slots, row_count, width, LAGS), jnp.float32),
        grid_spec=pltpu.PrefetchScalarGridSpec(
            num_scalar_prefetch=1,
            grid=(slots,),
            in_specs=[owner_spec(term) for term in terms],
            out_specs=pl.BlockSpec((1, row_count, width, LAGS), lambda t, sc: (t, 0, 0, 0)),
        ),
        compiler_params=PARAMS,
        cost_estimate=FREE,
    )(scalars, *terms)


def write_late(scalars, values, out, norm_scale):
    slots, row_count, width, _ = out.shape
    shapes = [(step, [(len(terms), columns) for columns, terms in parts]) for step, parts in values]
    operands = [term for _, parts in values for _, terms in parts for term in terms]
    return pl.pallas_call(
        functools.partial(late_kernel, shapes, slots, norm_scale),
        out_shape=jax.ShapeDtypeStruct(out.shape, out.dtype),
        grid_spec=pltpu.PrefetchScalarGridSpec(
            num_scalar_prefetch=1,
            grid=(1,),
            in_specs=[owner_spec(term) for term in operands] + [ANY],
            out_specs=ANY,
            scratch_shapes=[
                pltpu.VMEM((len(values), row_count, width, LAGS), jnp.float32),
                pltpu.SemaphoreType.DMA((len(values),)),
            ],
        ),
        input_output_aliases={len(operands) + 1: 0},
        compiler_params=PARAMS,
        cost_estimate=FREE,
    )(scalars, *operands, out)


def on_device(spectra, tile_offset, pair_reach):
    blocks = lax.axis_size("chan")
    days, cores = lax.axis_size("day"), lax.axis_size("sub")
    steps = min(MAX_STEPS, blocks - 1)
    wraps = blocks >= 3 and steps == blocks - 1
    local_days, local_windows, width, _, bins = spectra.shape
    norm_scale = 1.0 / math.sqrt(bins * local_days * days * local_windows * cores)
    row_count = width // (days * cores)
    slots = tile_offset.shape[1]
    day, core, block = lax.axis_index("day"), lax.axis_index("sub"), lax.axis_index("chan")
    table = jnp.asarray(lag_table(bins))

    half = width // 2
    halves = [
        jnp.transpose(spectra[:, :, at : at + half], (3, 0, 1, 2, 4)).reshape(2, -1, half, bins)
        for at in (0, half)
    ]

    is_last = (block == blocks - 1).astype(jnp.int32) if wraps else jnp.int32(0)
    scalars = jnp.stack([core, day, is_last]).astype(jnp.int32)
    slot_scalars = jnp.concatenate([tile_offset[0], pair_reach[0], (day * cores + core).reshape(1)])

    def reduce_tile(keep, sends):
        got = [lax.ppermute(send, "sub", [(k, (k + 1) % cores) for k in range(cores)]) for send in sends]
        terms, pieces = [(keep, 0), (got[0], 0)], []
        for shift in range(1, days):
            (piece,) = add_terms([(keep, shift), (got[shift], 0)], [jnp.bfloat16])
            pieces.append(piece)
            moved = lax.ppermute(piece, "day", [(k, (k + shift) % days) for k in range(days)])
            terms.append((moved, 0))
        return terms, pieces

    keep, sends, own_rows = own_tile(scalars, halves, table, days)
    own_terms, _ = reduce_tile(keep, sends)
    out = write_early(slot_scalars, [a for a, _ in own_terms], slots, row_count, width, norm_scale)

    values = []
    moving = halves
    for step in range(1, steps + 1 - wraps):
        pairs = [(a + 1, a) for a in range(blocks - step)]
        if wraps and step == 1:
            pairs.append((0, blocks - 1))
        if step == 2:
            moving = [lax.optimization_barrier((part, sends[0]))[0] for part in moving]
        moving = [lax.ppermute(part, "chan", pairs) for part in moving]
        if step == 1:
            keep, sends1 = partner_tile(scalars, own_rows, moving, table, days, wraps, [])
            terms, pieces = reduce_tile(keep, sends1)
            if wraps:
                total, narrow = add_terms(terms, [jnp.float32, jnp.bfloat16])
                terms = [(total, 0)]
                back = lax.ppermute(narrow, "chan", [(blocks - 1, 0)])
            values.append((step, [(width, [a for a, _ in terms])]))
        else:
            listed = []
            for at, part in enumerate(moving):
                after = pieces if at else []
                keep, sends2 = partner_tile(scalars, own_rows, [part], table, days, False, after)
                terms, _ = reduce_tile(keep, sends2)
                listed.append((half, [a for a, _ in terms]))
            values.append((step, listed))
    if wraps:
        values.append((steps, [(width, [back])]))
    return write_late(slot_scalars, values, out, norm_scale)[None]


def solution(mesh):
    in_specs = (P(("groups", "day"), "sub", "chan", None, None), P("chan", None), P("chan", None))
    out_specs = P(("groups", "chan"), None, ("day", "sub"), None, None)
    return jax.shard_map(
        on_device, mesh=mesh, in_specs=in_specs, out_specs=out_specs, check_vma=False
    )
```

time: 59 us -> 47.6 us (0.81)
  waiting for transfers between devices: 17.6 us -> 7.05 us
  local copies, waits for them, and re-layouts: 2.73 us -> 1.55 us
    ppermute x9 -> x13, waiting for transfers between devices: 9.91 us -> 3.9 us  [the longest x4 1.64 us: reduce_tile(): lax.ppermute(piece, 'day', [(k, (k + shift) % days) for k in range(days)])]
    ppermute x4, waiting for transfers between devices: 7.71 us -> 3.15 us  [on_device(): moving = [lax.ppermute(part, 'chan', pairs) for part in moving]]
    unnamed x7 -> x8, local copies, waits for them, and re-layouts: 2.7 us -> 0.08 us
    slice x1, local copies, waits for them, and re-layouts: 0.04 us -> 1.47 us  [on_device(): spectra[:, :, at:at + half]]
    pallas_call x5 -> x11, Pallas kernels: 22.4 us -> 22.8 us  [the longest x3 13.1 us: partner_tile(): pl.pallas_call(functools.partial(partner_kernel, len(parts), len(after),...]
    ppermute x9 -> x13, starting transfers between devices: 7.81 us -> 7.49 us  [the longest x4 4.25 us: reduce_tile(): lax.ppermute(piece, 'day', [(k, (k + shift) % days) for k in range(days)])]
  transfers between devices with their start and end apart: 13 -> 17, of which waited for: 5 -> 5; matrix products, arithmetic and copies ran while one was open for 0% -> 0% of each run, Pallas kernels for 24% -> 45%
where the time goes in v2:
time: 47.6 us; the launch traced here: 47.4 us
  Pallas kernels  22.8 us (48%)
  starting transfers between devices  15.7 us (33%)
  waiting for transfers between devices  7.05 us (15%)
  local copies, waits for them, and re-layouts  1.55 us (3%)
    pallas_call x3, Pallas kernels, partner_tile(): pl.pallas_call(functools.partial(partner_kernel, len(parts), len(after),...  13.1 us
    ppermute x4, starting transfers between devices, on_device(): moving = [lax.ppermute(part, 'chan', pairs) for part in moving]  8.18 us
    pallas_call x1, Pallas kernels, own_tile(): pl.pallas_call(functools.partial(own_kernel, len(parts)), out_shape=sums_...  6.11 us
    ppermute x4, starting transfers between devices, reduce_tile(): lax.ppermute(piece, 'day', [(k, (k + shift) % days) for k in range(days)])  4.25 us
    ppermute x4, waiting for transfers between devices, on_device(): moving = [lax.ppermute(part, 'chan', pairs) for part in moving]  3.15 us
    pallas_call x1, Pallas kernels, write_early(): pl.pallas_call(functools.partial(early_kernel, norm_scale), out_shape=jax...  2 us
    ppermute x8, starting transfers between devices, reduce_tile(): lax.ppermute(send, 'sub', [(k, (k + 1) % cores) for k in range(cores)])  1.95 us
    ppermute x4, waiting for transfers between devices, reduce_tile(): lax.ppermute(piece, 'day', [(k, (k + shift) % days) for k in range(days)])  1.64 us
  transfers between devices with their start and end apart: 17, of which 5 were waited for; matrix products, arithmetic and copies ran while one was open for 0% of the time, Pallas kernels for 45%

profile of v2, /device:TPU:0, one launch (start us, length us, event | category | flops | bytes accessed | tf_op | source)
XLA Modules:
  0.0 47.4 jit_solution(12860082120769544405)
XLA Ops:
  0.0 1.5 %fusion = (bf16[1,8,16,2,512]{4,3,2,1,0:T(2,128)(2,1)S(1)}, bf16[1,8,16,2,512]{4,3,2,1,0:T(2,128)(2,1)S(1)}) fusion(bf16[1,8,32,2,512]{4,3,2,1,0:T(2,128)(2,1)} %param.4), kind=kLoop, calls=%fused_computation.4 | loop fusion | bytes 1048576 | tf_op jit(solution)/shard_map/slice | solution.py:356
  1.5 5.1 %collective-permute-start = (bf16[2,8,16,512]{3,2,1,0:T(8,128)(2,1)S(1)}, bf16[2,8,16,512]{3,2,1,0:T(8,128)(2,1)S(1)}, u32[]{:S(2)}, u32[]{:S(2)}) collective-permute-start(bf16[2,8,16,512]{3,2,1,0:T(8,128)(2,1)S(1)} %bitcast.19), channel_id=1, source_target_pairs={{4,0},{8,4},{12,8},{0,12},{5,1},{9,5},{13,9},{1,13},{6,2},{10,6},{... | collective-permute-start | bytes 786440 | tf_op jit(solution)/shard_map/ppermute | solution.py:386
  6.7 0.5 %collective-permute-start.1 = (bf16[2,8,16,512]{3,2,1,0:T(8,128)(2,1)S(1)}, bf16[2,8,16,512]{3,2,1,0:T(8,128)(2,1)S(1)}, u32[]{:S(2)}, u32[]{:S(2)}) collective-permute-start(bf16[2,8,16,512]{3,2,1,0:T(8,128)(2,1)S(1)} %bitcast.17), channel_id=1, source_target_pairs={{4,0},{8,4},{12,8},{0,12},{5,1},{9,5},{13,9},{1,13},{6,2},{10,6},{... | collective-permute-start | bytes 786440 | tf_op jit(solution)/shard_map/ppermute | solution.py:386
  7.2 0.1 pad_add_fusion.1.scalars
  7.2 6.1 %shard_map.46 = (f32[2,256,256]{2,1,0:T(8,128)S(1)}, bf16[1,256,256]{2,1,0:T(8,128)(2,1)S(1)}, bf16[1,256,256]{2,1,0:T(8,128)(2,1)S(1)}, f32[3,8,32,512]{3,2,1,0:T(8,128)S(1)}) custom-call(s32[3]{0:T(128)S(1)} %pad_add_fusion.1.scalars, bf16[1024,256]{1,0:T(8,128)(2,1)S(1)} %copy-done, bf16[2,8,16,512]{3,2,1,0:T(8,128)(2,1)S(1)} %bitcast.20, ...), custom_call_target="tpu_custom_call" | custom-call | tf_op jit(solution)/shard_map/pallas_call | solution.py:185
  13.4 1.3 %collective-permute-start.5 = (bf16[2,8,16,512]{3,2,1,0:T(8,128)(2,1)S(1)}, bf16[2,8,16,512]{3,2,1,0:T(8,128)(2,1)S(1)}, u32[]{:S(2)}, u32[]{:S(2)}) collective-permute-start(bf16[2,8,16,512]{3,2,1,0:T(8,128)(2,1)S(1)} %collective-permute-done.refs_0_), channel_id=1, source_target_pairs={{4,0},{8,4},{5,1},{9,5},{6,2},{10,6},{7,3},{11,7},{20,16},{24,20},... | collective-permute-start | bytes 786440 | tf_op jit(solution)/shard_map/ppermute | solution.py:386
  14.7 3.1 %collective-permute-done.1.refs_1_ = bf16[2,8,16,512]{3,2,1,0:T(8,128)(2,1)S(1)} collective-permute-done((bf16[2,8,16,512]{3,2,1,0:T(8,128)(2,1)S(1)}, bf16[2,8,16,512]{3,2,1,0:T(8,128)(2,1)S(1)}, u32[]{:S(2)}, u32[]{:S(2)}) %collective-permute-start.1) | collective-permute-done | bytes 262176 | tf_op jit(solution)/shard_map/ppermute | solution.py:386
  17.8 1.3 %collective-permute-start.9 = (bf16[2,8,16,512]{3,2,1,0:T(8,128)(2,1)S(1)}, bf16[2,8,16,512]{3,2,1,0:T(8,128)(2,1)S(1)}, u32[]{:S(2)}, u32[]{:S(2)}) collective-permute-start(bf16[2,8,16,512]{3,2,1,0:T(8,128)(2,1)S(1)} %collective-permute-done.1.refs_1_), channel_id=1, source_target_pairs={{4,0},{8,4},{5,1},{9,5},{6,2},{10,6},{7,3},{11,7},{20,16},{24,20},... | collective-permute-start | bytes 786440 | tf_op jit(solution)/shard_map/ppermute | solution.py:386
  19.1 6.1 %shard_map.47 = (f32[2,256,256]{2,1,0:T(8,128)S(1)}, bf16[1,256,256]{2,1,0:T(8,128)(2,1)S(1)}, bf16[1,256,256]{2,1,0:T(8,128)(2,1)S(1)}) custom-call(s32[3]{0:T(128)S(1)} %pad_add_fusion.1.scalars, f32[3,8,32,512]{3,2,1,0:T(8,128)S(1)} %get-tuple-element.22.own_rows, bf16[1024,256]{1,0:T(8,128)(2,1)S(1)} %copy-done, ...), custom_call_target="tpu_custom_call" | custom-call | tf_op jit(solution)/shard_map/pallas_call | solution.py:203
  25.2 0.1 collective-permute-start.3
  25.3 0.5 %collective-permute-start.15 = (bf16[1,256,256]{2,1,0:T(8,128)(2,1)S(1)}, bf16[1,256,256]{2,1,0:T(8,128)(2,1)S(1)}, u32[]{:S(2)}, u32[]{:S(2)}) collective-permute-start(bf16[1,256,256]{2,1,0:T(8,128)(2,1)S(1)} %get-tuple-element.38), channel_id=1, source_target_pairs={{0,1},{1,0},{2,3},{3,2},{4,5},{5,4},{6,7},{7,6},{8,9},{9,8},{10,11... | collective-permute-start | bytes 393224 | tf_op jit(solution)/shard_map/ppermute | solution.py:365
  25.8 0.1 collective-permute-start.2
  25.8 0.8 %collective-permute-done.3.refs_1_ = bf16[1,256,256]{2,1,0:T(8,128)(2,1)S(1)} collective-permute-done((bf16[1,256,256]{2,1,0:T(8,128)(2,1)S(1)}, bf16[1,256,256]{2,1,0:T(8,128)(2,1)S(1)}, u32[]{:S(2)}, u32[]{:S(2)}) %collective-permute-start.3) | collective-permute-done | bytes 131104 | tf_op jit(solution)/shard_map/ppermute | solution.py:365
  26.6 1.6 %collective-permute-start.4 = (bf16[1,256,256]{2,1,0:T(8,128)(2,1)S(1)}, bf16[1,256,256]{2,1,0:T(8,128)(2,1)S(1)}, u32[]{:S(2)}, u32[]{:S(2)}) collective-permute-start(bf16[1,256,256]{2,1,0:T(8,128)(2,1)S(1)} %shard_map.48.refs_1_), channel_id=1, source_target_pairs={{0,2},{2,0},{1,3},{3,1},{4,6},{6,4},{5,7},{7,5},{8,10},{10,8},{9,1... | collective-permute-start | bytes 393224 | tf_op jit(solution)/shard_map/ppermute | solution.py:370
  28.2 0.6 %collective-permute-start.16 = (bf16[1,256,256]{2,1,0:T(8,128)(2,1)S(1)}, bf16[1,256,256]{2,1,0:T(8,128)(2,1)S(1)}, u32[]{:S(2)}, u32[]{:S(2)}) collective-permute-start(bf16[1,256,256]{2,1,0:T(8,128)(2,1)S(1)} %shard_map.54), channel_id=1, source_target_pairs={{0,2},{2,0},{1,3},{3,1},{4,6},{6,4},{5,7},{7,5},{8,10},{10,8},{9,1... | collective-permute-start | bytes 393224 | tf_op jit(solution)/shard_map/ppermute | solution.py:370
  28.8 3.5 %shard_map.50 = (f32[2,128,256]{2,1,0:T(8,128)S(1)}, bf16[1,128,256]{2,1,0:T(8,128)(2,1)S(1)}, bf16[1,128,256]{2,1,0:T(8,128)(2,1)S(1)}) custom-call(s32[3]{0:T(128)S(1)} %pad_add_fusion.1.scalars, f32[3,8,32,512]{3,2,1,0:T(8,128)S(1)} %get-tuple-element.22.own_rows, bf16[1024,256]{1,0:T(8,128)(2,1)S(1)} %copy-done, ...), custom_call_target="tpu_custom_call" | custom-call | tf_op jit(solution)/shard_map/pallas_call | solution.py:203
  32.4 0.0 copy-start.2
  32.4 0.3 collective-permute-start.7
  32.7 3.5 %shard_map.52 = (f32[2,128,256]{2,1,0:T(8,128)S(1)}, bf16[1,128,256]{2,1,0:T(8,128)(2,1)S(1)}, bf16[1,128,256]{2,1,0:T(8,128)(2,1)S(1)}) custom-call(s32[3]{0:T(128)S(1)} %pad_add_fusion.1.scalars, f32[3,8,32,512]{3,2,1,0:T(8,128)S(1)} %get-tuple-element.22.own_rows, bf16[1024,256]{1,0:T(8,128)(2,1)S(1)} %copy-done, ...), custom_call_target="tpu_custom_call" | custom-call | tf_op jit(solution)/shard_map/pallas_call | solution.py:203
  36.3 0.3 collective-permute-start.11
  36.6 0.1 shard_map.49
  36.7 1.3 %collective-permute-start.13 = (bf16[1,256,256]{2,1,0:T(8,128)(2,1)S(1)}, bf16[1,256,256]{2,1,0:T(8,128)(2,1)S(1)}, u32[]{:S(2)}, u32[]{:S(2)}) collective-permute-start(bf16[1,256,256]{2,1,0:T(8,128)(2,1)S(1)} %get-tuple-element.36), channel_id=1, source_target_pairs={{12,0},{13,1},{14,2},{15,3},{28,16},{29,17},{30,18},{31,19}} | collective-permute-start | bytes 393224 | tf_op jit(solution)/shard_map/ppermute | solution.py:393
  38.0 0.3 collective-permute-start.6
  38.3 0.3 collective-permute-start.10
  38.7 1.6 %collective-permute-start.8 = (bf16[1,128,256]{2,1,0:T(8,128)(2,1)S(1)}, bf16[1,128,256]{2,1,0:T(8,128)(2,1)S(1)}, u32[]{:S(2)}, u32[]{:S(2)}) collective-permute-start(bf16[1,128,256]{2,1,0:T(8,128)(2,1)S(1)} %shard_map.51), channel_id=1, source_target_pairs={{0,2},{2,0},{1,3},{3,1},{4,6},{6,4},{5,7},{7,5},{8,10},{10,8},{9,1... | collective-permute-start | bytes 196616 | tf_op jit(solution)/shard_map/ppermute | solution.py:370
  40.2 0.5 %collective-permute-start.12 = (bf16[1,128,256]{2,1,0:T(8,128)(2,1)S(1)}, bf16[1,128,256]{2,1,0:T(8,128)(2,1)S(1)}, u32[]{:S(2)}, u32[]{:S(2)}) collective-permute-start(bf16[1,128,256]{2,1,0:T(8,128)(2,1)S(1)} %shard_map.53), channel_id=1, source_target_pairs={{0,2},{2,0},{1,3},{3,1},{4,6},{6,4},{5,7},{7,5},{8,10},{10,8},{9,1... | collective-permute-start | bytes 196616 | tf_op jit(solution)/shard_map/ppermute | solution.py:370
  40.8 0.1 pad_add_fusion.scalars
  40.9 2.0 %shard_map.55.refs_8_ = f32[3,8,32,256]{3,2,1,0:T(8,128)} custom-call(s32[7]{0:T(128)S(1)} %pad_add_fusion.scalars, f32[2,256,256]{2,1,0:T(8,128)S(1)} %get-tuple-element.37.refs_0_, bf16[1,256,256]{2,1,0:T(8,128)(2,1)S(1)} %collective-permute-done.14.refs_1_, bf16[1,256,256]{2,1,0:T(8,128)(2,1)S(1)} %collective-permute-done.16.refs_2_), custom_call_target="tpu_custom_call" | custom-call | tf_op jit(solution)/shard_map/pallas_call | solution.py:305
  42.9 0.5 collective-permute-done.8.refs_3_
  43.3 1.2 %collective-permute-done.12.refs_6_ = bf16[1,128,256]{2,1,0:T(8,128)(2,1)S(1)} collective-permute-done((bf16[1,128,256]{2,1,0:T(8,128)(2,1)S(1)}, bf16[1,128,256]{2,1,0:T(8,128)(2,1)S(1)}, u32[]{:S(2)}, u32[]{:S(2)}) %collective-permute-start.12) | collective-permute-done | bytes 65568 | tf_op jit(solution)/shard_map/ppermute | solution.py:370
  44.5 1.5 %collective-permute-done.13.refs_7_ = bf16[1,256,256]{2,1,0:T(8,128)(2,1)S(1)} collective-permute-done((bf16[1,256,256]{2,1,0:T(8,128)(2,1)S(1)}, bf16[1,256,256]{2,1,0:T(8,128)(2,1)S(1)}, u32[]{:S(2)}, u32[]{:S(2)}) %collective-permute-start.13) | collective-permute-done | bytes 131104 | tf_op jit(solution)/shard_map/ppermute | solution.py:393
  46.0 1.4 %shard_map.56 = f32[3,8,32,256]{3,2,1,0:T(8,128)} custom-call(s32[7]{0:T(128)S(1)} %pad_add_fusion.scalars, f32[1,256,256]{2,1,0:T(8,128)S(1)} %get-tuple-element.26.refs_0_, f32[2,128,256]{2,1,0:T(8,128)S(1)} %get-tuple-element.29.refs_0_.refs_1_, bf16[1,128,256]{2,1,0:T(8,128)(2,1)S(1)} %collective-permute-done.6.refs_2_, ...), custom_call_target="tpu_custom_call", output_to_operand_aliasing={{}: (9, {})} | custom-call | tf_op jit(solution)/shard_map/pallas_call | solution.py:323
  (24 shorter events, 0.2 us)
Async XLA Ops:
  0.0 7.2 %copy-start = (bf16[1024,256]{1,0:T(8,128)(2,1)S(1)}, bf16[1024,256]{1,0:T(8,128)(2,1)}, u32[]{:S(2)}) copy-start(bf16[1024,256]{1,0:T(8,128)(2,1)} %constant.17.clone.table) | copy-start | bytes 1572868
  1.5 11.8 %collective-permute-start = (bf16[2,8,16,512]{3,2,1,0:T(8,128)(2,1)S(1)}, bf16[2,8,16,512]{3,2,1,0:T(8,128)(2,1)S(1)}, u32[]{:S(2)}, u32[]{:S(2)}) collective-permute-start(bf16[2,8,16,512]{3,2,1,0:T(8,128)(2,1)S(1)} %bitcast.19), channel_id=1, source_target_pairs={{4,0},{8,4},{12,8},{0,12},{5,1},{9,5},{13,9},{1,13},{6,2},{10,6},{... | collective-permute-start | bytes 786440 | tf_op jit(solution)/shard_map/ppermute | solution.py:386
  6.7 11.1 %collective-permute-start.1 = (bf16[2,8,16,512]{3,2,1,0:T(8,128)(2,1)S(1)}, bf16[2,8,16,512]{3,2,1,0:T(8,128)(2,1)S(1)}, u32[]{:S(2)}, u32[]{:S(2)}) collective-permute-start(bf16[2,8,16,512]{3,2,1,0:T(8,128)(2,1)S(1)} %bitcast.17), channel_id=1, source_target_pairs={{4,0},{8,4},{12,8},{0,12},{5,1},{9,5},{13,9},{1,13},{6,2},{10,6},{... | collective-permute-start | bytes 786440 | tf_op jit(solution)/shard_map/ppermute | solution.py:386
  13.4 14.8 %collective-permute-start.5 = (bf16[2,8,16,512]{3,2,1,0:T(8,128)(2,1)S(1)}, bf16[2,8,16,512]{3,2,1,0:T(8,128)(2,1)S(1)}, u32[]{:S(2)}, u32[]{:S(2)}) collective-permute-start(bf16[2,8,16,512]{3,2,1,0:T(8,128)(2,1)S(1)} %collective-permute-done.refs_0_), channel_id=1, source_target_pairs={{4,0},{8,4},{5,1},{9,5},{6,2},{10,6},{7,3},{11,7},{20,16},{24,20},... | collective-permute-start | bytes 786440 | tf_op jit(solution)/shard_map/ppermute | solution.py:386
  17.8 14.6 %collective-permute-start.9 = (bf16[2,8,16,512]{3,2,1,0:T(8,128)(2,1)S(1)}, bf16[2,8,16,512]{3,2,1,0:T(8,128)(2,1)S(1)}, u32[]{:S(2)}, u32[]{:S(2)}) collective-permute-start(bf16[2,8,16,512]{3,2,1,0:T(8,128)(2,1)S(1)} %collective-permute-done.1.refs_1_), channel_id=1, source_target_pairs={{4,0},{8,4},{5,1},{9,5},{6,2},{10,6},{7,3},{11,7},{20,16},{24,20},... | collective-permute-start | bytes 786440 | tf_op jit(solution)/shard_map/ppermute | solution.py:386
  25.2 1.4 %collective-permute-start.3 = (bf16[1,256,256]{2,1,0:T(8,128)(2,1)S(1)}, bf16[1,256,256]{2,1,0:T(8,128)(2,1)S(1)}, u32[]{:S(2)}, u32[]{:S(2)}) collective-permute-start(bf16[1,256,256]{2,1,0:T(8,128)(2,1)S(1)} %get-tuple-element.25), channel_id=1, source_target_pairs={{0,1},{1,0},{2,3},{3,2},{4,5},{5,4},{6,7},{7,6},{8,9},{9,8},{10,11... | collective-permute-start | bytes 393224 | tf_op jit(solution)/shard_map/ppermute | solution.py:365
  25.3 2.9 %collective-permute-start.15 = (bf16[1,256,256]{2,1,0:T(8,128)(2,1)S(1)}, bf16[1,256,256]{2,1,0:T(8,128)(2,1)S(1)}, u32[]{:S(2)}, u32[]{:S(2)}) collective-permute-start(bf16[1,256,256]{2,1,0:T(8,128)(2,1)S(1)} %get-tuple-element.38), channel_id=1, source_target_pairs={{0,1},{1,0},{2,3},{3,2},{4,5},{5,4},{6,7},{7,6},{8,9},{9,8},{10,11... | collective-permute-start | bytes 393224 | tf_op jit(solution)/shard_map/ppermute | solution.py:365
  25.8 10.5 %collective-permute-start.2 = (bf16[1,256,256]{2,1,0:T(8,128)(2,1)S(1)}, bf16[1,256,256]{2,1,0:T(8,128)(2,1)S(1)}, u32[]{:S(2)}, u32[]{:S(2)}) collective-permute-start(bf16[1,256,256]{2,1,0:T(8,128)(2,1)S(1)} %get-tuple-element.24), channel_id=1, source_target_pairs={{0,1},{1,0},{2,3},{3,2},{4,5},{5,4},{6,7},{7,6},{8,9},{9,8},{10,11... | collective-permute-start | bytes 393224 | tf_op jit(solution)/shard_map/ppermute | solution.py:365
  26.6 10.0 %collective-permute-start.4 = (bf16[1,256,256]{2,1,0:T(8,128)(2,1)S(1)}, bf16[1,256,256]{2,1,0:T(8,128)(2,1)S(1)}, u32[]{:S(2)}, u32[]{:S(2)}) collective-permute-start(bf16[1,256,256]{2,1,0:T(8,128)(2,1)S(1)} %shard_map.48.refs_1_), channel_id=1, source_target_pairs={{0,2},{2,0},{1,3},{3,1},{4,6},{6,4},{5,7},{7,5},{8,10},{10,8},{9,1... | collective-permute-start | bytes 393224 | tf_op jit(solution)/shard_map/ppermute | solution.py:370
  28.2 10.5 %collective-permute-start.14 = (bf16[1,256,256]{2,1,0:T(8,128)(2,1)S(1)}, bf16[1,256,256]{2,1,0:T(8,128)(2,1)S(1)}, u32[]{:S(2)}, u32[]{:S(2)}) collective-permute-start(bf16[1,256,256]{2,1,0:T(8,128)(2,1)S(1)} %get-tuple-element.27), channel_id=1, source_target_pairs={{0,1},{1,0},{2,3},{3,2},{4,5},{5,4},{6,7},{7,6},{8,9},{9,8},{10,11... | collective-permute-start | bytes 393224 | tf_op jit(solution)/shard_map/ppermute | solution.py:365
  28.2 12.0 %collective-permute-start.16 = (bf16[1,256,256]{2,1,0:T(8,128)(2,1)S(1)}, bf16[1,256,256]{2,1,0:T(8,128)(2,1)S(1)}, u32[]{:S(2)}, u32[]{:S(2)}) collective-permute-start(bf16[1,256,256]{2,1,0:T(8,128)(2,1)S(1)} %shard_map.54), channel_id=1, source_target_pairs={{0,2},{2,0},{1,3},{3,1},{4,6},{6,4},{5,7},{7,5},{8,10},{10,8},{9,1... | collective-permute-start | bytes 393224 | tf_op jit(solution)/shard_map/ppermute | solution.py:370
  32.4 8.4 %copy-start.1 = (s32[1,3]{1,0:T(1,128)S(1)}, s32[1,3]{1,0:T(1,128)}, u32[]{:S(2)}) copy-start(s32[1,3]{1,0:T(1,128)} %param.6) | copy-start | bytes 40
  32.4 8.4 %copy-start.2 = (s32[1,3]{1,0:T(1,128)S(1)}, s32[1,3]{1,0:T(1,128)}, u32[]{:S(2)}) copy-start(s32[1,3]{1,0:T(1,128)} %param.5) | copy-start | bytes 40
  32.4 5.6 %collective-permute-start.7 = (bf16[1,128,256]{2,1,0:T(8,128)(2,1)S(1)}, bf16[1,128,256]{2,1,0:T(8,128)(2,1)S(1)}, u32[]{:S(2)}, u32[]{:S(2)}) collective-permute-start(bf16[1,128,256]{2,1,0:T(8,128)(2,1)S(1)} %get-tuple-element.31), channel_id=1, source_target_pairs={{0,1},{1,0},{2,3},{3,2},{4,5},{5,4},{6,7},{7,6},{8,9},{9,8},{10,11... | collective-permute-start | bytes 196616 | tf_op jit(solution)/shard_map/ppermute | solution.py:365
  36.3 2.0 %collective-permute-start.11 = (bf16[1,128,256]{2,1,0:T(8,128)(2,1)S(1)}, bf16[1,128,256]{2,1,0:T(8,128)(2,1)S(1)}, u32[]{:S(2)}, u32[]{:S(2)}) collective-permute-start(bf16[1,128,256]{2,1,0:T(8,128)(2,1)S(1)} %get-tuple-element.35), channel_id=1, source_target_pairs={{0,1},{1,0},{2,3},{3,2},{4,5},{5,4},{6,7},{7,6},{8,9},{9,8},{10,11... | collective-permute-start | bytes 196616 | tf_op jit(solution)/shard_map/ppermute | solution.py:365
  36.7 9.3 %collective-permute-start.13 = (bf16[1,256,256]{2,1,0:T(8,128)(2,1)S(1)}, bf16[1,256,256]{2,1,0:T(8,128)(2,1)S(1)}, u32[]{:S(2)}, u32[]{:S(2)}) collective-permute-start(bf16[1,256,256]{2,1,0:T(8,128)(2,1)S(1)} %get-tuple-element.36), channel_id=1, source_target_pairs={{12,0},{13,1},{14,2},{15,3},{28,16},{29,17},{30,18},{31,19}} | collective-permute-start | bytes 393224 | tf_op jit(solution)/shard_map/ppermute | solution.py:393
  38.0 4.9 %collective-permute-start.6 = (bf16[1,128,256]{2,1,0:T(8,128)(2,1)S(1)}, bf16[1,128,256]{2,1,0:T(8,128)(2,1)S(1)}, u32[]{:S(2)}, u32[]{:S(2)}) collective-permute-start(bf16[1,128,256]{2,1,0:T(8,128)(2,1)S(1)} %get-tuple-element.30), channel_id=1, source_target_pairs={{0,1},{1,0},{2,3},{3,2},{4,5},{5,4},{6,7},{7,6},{8,9},{9,8},{10,11... | collective-permute-start | bytes 196616 | tf_op jit(solution)/shard_map/ppermute | solution.py:365
  38.3 4.6 %collective-permute-start.10 = (bf16[1,128,256]{2,1,0:T(8,128)(2,1)S(1)}, bf16[1,128,256]{2,1,0:T(8,128)(2,1)S(1)}, u32[]{:S(2)}, u32[]{:S(2)}) collective-permute-start(bf16[1,128,256]{2,1,0:T(8,128)(2,1)S(1)} %get-tuple-element.34), channel_id=1, source_target_pairs={{0,1},{1,0},{2,3},{3,2},{4,5},{5,4},{6,7},{7,6},{8,9},{9,8},{10,11... | collective-permute-start | bytes 196616 | tf_op jit(solution)/shard_map/ppermute | solution.py:365
  38.7 4.6 %collective-permute-start.8 = (bf16[1,128,256]{2,1,0:T(8,128)(2,1)S(1)}, bf16[1,128,256]{2,1,0:T(8,128)(2,1)S(1)}, u32[]{:S(2)}, u32[]{:S(2)}) collective-permute-start(bf16[1,128,256]{2,1,0:T(8,128)(2,1)S(1)} %shard_map.51), channel_id=1, source_target_pairs={{0,2},{2,0},{1,3},{3,1},{4,6},{6,4},{5,7},{7,5},{8,10},{10,8},{9,1... | collective-permute-start | bytes 196616 | tf_op jit(solution)/shard_map/ppermute | solution.py:370
  40.2 4.3 %collective-permute-start.12 = (bf16[1,128,256]{2,1,0:T(8,128)(2,1)S(1)}, bf16[1,128,256]{2,1,0:T(8,128)(2,1)S(1)}, u32[]{:S(2)}, u32[]{:S(2)}) collective-permute-start(bf16[1,128,256]{2,1,0:T(8,128)(2,1)S(1)} %shard_map.53), channel_id=1, source_target_pairs={{0,2},{2,0},{1,3},{3,1},{4,6},{6,4},{5,7},{7,5},{8,10},{10,8},{9,1... | collective-permute-start | bytes 196616 | tf_op jit(solution)/shard_map/ppermute | solution.py:370

commit v3 on v0

v3 whole, which is shorter than its diff:
```python
import functools
import math

import jax
import jax.numpy as jnp
import ml_dtypes
import numpy as np
from jax import lax
from jax.experimental import pallas as pl
from jax.experimental.pallas import tpu as pltpu
from jax.sharding import PartitionSpec as P

BAND = 32
LAGS = 256
MAX_STEPS = 4
EPSILON = 1e-06
LANES = 128
ROWS = 16
OWN = 4
VMEM_LIMIT = 40 << 20
FAR = 1 << 20
HALVES = 2
SLOT_AT = 4


def lag_table(bin_count):
    bins = np.arange(bin_count, dtype=np.float64)[:, None]
    lags = np.arange(LAGS, dtype=np.float64)[None, :] - LAGS // 2
    angle = np.pi * bins * lags / bin_count
    table = np.concatenate([np.cos(angle), -np.sin(angle)], axis=0).astype(np.float32)
    return table.astype(ml_dtypes.bfloat16)


def whiten(source):
    _, windows, channels, bins = source.shape
    width = 2 * LANES
    row = lax.broadcasted_iota(jnp.int32, (width, width), 0) // BAND
    col = lax.broadcasted_iota(jnp.int32, (width, width), 1) // BAND
    mean_matrix = jnp.where(row == col, 1.0 / BAND, 0.0).astype(jnp.bfloat16)
    for at in range(0, bins, width):
        lanes = pl.ds(at, width)
        real = source[0, :, :, lanes].astype(jnp.float32).reshape(windows * channels, width)
        imag = source[1, :, :, lanes].astype(jnp.float32).reshape(windows * channels, width)
        rest = real * real + imag * imag
        mean = jnp.zeros_like(rest)
        for _ in range(3):
            piece = rest.astype(jnp.bfloat16)
            mean += jnp.dot(piece, mean_matrix, preferred_element_type=jnp.float32)
            rest = rest - piece.astype(jnp.float32)
        scale = lax.rsqrt(mean + EPSILON)
        shape = (windows, channels, width)
        yield (
            lanes,
            (real * scale).astype(jnp.bfloat16).astype(jnp.float32).reshape(shape),
            (imag * scale).astype(jnp.bfloat16).astype(jnp.float32).reshape(shape),
        )


def row_factors(real, imag):
    return real + imag, real, imag


def col_factors(real, imag):
    return real, -(real + imag), real - imag


def store_factors(source, target, begin, factors):
    for lanes, real, imag in whiten(source):
        for k, value in enumerate(factors(real, imag)):
            target[k, :, pl.ds(begin, source.shape[2]), lanes] = value


def reach_of(scalars, step):
    slots = (scalars.shape[0] - SLOT_AT) // 2
    picked = [
        jnp.where(scalars[SLOT_AT + k] == step, scalars[SLOT_AT + slots + k], 0) for k in range(slots)
    ]
    return functools.reduce(lambda x, y: x + y, picked)


def cross_tile(rows, cols, cross, reach, first_distance):
    _, windows, row_count, bins = rows.shape
    groups = cols.shape[2] // ROWS

    def body(step, carry):
        row_at = pl.multiple_of((step // groups) * 8, 8)
        group = step % groups
        col_at = pl.multiple_of(group * ROWS, ROWS)
        nearest = first_distance + col_at - row_at
        active = (nearest - 7 < reach) & (-(nearest + ROWS - 1) < reach)

        @pl.when(active)
        def _():
            for at in range(0, bins, LANES):
                lanes = pl.ds(at, LANES)
                for first in range(0, 8, OWN):
                    sums = [[None] * 3 for _ in range(OWN)]
                    for w in range(windows):
                        for k in range(3):
                            right = cols[k, w, pl.ds(col_at, ROWS), lanes]
                            left = rows.at[k, w, pl.ds(row_at, 8), lanes]
                            for i in range(OWN):
                                product = right * left[pl.ds(first + i, 1)]
                                sums[i][k] = product if w == 0 else sums[i][k] + product
                    for i in range(OWN):
                        k1, k2, k3 = sums[i]
                        at_row = (group * row_count + row_at + first + i) * ROWS
                        place = pl.ds(pl.multiple_of(at_row, ROWS), ROWS)
                        cross[place, pl.ds(at, LANES)] = (k1 - k3).astype(jnp.bfloat16)
                        cross[place, pl.ds(bins + at, LANES)] = (k1 + k2).astype(jnp.bfloat16)

        return carry

    lax.fori_loop(0, (row_count // 8) * groups, body, 0)


def lag_block(core, cross, begin, table, size, store):
    place = pl.ds(pl.multiple_of(begin, 2 * size), 2 * size)
    lags = jnp.dot(cross[place], table[...], preferred_element_type=jnp.float32)
    low, high = lags[:size], lags[size:]
    pl.when(core == 0)(lambda: store(low, high.astype(jnp.bfloat16)))
    pl.when(core != 0)(lambda: store(high, low.astype(jnp.bfloat16)))


def store_at(keep, sends, shift, half):
    def store(kept, sent):
        size = sent.shape[0]
        keep[shift, pl.ds(half * size, size)] = kept
        sends[shift * HALVES + half][0] = sent

    return store


def lag_sums(scalars, cross, table, keep, sends):
    owners, size = keep.shape[0], keep.shape[1] // HALVES
    core, day = scalars[0], scalars[1]
    for shift in range(owners):
        owner = lax.rem(day + shift, owners)
        for half in range(HALVES):
            begin = (half * owners + owner) * (2 * size)
            lag_block(core, cross, begin, table, size, store_at(keep, sends, shift, half))


def begins_of(parts):
    return [sum(p.shape[2] for p in parts[:k]) for k in range(len(parts))]


def own_kernel(part_count, scalars, table, *refs):
    parts = refs[:part_count]
    keep, *sends, rows, cols, cross = refs[part_count:]
    for part, begin in zip(parts, begins_of(parts)):
        for lanes, real, imag in whiten(part):
            for k in range(3):
                rows[k, :, pl.ds(begin, part.shape[2]), lanes] = row_factors(real, imag)[k]
                cols[k, :, pl.ds(begin, part.shape[2]), lanes] = col_factors(real, imag)[k]
    cross_tile(rows, cols, cross, reach_of(scalars, 0), 0)
    lag_sums(scalars, cross, table, keep, sends)


def partner_kernel(part_count, after_count, step, scalars, own_rows, table, *refs):
    parts = refs[:part_count]
    keep, *sends, cols, cross = refs[part_count + after_count :]
    reach = reach_of(scalars, step)

    @pl.when(reach > 0)
    def _():
        for part, begin in zip(parts, begins_of(parts)):
            store_factors(part, cols, begin, col_factors)
        cross_tile(own_rows, cols, cross, reach, step * own_rows.shape[2])
        lag_sums(scalars, cross, table, keep, sends)


def half_cross(can_swap, step, half, scalars, own_rows, part, cols, cross, swap_refs, finish):
    width, count = own_rows.shape[2], part.shape[2]
    reach = reach_of(scalars, step)

    @pl.when(reach > 0)
    def _():
        store_factors(part, cols, 0, col_factors)
        cross_tile(own_rows, cols, cross, reach, step * width + half * count)
        finish(False)

    if can_swap:
        rows, wide_cols = swap_refs

        @pl.when(scalars[2] != 0)
        def _():
            for at in range(0, own_rows.shape[3], LANES):
                lanes = pl.ds(at, LANES)
                real, imag = own_rows[1, :, :, lanes], own_rows[2, :, :, lanes]
                for k, value in enumerate(col_factors(real, imag)):
                    wide_cols[k, :, :, lanes] = value
            store_factors(part, rows, 0, row_factors)
            cross_tile(rows, wide_cols, cross, FAR, 0)
            finish(True)


def first_half_kernel(can_swap, step, scalars, own_rows, table, part, keep, send, cols, cross, *swap_refs):
    owners, size = keep.shape[0], keep.shape[1]

    def finish(swapped):
        for k in range(owners):

            def store(kept, sent, k=k):
                keep[k] = kept
                send[k] = sent

            lag_block(scalars[0], cross, k * 2 * size, table, size, store)

    half_cross(can_swap, step, 0, scalars, own_rows, part, cols, cross, swap_refs, finish)


def second_half_kernel(
    can_swap, step, after_count, scalars, own_rows, table, part, first_keep, first_send, *refs
):
    keep, *refs = refs[after_count:]
    sends = refs[: keep.shape[0] * HALVES]
    cols, cross, *swap_refs = refs[keep.shape[0] * HALVES :]
    owners, size = keep.shape[0], keep.shape[1] // HALVES
    core, day = scalars[0], scalars[1]

    def finish(swapped):
        for shift in range(owners):
            owner = lax.rem(day + shift, owners)
            if not swapped:
                store_at(keep, sends, shift, 0)(first_keep[owner], first_send[owner])
                lag_block(core, cross, owner * 2 * size, table, size, store_at(keep, sends, shift, 1))
                continue
            for half in range(HALVES):
                store = store_at(keep, sends, shift, half)
                pl.when(owner == 0)(lambda store=store, half=half: store(first_keep[half], first_send[half]))
                pl.when(owner != 0)(
                    lambda store=store, half=half: lag_block(
                        core, cross, half * 2 * size, table, size, store
                    )
                )

    half_cross(can_swap, step, 1, scalars, own_rows, part, cols, cross, swap_refs, finish)


VMEM = pl.BlockSpec(memory_space=pltpu.VMEM)
SMEM = pl.BlockSpec(memory_space=pltpu.SMEM)
ANY = pl.BlockSpec(memory_space=pl.ANY)
FREE = pl.CostEstimate(flops=0, bytes_accessed=0, transcendentals=0)
PARAMS = pltpu.CompilerParams(vmem_limit_bytes=VMEM_LIMIT)


def sums_shapes(owners, width):
    size = width * width // (2 * owners * HALVES)
    return [jax.ShapeDtypeStruct((owners, HALVES * size, LAGS), jnp.float32)] + [
        jax.ShapeDtypeStruct((1, size, LAGS), jnp.bfloat16)
    ] * (owners * HALVES)


def own_tile(scalars, parts, table, owners):
    _, windows, _, bins = parts[0].shape
    width = sum(part.shape[2] for part in parts)
    factors = (3, windows, width, bins)
    keep, *sends, rows = pl.pallas_call(
        functools.partial(own_kernel, len(parts)),
        out_shape=sums_shapes(owners, width) + [jax.ShapeDtypeStruct(factors, jnp.float32)],
        in_specs=[SMEM] + [VMEM] * (1 + len(parts)),
        out_specs=[VMEM] * (owners * HALVES + 2),
        scratch_shapes=[
            pltpu.VMEM(factors, jnp.float32),
            pltpu.VMEM((width * width, 2 * bins), jnp.bfloat16),
        ],
        compiler_params=PARAMS,
        cost_estimate=FREE,
    )(scalars, table, *parts)
    return keep, sends, rows


def partner_tile(scalars, own_rows, parts, table, owners, step, after):
    _, windows, width, bins = own_rows.shape
    keep, *sends = pl.pallas_call(
        functools.partial(partner_kernel, len(parts), len(after), step),
        out_shape=sums_shapes(owners, width),
        in_specs=[SMEM] + [VMEM] * (2 + len(parts)) + [ANY] * len(after),
        out_specs=[VMEM] * (owners * HALVES + 1),
        scratch_shapes=[
            pltpu.VMEM((3, windows, width, bins), jnp.float32),
            pltpu.VMEM((width * width, 2 * bins), jnp.bfloat16),
        ],
        compiler_params=PARAMS,
        cost_estimate=FREE,
    )(scalars, own_rows, table, *parts, *after)
    return keep, sends


def half_scratch(own_rows, can_swap):
    _, windows, width, bins = own_rows.shape
    half = width // HALVES
    wide, narrow = (3, windows, width, bins), (3, windows, half, bins)
    scratch = [pltpu.VMEM(narrow, jnp.float32), pltpu.VMEM((width * half, 2 * bins), jnp.bfloat16)]
    if can_swap:
        scratch += [pltpu.VMEM(narrow, jnp.float32), pltpu.VMEM(wide, jnp.float32)]
    return scratch


def first_half_tile(scalars, own_rows, part, table, owners, step, can_swap):
    width = own_rows.shape[2]
    size = width * width // (2 * owners * HALVES)
    return pl.pallas_call(
        functools.partial(first_half_kernel, can_swap, step),
        out_shape=[
            jax.ShapeDtypeStruct((owners, size, LAGS), jnp.float32),
            jax.ShapeDtypeStruct((owners, size, LAGS), jnp.bfloat16),
        ],
        in_specs=[SMEM, VMEM, VMEM, VMEM],
        out_specs=[VMEM, VMEM],
        scratch_shapes=half_scratch(own_rows, can_swap),
        compiler_params=PARAMS,
        cost_estimate=FREE,
    )(scalars, own_rows, table, part)


def second_half_tile(scalars, own_rows, part, first, table, owners, step, can_swap, after):
    keep, *sends = pl.pallas_call(
        functools.partial(second_half_kernel, can_swap, step, len(after)),
        out_shape=sums_shapes(owners, own_rows.shape[2]),
        in_specs=[SMEM] + [VMEM] * 5 + [ANY] * len(after),
        out_specs=[VMEM] * (owners * HALVES + 1),
        scratch_shapes=half_scratch(own_rows, can_swap),
        compiler_params=PARAMS,
        cost_estimate=FREE,
    )(scalars, own_rows, table, part, *first, *after)
    return keep, sends


def add_kernel(tiles, shift, *refs):
    out = refs[-1]
    for tile in range(tiles):
        keep, *got = refs[tile * (1 + HALVES) : (tile + 1) * (1 + HALVES)]
        for half, sent in enumerate(got):
            place = pl.ds(half * sent.shape[1], sent.shape[1])
            out[tile, place] = (keep[shift, place] + sent[0].astype(jnp.float32)).astype(out.dtype)


def add_cores(tiles, shift, after=()):
    operands = [term for keep, got in tiles for term in [keep] + got[shift]]
    rows = tiles[0][0].shape[1]
    return pl.pallas_call(
        functools.partial(add_kernel, len(tiles), shift),
        out_shape=jax.ShapeDtypeStruct((len(tiles), rows, LAGS), jnp.bfloat16),
        in_specs=[VMEM] * len(operands) + [ANY] * len(after),
        out_specs=VMEM,
        compiler_params=PARAMS,
        cost_estimate=FREE,
    )(*operands, *after)


def write_tile(scalars, step, terms, tile, norm_scale):
    row_count, width, _ = tile.shape
    slots = (scalars.shape[0] - SLOT_AT) // 2
    reach = reach_of(scalars, step)
    half_width = width // HALVES
    size = row_count * half_width
    for half in range(HALVES):
        value = None
        for term in terms:
            if isinstance(term, list):
                part = term[half][0]
            else:
                array, at = term
                part = array[at, pl.ds(half * size, size)]
            part = part.astype(jnp.float32)
            value = part if value is None else value + part
        value = value.reshape(row_count, half_width, LAGS)
        row = lax.broadcasted_iota(jnp.int32, value.shape, 0) + scalars[3] * row_count
        col = lax.broadcasted_iota(jnp.int32, value.shape, 1) + half * half_width
        distance = jnp.abs(step * width + col - row)
        kept = (distance > 0) & (distance < reach)
        tile[:, pl.ds(half * half_width, half_width), :] = jnp.where(kept, value * norm_scale, 0.0)


def grouped(refs, counts):
    terms = []
    for at, count in counts:
        if at is not None:
            terms.append((refs.pop(0), at))
        else:
            terms.append([refs.pop(0) for _ in range(count)])
    return terms


def tile_kernel(step, counts, norm_scale, scalars, *refs):
    *terms, tile = refs
    write_tile(scalars, step, grouped(terms, counts), tile, norm_scale)


def flat(terms):
    operands, counts = [], []
    for term in terms:
        listed = isinstance(term, list)
        operands += term if listed else [term[0]]
        counts.append((None, len(term)) if listed else (term[1], 1))
    return operands, counts


def finished_tile(scalars, step, terms, row_count, width, norm_scale):
    operands, counts = flat(terms)
    return pl.pallas_call(
        functools.partial(tile_kernel, step, counts, norm_scale),
        out_shape=jax.ShapeDtypeStruct((row_count, width, LAGS), jnp.float32),
        in_specs=[SMEM] + [VMEM] * len(operands),
        out_specs=VMEM,
        compiler_params=PARAMS,
        cost_estimate=FREE,
    )(scalars, *operands)


def output_kernel(ready_steps, late, norm_scale, scalars, *refs):
    out, tiles, zeros, sems = refs[-4:]
    slots = out.shape[0]
    ready, rest = refs[: len(ready_steps)], list(refs[len(ready_steps) : -4])

    def copies(slot, source):
        return pltpu.make_async_copy(source, out.at[slot], sems.at[slot])

    def start(step, source):
        for slot in range(slots):
            pl.when(scalars[SLOT_AT + slot] == step)(copies(slot, source).start)

    for step, tile in zip(ready_steps, ready):
        start(step, tile)
    zeros[...] = jnp.zeros_like(zeros)
    start(-1, zeros)
    for place, (step, counts) in enumerate(late):
        terms = grouped(rest, counts)

        @pl.when(reach_of(scalars, step) > 0)
        def _(step=step, terms=terms, place=place):
            write_tile(scalars, step, terms, tiles.at[place], norm_scale)

        start(step, tiles.at[place])
    for slot in range(slots):
        copies(slot, zeros).wait()


def write_output(scalars, ready, late, slots, norm_scale):
    tile_shape = ready[0][1].shape
    operands, listed = [tile for _, tile in ready], []
    for step, terms in late:
        more, counts = flat(terms)
        operands += more
        listed.append((step, counts))
    return pl.pallas_call(
        functools.partial(output_kernel, [step for step, _ in ready], listed, norm_scale),
        out_shape=jax.ShapeDtypeStruct((slots,) + tile_shape, jnp.float32),
        in_specs=[SMEM] + [VMEM] * len(operands),
        out_specs=ANY,
        scratch_shapes=[
            pltpu.VMEM((len(late),) + tile_shape, jnp.float32),
            pltpu.VMEM(tile_shape, jnp.float32),
            pltpu.SemaphoreType.DMA((slots,)),
        ],
        compiler_params=PARAMS,
        cost_estimate=FREE,
    )(scalars, *operands)


def on_device(spectra, tile_offset, pair_reach):
    blocks = lax.axis_size("chan")
    days, cores = lax.axis_size("day"), lax.axis_size("sub")
    steps = min(MAX_STEPS, blocks - 1)
    wraps = blocks >= 3 and steps == blocks - 1 and days == 2
    local_days, local_windows, width, _, bins = spectra.shape
    norm_scale = 1.0 / math.sqrt(bins * local_days * days * local_windows * cores)
    row_count = width // (days * cores)
    slots = tile_offset.shape[1]
    day, core, block = lax.axis_index("day"), lax.axis_index("sub"), lax.axis_index("chan")
    table = jnp.asarray(lag_table(bins))

    half = width // HALVES
    halves = [
        jnp.transpose(spectra[:, :, at : at + half], (3, 0, 1, 2, 4)).reshape(2, -1, half, bins)
        for at in range(0, width, half)
    ]
    is_last = (block == blocks - 1).astype(jnp.int32) if wraps else jnp.int32(0)
    scalars = jnp.stack([core, day, is_last, day * cores + core]).astype(jnp.int32)
    scalars = jnp.concatenate([scalars, tile_offset[0], pair_reach[0]])

    def over_cores(sends):
        got = [lax.ppermute(send, "sub", [(k, (k + 1) % cores) for k in range(cores)]) for send in sends]
        return [got[k * HALVES : (k + 1) * HALVES] for k in range(days)]

    def over_days(pieces):
        return [
            lax.ppermute(piece, "day", [(k, (k + shift) % days) for k in range(days)])
            for shift, piece in enumerate(pieces, 1)
        ]

    def to_first(piece, shift):
        pairs = [((blocks - 1) * days + k, (k + shift) % days) for k in range(days)]
        return lax.ppermute(piece, ("chan", "day"), pairs)

    keep, sends, own_rows = own_tile(scalars, halves, table, days)
    own_sums = (keep, over_cores(sends))
    ready, late, back = [], [], []

    pairs = [(a + 1, a) for a in range(blocks - 1)] + [(0, blocks - 1)] * wraps
    moving = [lax.ppermute(part, "chan", pairs) for part in halves]
    first = first_half_tile(scalars, own_rows, moving[0], table, days, 1, wraps)
    ahead = moving
    after = [x for pair in own_sums[1] for x in pair] if 0 else []
    keep, sends1 = second_half_tile(scalars, own_rows, moving[1], first, table, days, 1, wraps, after)
    sums = (keep, over_cores(sends1))
    pieces = [add_cores([sums, own_sums], shift) for shift in range(1, days)]
    if wraps:
        back = [to_first(add_cores([sums], shift), shift) for shift in range(days)]
    moved = over_days(pieces)
    for step, (keep, got) in enumerate([own_sums, sums]):
        terms = [(keep, 0), got[0]] + [(piece, 1 - step) for piece in moved]
        ready.append((step, finished_tile(scalars, step, terms, row_count, width, norm_scale)))

    waits = [sends[0], first[0]]
    for step in range(2, steps + 1 - wraps):
        pairs = [(a + 1, a) for a in range(blocks - step)]
        ahead = [
            lax.ppermute(lax.optimization_barrier((part, wait))[0], "chan", pairs)
            for part, wait in zip(ahead, waits)
        ]
        keep, sends2 = partner_tile(scalars, own_rows, ahead, table, days, step, pieces)
        sums = (keep, over_cores(sends2))
        last = [add_cores([sums], shift, back) for shift in range(1, days)]
        terms = [(keep, 0), sums[1][0]] + [(piece, 0) for piece in over_days(last)]
        late.append((step, terms))
    if wraps:
        late.append((steps, [(piece, 0) for piece in back]))
    return write_output(scalars, ready, late, slots, norm_scale)[None]


def solution(mesh):
    in_specs = (P(("groups", "day"), "sub", "chan", None, None), P("chan", None), P("chan", None))
    out_specs = P(("groups", "chan"), None, ("day", "sub"), None, None)
    return jax.shard_map(
        on_device, mesh=mesh, in_specs=in_specs, out_specs=out_specs, check_vma=False
    )
```

time: 206 us -> 46.2 us (0.22)
  local copies, waits for them, and re-layouts: 65.5 us -> 1.63 us
  waiting for transfers between devices: 61.5 us -> 11 us
  matrix products: 44.2 us -> 0 us
  between operations: 19.3 us -> 0.2 us
  Pallas kernels: 0 us -> 17 us
  starting transfers between devices: 4.04 us -> 16.4 us
  other arithmetic: 10.6 us -> 0 us
    dot_general x9 -> x0, matrix products: 44.2 us -> none  [the longest x3 19.4 us: lag_tile(): jnp.einsum('dwicf,dwjcf->ijf', own_turned, partner, preferred_element_typ...]
    unnamed x2 -> x0, waiting for transfers between devices: 39.7 us -> none
    transpose x6 -> x0, local copies, waits for them, and re-layouts: 39.1 us -> none  [the longest x3 20 us: lag_tile(): jnp.einsum('dwicf,dwjcf->ijf', own_rows, partner, preferred_element_type=...]
    pallas_call x0 -> x11, Pallas kernels: none -> 17 us  [the longest x1 6.43 us: own_tile(): pl.pallas_call(functools.partial(own_kernel, len(parts)), out_shape=sums_...]
    ppermute x3 -> x20, starting transfers between devices: 4.03 us -> 16.4 us  [the longest x2 5.61 us: on_device(): moving = [lax.ppermute(part, 'chan', pairs) for part in halves]]
    ppermute x3 -> x20, waiting for transfers between devices: 21.8 us -> 11 us  [the longest x2 8.6 us: to_first(): return lax.ppermute(piece, ('chan', 'day'), pairs)]
    dynamic_slice x4 -> x0, local copies, waits for them, and re-layouts: 10.3 us -> none  [lag_tile(): lax.dynamic_index_in_dim(partners, jnp.maximum(offset, 0), 0, keepdims=Fa...]
    another operation x2 -> x0, local copies, waits for them, and re-layouts: 6.65 us -> none
  transfers between devices with their start and end apart: 4 -> 20, of which waited for: 4 -> 5; matrix products, arithmetic and copies ran while one was open for 7% -> 0% of each run, Pallas kernels for 0% -> 34%
where the time goes in v3:
time: 46.2 us
  Pallas kernels  17 us (37%)
  starting transfers between devices  16.4 us (35%)
  waiting for transfers between devices  11 us (24%)
  local copies, waits for them, and re-layouts  1.63 us (4%)
    ppermute x2, waiting for transfers between devices, to_first(): return lax.ppermute(piece, ('chan', 'day'), pairs)  8.6 us
    pallas_call x1, Pallas kernels, own_tile(): pl.pallas_call(functools.partial(own_kernel, len(parts)), out_shape=sums_...  6.43 us
    ppermute x2, starting transfers between devices, on_device(): moving = [lax.ppermute(part, 'chan', pairs) for part in halves]  5.61 us
    pallas_call x1, Pallas kernels, first_half_tile(): pl.pallas_call(functools.partial(first_half_kernel, can_swap, step), out_...  3.58 us
    pallas_call x1, Pallas kernels, second_half_tile(): pl.pallas_call(functools.partial(second_half_kernel, can_swap, step, len(...  3.58 us
    ppermute x12, starting transfers between devices, over_cores(): lax.ppermute(send, 'sub', [(k, (k + 1) % cores) for k in range(cores)])  3.05 us
    ppermute x2, starting transfers between devices, over_days(): lax.ppermute(piece, 'day', [(k, (k + shift) % days) for k in range(days)])  2.6 us
    ppermute x2, starting transfers between devices, on_device(): lax.ppermute(lax.optimization_barrier((part, wait))[0], 'chan', pairs)  2.58 us
  transfers between devices with their start and end apart: 20, of which 5 were waited for; matrix products, arithmetic and copies ran while one was open for 0% of the time, Pallas kernels for 34%

profile of v3, /device:TPU:0, one launch (start us, length us, event | category | flops | bytes accessed | tf_op | source)
XLA Modules:
  0.0 46.2 jit_solution(1480050679664683661)
XLA Ops:
  0.0 1.5 %fusion = (bf16[1,8,16,2,512]{4,3,2,1,0:T(2,128)(2,1)S(1)}, bf16[1,8,16,2,512]{4,3,2,1,0:T(2,128)(2,1)S(1)}) fusion(bf16[1,8,32,2,512]{4,3,2,1,0:T(2,128)(2,1)} %param.4), kind=kLoop, calls=%fused_computation.2 | loop fusion | bytes 1048576 | tf_op jit(solution)/shard_map/slice | solution.py:477
  1.5 5.1 %collective-permute-start.3 = (bf16[2,8,16,512]{3,2,1,0:T(8,128)(2,1)S(1)}, bf16[2,8,16,512]{3,2,1,0:T(8,128)(2,1)S(1)}, u32[]{:S(2)}, u32[]{:S(2)}) collective-permute-start(bf16[2,8,16,512]{3,2,1,0:T(8,128)(2,1)S(1)} %bitcast.19), channel_id=1, source_target_pairs={{4,0},{8,4},{12,8},{0,12},{5,1},{9,5},{13,9},{1,13},{6,2},{10,6},{... | collective-permute-start | bytes 786440 | tf_op jit(solution)/shard_map/ppermute | solution.py:503
  6.7 0.5 %collective-permute-start.2 = (bf16[2,8,16,512]{3,2,1,0:T(8,128)(2,1)S(1)}, bf16[2,8,16,512]{3,2,1,0:T(8,128)(2,1)S(1)}, u32[]{:S(2)}, u32[]{:S(2)}) collective-permute-start(bf16[2,8,16,512]{3,2,1,0:T(8,128)(2,1)S(1)} %bitcast.17), channel_id=1, source_target_pairs={{4,0},{8,4},{12,8},{0,12},{5,1},{9,5},{13,9},{1,13},{6,2},{10,6},{... | collective-permute-start | bytes 786440 | tf_op jit(solution)/shard_map/ppermute | solution.py:503
  7.2 0.1 concatenate.3.scalars
  7.3 6.4 %shard_map.46 = (f32[2,256,256]{2,1,0:T(8,128)S(1)}, bf16[1,128,256]{2,1,0:T(8,128)(2,1)S(1)}, bf16[1,128,256]{2,1,0:T(8,128)(2,1)S(1)}, bf16[1,128,256]{2,1,0:T...) custom-call(s32[10]{0:T(128)S(1)} %concatenate.3.scalars, ...), custom_call_target="tpu_custom_call" | custom-call | tf_op jit(solution)/shard_map/pallas_call | solution.py:259
  13.7 0.1 collective-permute-start.6
  13.8 1.3 %collective-permute-start.11 = (bf16[2,8,16,512]{3,2,1,0:T(8,128)(2,1)S(1)}, bf16[2,8,16,512]{3,2,1,0:T(8,128)(2,1)S(1)}, u32[]{:S(2)}, u32[]{:S(2)}) collective-permute-start(bf16[2,8,16,512]{3,2,1,0:T(8,128)(2,1)S(1)} %collective-permute-done.3.part), channel_id=1, source_target_pairs={{4,0},{8,4},{5,1},{9,5},{6,2},{10,6},{7,3},{11,7},{20,16},{24,20},... | collective-permute-start | bytes 786440 | tf_op jit(solution)/shard_map/ppermute | solution.py:521
  15.1 3.6 %shard_map.47 = (f32[2,128,256]{2,1,0:T(8,128)S(1)}, bf16[2,128,256]{2,1,0:T(8,128)(2,1)S(1)}) custom-call(s32[10]{0:T(128)S(1)} %concatenate.3.scalars, f32[3,8,32,512]{3,2,1,0:T(8,128)S(1)} %get-tuple-element.28.own_rows, bf16[1024,256]{1,0:T(8,128)(2,1)S(1)} %copy-done, bf16[2,8,16,512]{3,2,1,0:T(8,128)(2,1)S(1)} %collective-permute-done.3.part), custom_call_target="tpu_custom_call" | custom-call | tf_op jit(solution)/shard_map/pallas_call | solution.py:304
  18.7 1.3 %collective-permute-start.12 = (bf16[2,8,16,512]{3,2,1,0:T(8,128)(2,1)S(1)}, bf16[2,8,16,512]{3,2,1,0:T(8,128)(2,1)S(1)}, u32[]{:S(2)}, u32[]{:S(2)}) collective-permute-start(bf16[2,8,16,512]{3,2,1,0:T(8,128)(2,1)S(1)} %collective-permute-done.2.part), channel_id=1, source_target_pairs={{4,0},{8,4},{5,1},{9,5},{6,2},{10,6},{7,3},{11,7},{20,16},{24,20},... | collective-permute-start | bytes 786440 | tf_op jit(solution)/shard_map/ppermute | solution.py:521
  20.0 0.6 %collective-permute-start.7 = (bf16[1,128,256]{2,1,0:T(8,128)(2,1)S(1)}, bf16[1,128,256]{2,1,0:T(8,128)(2,1)S(1)}, u32[]{:S(2)}, u32[]{:S(2)}) collective-permute-start(bf16[1,128,256]{2,1,0:T(8,128)(2,1)S(1)} %get-tuple-element.35), channel_id=1, source_target_pairs={{0,1},{1,0},{2,3},{3,2},{4,5},{5,4},{6,7},{7,6},{8,9},{9,8},{10,11... | collective-permute-start | bytes 196616 | tf_op jit(solution)/shard_map/ppermute | solution.py:485
  20.5 3.6 %shard_map.48 = (f32[2,256,256]{2,1,0:T(8,128)S(1)}, bf16[1,128,256]{2,1,0:T(8,128)(2,1)S(1)}, bf16[1,128,256]{2,1,0:T(8,128)(2,1)S(1)}, bf16[1,128,256]{2,1,0:T(8,128)(2,1)S(1)}, bf16[1,128,256]{2,1,0:T(8,128)(2,1)S(1)}) custom-call(s32[10]{0:T(128)S(1)} %concatenate.3.scalars, f32[3,8,32,512]{3,2,1,0:T(8,128)S(1)} %get-tuple-element.28.own_rows, ...), custom_call_target="tpu_custom_call" | custom-call | tf_op jit(solution)/shard_map/pallas_call | solution.py:319
  24.1 0.1 collective-permute-start.4
  24.2 0.5 %collective-permute-start.5 = (bf16[1,128,256]{2,1,0:T(8,128)(2,1)S(1)}, bf16[1,128,256]{2,1,0:T(8,128)(2,1)S(1)}, u32[]{:S(2)}, u32[]{:S(2)}) collective-permute-start(bf16[1,128,256]{2,1,0:T(8,128)(2,1)S(1)} %get-tuple-element.33), channel_id=1, source_target_pairs={{0,1},{1,0},{2,3},{3,2},{4,5},{5,4},{6,7},{7,6},{8,9},{9,8},{10,11... | collective-permute-start | bytes 196616 | tf_op jit(solution)/shard_map/ppermute | solution.py:485
  24.7 0.1 collective-permute-start.9
  24.8 0.7 %collective-permute-done.4.refs_1_ = bf16[1,128,256]{2,1,0:T(8,128)(2,1)S(1)} collective-permute-done((bf16[1,128,256]{2,1,0:T(8,128)(2,1)S(1)}, bf16[1,128,256]{2,1,0:T(8,128)(2,1)S(1)}, u32[]{:S(2)}, u32[]{:S(2)}) %collective-permute-start.4) | collective-permute-done | bytes 65568 | tf_op jit(solution)/shard_map/ppermute | solution.py:485
  25.5 0.2 collective-permute-start.10
  25.7 1.6 %collective-permute-start.8 = (bf16[2,256,256]{2,1,0:T(8,128)(2,1)S(1)}, bf16[2,256,256]{2,1,0:T(8,128)(2,1)S(1)}, u32[]{:S(2)}, u32[]{:S(2)}) collective-permute-start(bf16[2,256,256]{2,1,0:T(8,128)(2,1)S(1)} %shard_map.49.refs_2_), channel_id=1, source_target_pairs={{0,2},{2,0},{1,3},{3,1},{4,6},{6,4},{5,7},{7,5},{8,10},{10,8},{9,1... | collective-permute-start | bytes 786440 | tf_op jit(solution)/shard_map/ppermute | solution.py:490
  27.3 1.3 %collective-permute-start.17 = (bf16[1,256,256]{2,1,0:T(8,128)(2,1)S(1)}, bf16[1,256,256]{2,1,0:T(8,128)(2,1)S(1)}, u32[]{:S(2)}, u32[]{:S(2)}) collective-permute-start(bf16[1,256,256]{2,1,0:T(8,128)(2,1)S(1)} %shard_map.53), channel_id=1, source_target_pairs={{12,0},{14,2},{13,1},{15,3},{28,16},{30,18},{29,17},{31,19}} | collective-permute-start | bytes 393224 | tf_op jit(solution)/shard_map/ppermute | solution.py:496
  28.6 1.3 %collective-permute-start.18 = (bf16[1,256,256]{2,1,0:T(8,128)(2,1)S(1)}, bf16[1,256,256]{2,1,0:T(8,128)(2,1)S(1)}, u32[]{:S(2)}, u32[]{:S(2)}) collective-permute-start(bf16[1,256,256]{2,1,0:T(8,128)(2,1)S(1)} %shard_map.54), channel_id=1, source_target_pairs={{12,2},{14,0},{13,3},{15,1},{28,18},{30,16},{29,19},{31,17}} | collective-permute-start | bytes 393224 | tf_op jit(solution)/shard_map/ppermute | solution.py:496
  29.9 0.1 collective-permute-done.12.refs_1_
  30.0 0.6 %shard_map.52 = (f32[2,256,256]{2,1,0:T(8,128)S(1)}, bf16[1,128,256]{2,1,0:T(8,128)(2,1)S(1)}, bf16[1,128,256]{2,1,0:T(8,128)(2,1)S(1)}, bf16[1,128,256]{2,1,0:T(8,128)(2,1)S(1)}, bf16[1,128,256]{2,1,0:T(8,128)(2,1)S(1)}) custom-call(s32[10]{0:T(128)S(1)} %concatenate.3.scalars, f32[3,8,32,512]{3,2,1,0:T(8,128)S(1)} %get-tuple-element.28.own_rows, ...), custom_call_target="tpu_custom_call" | custom-call | tf_op jit(solution)/shard_map/pallas_call | solution.py:276
  30.5 0.1 collective-permute-start.15
  30.6 0.5 %collective-permute-start.16 = (bf16[1,128,256]{2,1,0:T(8,128)(2,1)S(1)}, bf16[1,128,256]{2,1,0:T(8,128)(2,1)S(1)}, u32[]{:S(2)}, u32[]{:S(2)}) collective-permute-start(bf16[1,128,256]{2,1,0:T(8,128)(2,1)S(1)} %get-tuple-element.44), channel_id=1, source_target_pairs={{0,1},{1,0},{2,3},{3,2},{4,5},{5,4},{6,7},{7,6},{8,9},{9,8},{10,11... | collective-permute-start | bytes 196616 | tf_op jit(solution)/shard_map/ppermute | solution.py:485
  31.1 6.2 %collective-permute-done.17.refs_3_.refs_6_ = bf16[1,256,256]{2,1,0:T(8,128)(2,1)S(1)} collective-permute-done((bf16[1,256,256]{2,1,0:T(8,128)(2,1)S(1)}, bf16[1,256,256]{2,1,0:T(8,128)(2,1)S(1)}, u32[]{:S(2)}, u32[]{:S(2)}) %collective-permute-start.17) | collective-permute-done | bytes 131104 | tf_op jit(solution)/shard_map/ppermute | solution.py:496
  37.3 2.4 %collective-permute-done.18.refs_4_.refs_7_ = bf16[1,256,256]{2,1,0:T(8,128)(2,1)S(1)} collective-permute-done((bf16[1,256,256]{2,1,0:T(8,128)(2,1)S(1)}, bf16[1,256,256]{2,1,0:T(8,128)(2,1)S(1)}, u32[]{:S(2)}, u32[]{:S(2)}) %collective-permute-start.18) | collective-permute-done | bytes 131104 | tf_op jit(solution)/shard_map/ppermute | solution.py:496
  39.8 1.0 %collective-permute-start.19 = (bf16[1,256,256]{2,1,0:T(8,128)(2,1)S(1)}, bf16[1,256,256]{2,1,0:T(8,128)(2,1)S(1)}, u32[]{:S(2)}, u32[]{:S(2)}) collective-permute-start(bf16[1,256,256]{2,1,0:T(8,128)(2,1)S(1)} %shard_map.55), channel_id=1, source_target_pairs={{0,2},{2,0},{1,3},{3,1},{4,6},{6,4},{5,7},{7,5},{8,10},{10,8},{9,1... | collective-permute-start | bytes 393224 | tf_op jit(solution)/shard_map/ppermute | solution.py:490
  40.8 0.5 %collective-permute-start.1 = (bf16[1,128,256]{2,1,0:T(8,128)(2,1)S(1)}, bf16[1,128,256]{2,1,0:T(8,128)(2,1)S(1)}, u32[]{:S(2)}, u32[]{:S(2)}) collective-permute-start(bf16[1,128,256]{2,1,0:T(8,128)(2,1)S(1)} %get-tuple-element.27), channel_id=1, source_target_pairs={{0,1},{1,0},{2,3},{3,2},{4,5},{5,4},{6,7},{7,6},{8,9},{9,8},{10,11... | collective-permute-start | bytes 196616 | tf_op jit(solution)/shard_map/ppermute | solution.py:485
  41.3 0.5 %collective-permute-start.14 = (bf16[1,128,256]{2,1,0:T(8,128)(2,1)S(1)}, bf16[1,128,256]{2,1,0:T(8,128)(2,1)S(1)}, u32[]{:S(2)}, u32[]{:S(2)}) collective-permute-start(bf16[1,128,256]{2,1,0:T(8,128)(2,1)S(1)} %get-tuple-element.42), channel_id=1, source_target_pairs={{0,1},{1,0},{2,3},{3,2},{4,5},{5,4},{6,7},{7,6},{8,9},{9,8},{10,11... | collective-permute-start | bytes 196616 | tf_op jit(solution)/shard_map/ppermute | solution.py:485
  41.8 0.6 %shard_map.51.refs_1_ = f32[8,32,256]{2,1,0:T(8,128)S(1)} custom-call(s32[10]{0:T(128)S(1)} %concatenate.3.scalars, f32[2,256,256]{2,1,0:T(8,128)S(1)} %get-tuple-element.31.refs_0_, bf16[1,128,256]{2,1,0:T(8,128)(2,1)S(1)} %collective-permute-done.9.refs_1_, bf16[1,128,256]{2,1,0:T(8,128)(2,1)S(1)} %collective-permute-done.10.refs_2_, ...), custom_call_target="tpu_custom_call" | custom-call | tf_op jit(solution)/shard_map/pallas_call | solution.py:403
  42.5 0.6 %shard_map.50.refs_0_ = f32[8,32,256]{2,1,0:T(8,128)S(1)} custom-call(s32[10]{0:T(128)S(1)} %concatenate.3.scalars, f32[2,256,256]{2,1,0:T(8,128)S(1)} %get-tuple-element.25.refs_3_.refs_0_, bf16[1,128,256]{2,1,0:T(8,128)(2,1)S(1)} %collective-permute-done.refs_1_, bf16[1,128,256]{2,1,0:T(8,128)(2,1)S(1)} %collective-permute-done.1.refs_2_, ...), custom_call_target="tpu_custom_call" | custom-call | tf_op jit(solution)/shard_map/pallas_call | solution.py:403
  43.1 1.7 %collective-permute-done.19.refs_5_ = bf16[1,256,256]{2,1,0:T(8,128)(2,1)S(1)} collective-permute-done((bf16[1,256,256]{2,1,0:T(8,128)(2,1)S(1)}, bf16[1,256,256]{2,1,0:T(8,128)(2,1)S(1)}, u32[]{:S(2)}, u32[]{:S(2)}) %collective-permute-start.19) | collective-permute-done | bytes 131104 | tf_op jit(solution)/shard_map/ppermute | solution.py:490
  44.8 1.4 %shard_map.56 = f32[3,8,32,256]{3,2,1,0:T(8,128)} custom-call(s32[10]{0:T(128)S(1)} %concatenate.3.scalars, f32[8,32,256]{2,1,0:T(8,128)S(1)} %shard_map.50.refs_0_, f32[8,32,256]{2,1,0:T(8,128)S(1)} %shard_map.51.refs_1_, f32[2,256,256]{2,1,0:T(8,128)S(1)} %get-tuple-element.40.refs_0_.refs_2_, bf16[1,128,256]{2,1,0:T(8,128)(2,1)S(1)} %collective-permute-done.13.refs_3_, ...), custom_call_target="tpu_custom_call" | custom-call | tf_op jit(solution)/shard_map/pallas_call | solution.py:448
  (29 shorter events, 0.3 us)
Async XLA Ops:
  0.0 7.3 %copy-start = (bf16[1024,256]{1,0:T(8,128)(2,1)S(1)}, bf16[1024,256]{1,0:T(8,128)(2,1)}, u32[]{:S(2)}) copy-start(bf16[1024,256]{1,0:T(8,128)(2,1)} %constant.17.clone.table) | copy-start | bytes 1572868
  0.0 7.2 %copy-start.2 = (s32[1,3]{1,0:T(1,128)S(1)}, s32[1,3]{1,0:T(1,128)}, u32[]{:S(2)}) copy-start(s32[1,3]{1,0:T(1,128)} %param.6) | copy-start | bytes 40
  0.0 7.2 %copy-start.1 = (s32[1,3]{1,0:T(1,128)S(1)}, s32[1,3]{1,0:T(1,128)}, u32[]{:S(2)}) copy-start(s32[1,3]{1,0:T(1,128)} %param.5) | copy-start | bytes 40
  1.5 12.3 %collective-permute-start.3 = (bf16[2,8,16,512]{3,2,1,0:T(8,128)(2,1)S(1)}, bf16[2,8,16,512]{3,2,1,0:T(8,128)(2,1)S(1)}, u32[]{:S(2)}, u32[]{:S(2)}) collective-permute-start(bf16[2,8,16,512]{3,2,1,0:T(8,128)(2,1)S(1)} %bitcast.19), channel_id=1, source_target_pairs={{4,0},{8,4},{12,8},{0,12},{5,1},{9,5},{13,9},{1,13},{6,2},{10,6},{... | collective-permute-start | bytes 786440 | tf_op jit(solution)/shard_map/ppermute | solution.py:503
  6.7 12.0 %collective-permute-start.2 = (bf16[2,8,16,512]{3,2,1,0:T(8,128)(2,1)S(1)}, bf16[2,8,16,512]{3,2,1,0:T(8,128)(2,1)S(1)}, u32[]{:S(2)}, u32[]{:S(2)}) collective-permute-start(bf16[2,8,16,512]{3,2,1,0:T(8,128)(2,1)S(1)} %bitcast.17), channel_id=1, source_target_pairs={{4,0},{8,4},{12,8},{0,12},{5,1},{9,5},{13,9},{1,13},{6,2},{10,6},{... | collective-permute-start | bytes 786440 | tf_op jit(solution)/shard_map/ppermute | solution.py:503
  13.7 10.5 %collective-permute-start.6 = (bf16[1,128,256]{2,1,0:T(8,128)(2,1)S(1)}, bf16[1,128,256]{2,1,0:T(8,128)(2,1)S(1)}, u32[]{:S(2)}, u32[]{:S(2)}) collective-permute-start(bf16[1,128,256]{2,1,0:T(8,128)(2,1)S(1)} %get-tuple-element.34), channel_id=1, source_target_pairs={{0,1},{1,0},{2,3},{3,2},{4,5},{5,4},{6,7},{7,6},{8,9},{9,8},{10,11... | collective-permute-start | bytes 196616 | tf_op jit(solution)/shard_map/ppermute | solution.py:485
  13.8 16.1 %collective-permute-start.11 = (bf16[2,8,16,512]{3,2,1,0:T(8,128)(2,1)S(1)}, bf16[2,8,16,512]{3,2,1,0:T(8,128)(2,1)S(1)}, u32[]{:S(2)}, u32[]{:S(2)}) collective-permute-start(bf16[2,8,16,512]{3,2,1,0:T(8,128)(2,1)S(1)} %collective-permute-done.3.part), channel_id=1, source_target_pairs={{4,0},{8,4},{5,1},{9,5},{6,2},{10,6},{7,3},{11,7},{20,16},{24,20},... | collective-permute-start | bytes 786440 | tf_op jit(solution)/shard_map/ppermute | solution.py:521
  18.7 11.3 %collective-permute-start.12 = (bf16[2,8,16,512]{3,2,1,0:T(8,128)(2,1)S(1)}, bf16[2,8,16,512]{3,2,1,0:T(8,128)(2,1)S(1)}, u32[]{:S(2)}, u32[]{:S(2)}) collective-permute-start(bf16[2,8,16,512]{3,2,1,0:T(8,128)(2,1)S(1)} %collective-permute-done.2.part), channel_id=1, source_target_pairs={{4,0},{8,4},{5,1},{9,5},{6,2},{10,6},{7,3},{11,7},{20,16},{24,20},... | collective-permute-start | bytes 786440 | tf_op jit(solution)/shard_map/ppermute | solution.py:521
  20.0 4.7 %collective-permute-start.7 = (bf16[1,128,256]{2,1,0:T(8,128)(2,1)S(1)}, bf16[1,128,256]{2,1,0:T(8,128)(2,1)S(1)}, u32[]{:S(2)}, u32[]{:S(2)}) collective-permute-start(bf16[1,128,256]{2,1,0:T(8,128)(2,1)S(1)} %get-tuple-element.35), channel_id=1, source_target_pairs={{0,1},{1,0},{2,3},{3,2},{4,5},{5,4},{6,7},{7,6},{8,9},{9,8},{10,11... | collective-permute-start | bytes 196616 | tf_op jit(solution)/shard_map/ppermute | solution.py:485
  24.1 1.3 %collective-permute-start.4 = (bf16[1,128,256]{2,1,0:T(8,128)(2,1)S(1)}, bf16[1,128,256]{2,1,0:T(8,128)(2,1)S(1)}, u32[]{:S(2)}, u32[]{:S(2)}) collective-permute-start(bf16[1,128,256]{2,1,0:T(8,128)(2,1)S(1)} %get-tuple-element.32), channel_id=1, source_target_pairs={{0,1},{1,0},{2,3},{3,2},{4,5},{5,4},{6,7},{7,6},{8,9},{9,8},{10,11... | collective-permute-start | bytes 196616 | tf_op jit(solution)/shard_map/ppermute | solution.py:485
  24.2 1.4 %collective-permute-start.5 = (bf16[1,128,256]{2,1,0:T(8,128)(2,1)S(1)}, bf16[1,128,256]{2,1,0:T(8,128)(2,1)S(1)}, u32[]{:S(2)}, u32[]{:S(2)}) collective-permute-start(bf16[1,128,256]{2,1,0:T(8,128)(2,1)S(1)} %get-tuple-element.33), channel_id=1, source_target_pairs={{0,1},{1,0},{2,3},{3,2},{4,5},{5,4},{6,7},{7,6},{8,9},{9,8},{10,11... | collective-permute-start | bytes 196616 | tf_op jit(solution)/shard_map/ppermute | solution.py:485
  24.7 2.5 %collective-permute-start.9 = (bf16[1,128,256]{2,1,0:T(8,128)(2,1)S(1)}, bf16[1,128,256]{2,1,0:T(8,128)(2,1)S(1)}, u32[]{:S(2)}, u32[]{:S(2)}) collective-permute-start(bf16[1,128,256]{2,1,0:T(8,128)(2,1)S(1)} %get-tuple-element.36), channel_id=1, source_target_pairs={{0,1},{1,0},{2,3},{3,2},{4,5},{5,4},{6,7},{7,6},{8,9},{9,8},{10,11... | collective-permute-start | bytes 196616 | tf_op jit(solution)/shard_map/ppermute | solution.py:485
  25.5 1.8 %collective-permute-start.10 = (bf16[1,128,256]{2,1,0:T(8,128)(2,1)S(1)}, bf16[1,128,256]{2,1,0:T(8,128)(2,1)S(1)}, u32[]{:S(2)}, u32[]{:S(2)}) collective-permute-start(bf16[1,128,256]{2,1,0:T(8,128)(2,1)S(1)} %get-tuple-element.37), channel_id=1, source_target_pairs={{0,1},{1,0},{2,3},{3,2},{4,5},{5,4},{6,7},{7,6},{8,9},{9,8},{10,11... | collective-permute-start | bytes 196616 | tf_op jit(solution)/shard_map/ppermute | solution.py:485
  25.7 15.7 %collective-permute-start.8 = (bf16[2,256,256]{2,1,0:T(8,128)(2,1)S(1)}, bf16[2,256,256]{2,1,0:T(8,128)(2,1)S(1)}, u32[]{:S(2)}, u32[]{:S(2)}) collective-permute-start(bf16[2,256,256]{2,1,0:T(8,128)(2,1)S(1)} %shard_map.49.refs_2_), channel_id=1, source_target_pairs={{0,2},{2,0},{1,3},{3,1},{4,6},{6,4},{5,7},{7,5},{8,10},{10,8},{9,1... | collective-permute-start | bytes 786440 | tf_op jit(solution)/shard_map/ppermute | solution.py:490
  27.3 10.0 %collective-permute-start.17 = (bf16[1,256,256]{2,1,0:T(8,128)(2,1)S(1)}, bf16[1,256,256]{2,1,0:T(8,128)(2,1)S(1)}, u32[]{:S(2)}, u32[]{:S(2)}) collective-permute-start(bf16[1,256,256]{2,1,0:T(8,128)(2,1)S(1)} %shard_map.53), channel_id=1, source_target_pairs={{12,0},{14,2},{13,1},{15,3},{28,16},{30,18},{29,17},{31,19}} | collective-permute-start | bytes 393224 | tf_op jit(solution)/shard_map/ppermute | solution.py:496
  28.6 11.1 %collective-permute-start.18 = (bf16[1,256,256]{2,1,0:T(8,128)(2,1)S(1)}, bf16[1,256,256]{2,1,0:T(8,128)(2,1)S(1)}, u32[]{:S(2)}, u32[]{:S(2)}) collective-permute-start(bf16[1,256,256]{2,1,0:T(8,128)(2,1)S(1)} %shard_map.54), channel_id=1, source_target_pairs={{12,2},{14,0},{13,3},{15,1},{28,18},{30,16},{29,19},{31,17}} | collective-permute-start | bytes 393224 | tf_op jit(solution)/shard_map/ppermute | solution.py:496
  30.5 9.2 %collective-permute-start.15 = (bf16[1,128,256]{2,1,0:T(8,128)(2,1)S(1)}, bf16[1,128,256]{2,1,0:T(8,128)(2,1)S(1)}, u32[]{:S(2)}, u32[]{:S(2)}) collective-permute-start(bf16[1,128,256]{2,1,0:T(8,128)(2,1)S(1)} %get-tuple-element.43), channel_id=1, source_target_pairs={{0,1},{1,0},{2,3},{3,2},{4,5},{5,4},{6,7},{7,6},{8,9},{9,8},{10,11... | collective-permute-start | bytes 196616 | tf_op jit(solution)/shard_map/ppermute | solution.py:485
  30.6 9.1 %collective-permute-start.16 = (bf16[1,128,256]{2,1,0:T(8,128)(2,1)S(1)}, bf16[1,128,256]{2,1,0:T(8,128)(2,1)S(1)}, u32[]{:S(2)}, u32[]{:S(2)}) collective-permute-start(bf16[1,128,256]{2,1,0:T(8,128)(2,1)S(1)} %get-tuple-element.44), channel_id=1, source_target_pairs={{0,1},{1,0},{2,3},{3,2},{4,5},{5,4},{6,7},{7,6},{8,9},{9,8},{10,11... | collective-permute-start | bytes 196616 | tf_op jit(solution)/shard_map/ppermute | solution.py:485
  39.8 5.0 %collective-permute-start.19 = (bf16[1,256,256]{2,1,0:T(8,128)(2,1)S(1)}, bf16[1,256,256]{2,1,0:T(8,128)(2,1)S(1)}, u32[]{:S(2)}, u32[]{:S(2)}) collective-permute-start(bf16[1,256,256]{2,1,0:T(8,128)(2,1)S(1)} %shard_map.55), channel_id=1, source_target_pairs={{0,2},{2,0},{1,3},{3,1},{4,6},{6,4},{5,7},{7,5},{8,10},{10,8},{9,1... | collective-permute-start | bytes 393224 | tf_op jit(solution)/shard_map/ppermute | solution.py:490
  40.8 1.7 %collective-permute-start = (bf16[1,128,256]{2,1,0:T(8,128)(2,1)S(1)}, bf16[1,128,256]{2,1,0:T(8,128)(2,1)S(1)}, u32[]{:S(2)}, u32[]{:S(2)}) collective-permute-start(bf16[1,128,256]{2,1,0:T(8,128)(2,1)S(1)} %get-tuple-element.26), channel_id=1, source_target_pairs={{0,1},{1,0},{2,3},{3,2},{4,5},{5,4},{6,7},{7,6},{8,9},{9,8},{10,11... | collective-permute-start | bytes 196616 | tf_op jit(solution)/shard_map/ppermute | solution.py:485
  40.8 1.7 %collective-permute-start.1 = (bf16[1,128,256]{2,1,0:T(8,128)(2,1)S(1)}, bf16[1,128,256]{2,1,0:T(8,128)(2,1)S(1)}, u32[]{:S(2)}, u32[]{:S(2)}) collective-permute-start(bf16[1,128,256]{2,1,0:T(8,128)(2,1)S(1)} %get-tuple-element.27), channel_id=1, source_target_pairs={{0,1},{1,0},{2,3},{3,2},{4,5},{5,4},{6,7},{7,6},{8,9},{9,8},{10,11... | collective-permute-start | bytes 196616 | tf_op jit(solution)/shard_map/ppermute | solution.py:485
  41.3 1.8 %collective-permute-start.13 = (bf16[1,128,256]{2,1,0:T(8,128)(2,1)S(1)}, bf16[1,128,256]{2,1,0:T(8,128)(2,1)S(1)}, u32[]{:S(2)}, u32[]{:S(2)}) collective-permute-start(bf16[1,128,256]{2,1,0:T(8,128)(2,1)S(1)} %get-tuple-element.41), channel_id=1, source_target_pairs={{0,1},{1,0},{2,3},{3,2},{4,5},{5,4},{6,7},{7,6},{8,9},{9,8},{10,11... | collective-permute-start | bytes 196616 | tf_op jit(solution)/shard_map/ppermute | solution.py:485
  41.3 1.8 %collective-permute-start.14 = (bf16[1,128,256]{2,1,0:T(8,128)(2,1)S(1)}, bf16[1,128,256]{2,1,0:T(8,128)(2,1)S(1)}, u32[]{:S(2)}, u32[]{:S(2)}) collective-permute-start(bf16[1,128,256]{2,1,0:T(8,128)(2,1)S(1)} %get-tuple-element.42), channel_id=1, source_target_pairs={{0,1},{1,0},{2,3},{3,2},{4,5},{5,4},{6,7},{7,6},{8,9},{9,8},{10,11... | collective-permute-start | bytes 196616 | tf_op jit(solution)/shard_map/ppermute | solution.py:485

commit v4 on v3

--- a/solution.py
+++ b/solution.py
@@ -20,6 +20,7 @@
 VMEM_LIMIT = 40 << 20
 FAR = 1 << 20
 HALVES = 2
+SETTLED = 144
 SLOT_AT = 4
 
 
@@ -71,9 +72,9 @@
 
 
 def reach_of(scalars, step):
-    slots = (scalars.shape[0] - SLOT_AT) // 2
+    slots = (scalars.shape[1] - SLOT_AT) // 2
     picked = [
-        jnp.where(scalars[SLOT_AT + k] == step, scalars[SLOT_AT + slots + k], 0) for k in range(slots)
+        jnp.where(scalars[0, SLOT_AT + k] == step, scalars[0, SLOT_AT + slots + k], 0) for k in range(slots)
     ]
     return functools.reduce(lambda x, y: x + y, picked)
 
@@ -133,7 +134,7 @@
 
 def lag_sums(scalars, cross, table, keep, sends):
     owners, size = keep.shape[0], keep.shape[1] // HALVES
-    core, day = scalars[0], scalars[1]
+    core, day = scalars[0, 0], scalars[0, 1]
     for shift in range(owners):
         owner = lax.rem(day + shift, owners)
         for half in range(HALVES):
@@ -183,7 +184,7 @@
     if can_swap:
         rows, wide_cols = swap_refs
 
-        @pl.when(scalars[2] != 0)
+        @pl.when(scalars[0, 2] != 0)
         def _():
             for at in range(0, own_rows.shape[3], LANES):
                 lanes = pl.ds(at, LANES)
@@ -205,7 +206,7 @@
                 keep[k] = kept
                 send[k] = sent
 
-            lag_block(scalars[0], cross, k * 2 * size, table, size, store)
+            lag_block(scalars[0, 0], cross, k * 2 * size, table, size, store)
 
     half_cross(can_swap, step, 0, scalars, own_rows, part, cols, cross, swap_refs, finish)
 
@@ -217,7 +218,7 @@
     sends = refs[: keep.shape[0] * HALVES]
     cols, cross, *swap_refs = refs[keep.shape[0] * HALVES :]
     owners, size = keep.shape[0], keep.shape[1] // HALVES
-    core, day = scalars[0], scalars[1]
+    core, day = scalars[0, 0], scalars[0, 1]
 
     def finish(swapped):
         for shift in range(owners):
@@ -239,7 +240,6 @@
 
 
 VMEM = pl.BlockSpec(memory_space=pltpu.VMEM)
-SMEM = pl.BlockSpec(memory_space=pltpu.SMEM)
 ANY = pl.BlockSpec(memory_space=pl.ANY)
 FREE = pl.CostEstimate(flops=0, bytes_accessed=0, transcendentals=0)
 PARAMS = pltpu.CompilerParams(vmem_limit_bytes=VMEM_LIMIT)
@@ -259,7 +259,7 @@
     keep, *sends, rows = pl.pallas_call(
         functools.partial(own_kernel, len(parts)),
         out_shape=sums_shapes(owners, width) + [jax.ShapeDtypeStruct(factors, jnp.float32)],
-        in_specs=[SMEM] + [VMEM] * (1 + len(parts)),
+        in_specs=[VMEM] + [VMEM] * (1 + len(parts)),
         out_specs=[VMEM] * (owners * HALVES + 2),
         scratch_shapes=[
             pltpu.VMEM(factors, jnp.float32),
@@ -276,7 +276,7 @@
     keep, *sends = pl.pallas_call(
         functools.partial(partner_kernel, len(parts), len(after), step),
         out_shape=sums_shapes(owners, width),
-        in_specs=[SMEM] + [VMEM] * (2 + len(parts)) + [ANY] * len(after),
+        in_specs=[VMEM] + [VMEM] * (2 + len(parts)) + [ANY] * len(after),
         out_specs=[VMEM] * (owners * HALVES + 1),
         scratch_shapes=[
             pltpu.VMEM((3, windows, width, bins), jnp.float32),
@@ -307,7 +307,7 @@
             jax.ShapeDtypeStruct((owners, size, LAGS), jnp.float32),
             jax.ShapeDtypeStruct((owners, size, LAGS), jnp.bfloat16),
         ],
-        in_specs=[SMEM, VMEM, VMEM, VMEM],
+        in_specs=[VMEM, VMEM, VMEM, VMEM],
         out_specs=[VMEM, VMEM],
         scratch_shapes=half_scratch(own_rows, can_swap),
         compiler_params=PARAMS,
@@ -319,7 +319,7 @@
     keep, *sends = pl.pallas_call(
         functools.partial(second_half_kernel, can_swap, step, len(after)),
         out_shape=sums_shapes(owners, own_rows.shape[2]),
-        in_specs=[SMEM] + [VMEM] * 5 + [ANY] * len(after),
+        in_specs=[VMEM] + [VMEM] * 5 + [ANY] * len(after),
         out_specs=[VMEM] * (owners * HALVES + 1),
         scratch_shapes=half_scratch(own_rows, can_swap),
         compiler_params=PARAMS,
@@ -352,7 +352,7 @@
 
 def write_tile(scalars, step, terms, tile, norm_scale):
     row_count, width, _ = tile.shape
-    slots = (scalars.shape[0] - SLOT_AT) // 2
+    slots = (scalars.shape[1] - SLOT_AT) // 2
     reach = reach_of(scalars, step)
     half_width = width // HALVES
     size = row_count * half_width
@@ -367,7 +367,7 @@
             part = part.astype(jnp.float32)
             value = part if value is None else value + part
         value = value.reshape(row_count, half_width, LAGS)
-        row = lax.broadcasted_iota(jnp.int32, value.shape, 0) + scalars[3] * row_count
+        row = lax.broadcasted_iota(jnp.int32, value.shape, 0) + scalars[0, 3] * row_count
         col = lax.broadcasted_iota(jnp.int32, value.shape, 1) + half * half_width
         distance = jnp.abs(step * width + col - row)
         kept = (distance > 0) & (distance < reach)
@@ -403,14 +403,14 @@
     return pl.pallas_call(
         functools.partial(tile_kernel, step, counts, norm_scale),
         out_shape=jax.ShapeDtypeStruct((row_count, width, LAGS), jnp.float32),
-        in_specs=[SMEM] + [VMEM] * len(operands),
+        in_specs=[VMEM] + [VMEM] * len(operands),
         out_specs=VMEM,
         compiler_params=PARAMS,
         cost_estimate=FREE,
     )(scalars, *operands)
 
 
-def output_kernel(ready_steps, late, norm_scale, scalars, *refs):
+def output_kernel(ready_steps, late, after_count, norm_scale, scalars, *refs):
     out, tiles, zeros, sems = refs[-4:]
     slots = out.shape[0]
     ready, rest = refs[: len(ready_steps)], list(refs[len(ready_steps) : -4])
@@ -420,7 +420,7 @@
 
     def start(step, source):
         for slot in range(slots):
-            pl.when(scalars[SLOT_AT + slot] == step)(copies(slot, source).start)
+            pl.when(scalars[0, SLOT_AT + slot] == step)(copies(slot, source).start)
 
     for step, tile in zip(ready_steps, ready):
         start(step, tile)
@@ -438,7 +438,7 @@
         copies(slot, zeros).wait()
 
 
-def write_output(scalars, ready, late, slots, norm_scale):
+def write_output(scalars, ready, late, slots, norm_scale, after):
     tile_shape = ready[0][1].shape
     operands, listed = [tile for _, tile in ready], []
     for step, terms in late:
@@ -446,9 +446,9 @@
         operands += more
         listed.append((step, counts))
     return pl.pallas_call(
-        functools.partial(output_kernel, [step for step, _ in ready], listed, norm_scale),
+        functools.partial(output_kernel, [step for step, _ in ready], listed, len(after), norm_scale),
         out_shape=jax.ShapeDtypeStruct((slots,) + tile_shape, jnp.float32),
-        in_specs=[SMEM] + [VMEM] * len(operands),
+        in_specs=[VMEM] + [VMEM] * len(operands) + [ANY] * len(after),
         out_specs=ANY,
         scratch_shapes=[
             pltpu.VMEM((len(late),) + tile_shape, jnp.float32),
@@ -457,7 +457,7 @@
         ],
         compiler_params=PARAMS,
         cost_estimate=FREE,
-    )(scalars, *operands)
+    )(scalars, *operands, *after)
 
 
 def on_device(spectra, tile_offset, pair_reach):
@@ -479,7 +479,7 @@
     ]
     is_last = (block == blocks - 1).astype(jnp.int32) if wraps else jnp.int32(0)
     scalars = jnp.stack([core, day, is_last, day * cores + core]).astype(jnp.int32)
-    scalars = jnp.concatenate([scalars, tile_offset[0], pair_reach[0]])
+    scalars = jnp.concatenate([scalars, tile_offset[0], pair_reach[0]])[None]
 
     def over_cores(sends):
         got = [lax.ppermute(send, "sub", [(k, (k + 1) % cores) for k in range(cores)]) for send in sends]
@@ -497,7 +497,7 @@
 
     keep, sends, own_rows = own_tile(scalars, halves, table, days)
     own_sums = (keep, over_cores(sends))
-    ready, late, back = [], [], []
+    ready, late, back, settled = [], [], [], []
 
     pairs = [(a + 1, a) for a in range(blocks - 1)] + [(0, blocks - 1)] * wraps
     moving = [lax.ppermute(part, "chan", pairs) for part in halves]
@@ -523,12 +523,15 @@
         ]
         keep, sends2 = partner_tile(scalars, own_rows, ahead, table, days, step, pieces)
         sums = (keep, over_cores(sends2))
-        last = [add_cores([sums], shift, back) for shift in range(1, days)]
+        last = [add_cores([sums], shift) for shift in range(1, days)]
         terms = [(keep, 0), sums[1][0]] + [(piece, 0) for piece in over_days(last)]
         late.append((step, terms))
     if wraps:
-        late.append((steps, [(piece, 0) for piece in back]))
-    return write_output(scalars, ready, late, slots, norm_scale)[None]
+        terms = [(piece, 0) for piece in back]
+        ready.append((steps, finished_tile(scalars, steps, terms, row_count, width, norm_scale)))
+        pairs = [(c, (c + 1) % cores) for c in range(cores)]
+        settled = [lax.ppermute(piece[:, :SETTLED], "sub", pairs) for piece in back]
+    return write_output(scalars, ready, late, slots, norm_scale, settled)[None]
 
 
 def solution(mesh):

time: 46.2 us -> 42.9 us (0.929); the launches traced: 46.2 us -> 42.4 us
  Pallas kernels: 17 us -> 14.2 us
  waiting for transfers between devices: 11 us -> 9.56 us
    ppermute x2, waiting for transfers between devices: 8.6 us -> 6.96 us  [to_first(): return lax.ppermute(piece, ('chan', 'day'), pairs)]
    ppermute x12, waiting for transfers between devices: 0.68 us -> 1.79 us  [over_cores(): lax.ppermute(send, 'sub', [(k, (k + 1) % cores) for k in range(cores)])]
    ppermute x2, waiting for transfers between devices: 1.67 us -> 0.7 us  [over_days(): lax.ppermute(piece, 'day', [(k, (k + shift) % days) for k in range(days)])]
    pallas_call x2 -> x3, Pallas kernels: 1.24 us -> 0.47 us  [finished_tile(): pl.pallas_call(functools.partial(tile_kernel, step, counts, norm_scale),...]
    ppermute x0 -> x2, starting transfers between devices: none -> 0.57 us  [on_device(): settled = [lax.ppermute(piece[:, :SETTLED], 'sub', pairs) for piece in back]]
  transfers between devices with their start and end apart: 20 -> 22, of which waited for: 5 -> 8; matrix products, arithmetic and copies ran while one was open for 0% -> 0% of each run, Pallas kernels for 34% -> 31%
where the time goes in v4:
time: 42.9 us; the launch traced here: 42.4 us
  starting transfers between devices  16.8 us (39%)
  Pallas kernels  14.2 us (33%)
  waiting for transfers between devices  9.56 us (22%)
  local copies, waits for them, and re-layouts  1.64 us (4%)
    ppermute x2, waiting for transfers between devices, to_first(): return lax.ppermute(piece, ('chan', 'day'), pairs)  6.96 us
    pallas_call x1, Pallas kernels, own_tile(): pl.pallas_call(functools.partial(own_kernel, len(parts)), out_shape=sums_...  5.97 us
    ppermute x2, starting transfers between devices, on_device(): moving = [lax.ppermute(part, 'chan', pairs) for part in halves]  5.61 us
    pallas_call x1, Pallas kernels, first_half_tile(): pl.pallas_call(functools.partial(first_half_kernel, can_swap, step), out_...  3.25 us
    pallas_call x1, Pallas kernels, second_half_tile(): pl.pallas_call(functools.partial(second_half_kernel, can_swap, step, len(...  3.24 us
    ppermute x12, starting transfers between devices, over_cores(): lax.ppermute(send, 'sub', [(k, (k + 1) % cores) for k in range(cores)])  3 us
    ppermute x2, starting transfers between devices, to_first(): return lax.ppermute(piece, ('chan', 'day'), pairs)  2.58 us
    ppermute x2, starting transfers between devices, on_device(): lax.ppermute(lax.optimization_barrier((part, wait))[0], 'chan', pairs)  2.57 us
  transfers between devices with their start and end apart: 22, of which 8 were waited for; matrix products, arithmetic and copies ran while one was open for 0% of the time, Pallas kernels for 31%

profile of v4, /device:TPU:0, one launch (start us, length us, event | category | flops | bytes accessed | tf_op | source)
XLA Modules:
  0.0 42.4 jit_solution(2035188699686814688)
XLA Ops:
  0.0 1.5 %fusion = (bf16[1,8,16,2,512]{4,3,2,1,0:T(2,128)(2,1)S(1)}, bf16[1,8,16,2,512]{4,3,2,1,0:T(2,128)(2,1)S(1)}) fusion(bf16[1,8,32,2,512]{4,3,2,1,0:T(2,128)(2,1)} %param.4), kind=kLoop, calls=%fused_computation.2 | loop fusion | bytes 1048576 | tf_op jit(solution)/shard_map/slice | solution.py:477
  1.5 5.1 %collective-permute-start.3 = (bf16[2,8,16,512]{3,2,1,0:T(8,128)(2,1)S(1)}, bf16[2,8,16,512]{3,2,1,0:T(8,128)(2,1)S(1)}, u32[]{:S(2)}, u32[]{:S(2)}) collective-permute-start(bf16[2,8,16,512]{3,2,1,0:T(8,128)(2,1)S(1)} %bitcast.20), channel_id=1, source_target_pairs={{4,0},{8,4},{12,8},{0,12},{5,1},{9,5},{13,9},{1,13},{6,2},{10,6},{... | collective-permute-start | bytes 786440 | tf_op jit(solution)/shard_map/ppermute | solution.py:503
  6.7 0.5 %collective-permute-start.2 = (bf16[2,8,16,512]{3,2,1,0:T(8,128)(2,1)S(1)}, bf16[2,8,16,512]{3,2,1,0:T(8,128)(2,1)S(1)}, u32[]{:S(2)}, u32[]{:S(2)}) collective-permute-start(bf16[2,8,16,512]{3,2,1,0:T(8,128)(2,1)S(1)} %bitcast.18), channel_id=1, source_target_pairs={{4,0},{8,4},{12,8},{0,12},{5,1},{9,5},{13,9},{1,13},{6,2},{10,6},{... | collective-permute-start | bytes 786440 | tf_op jit(solution)/shard_map/ppermute | solution.py:503
  7.3 6.0 %shard_map.46 = (f32[2,256,256]{2,1,0:T(8,128)S(1)}, bf16[1,128,256]{2,1,0:T(8,128)(2,1)S(1)}, bf16[1,128,256]{2,1,0:T(8,128)(2,1)S(1)}, bf16[1,128,256]{2,1,0:T...) custom-call(s32[1,10]{1,0:T(1,128)S(1)} %bitcast.22, bf16[1024,256]{1,0:T(8,128)(2,1)S(1)} %copy-done, ...), custom_call_target="tpu_custom_call" | custom-call | tf_op jit(solution)/shard_map/pallas_call | solution.py:259
  13.3 1.3 %collective-permute-start.13 = (bf16[2,8,16,512]{3,2,1,0:T(8,128)(2,1)S(1)}, bf16[2,8,16,512]{3,2,1,0:T(8,128)(2,1)S(1)}, u32[]{:S(2)}, u32[]{:S(2)}) collective-permute-start(bf16[2,8,16,512]{3,2,1,0:T(8,128)(2,1)S(1)} %collective-permute-done.3.part), channel_id=1, source_target_pairs={{4,0},{8,4},{5,1},{9,5},{6,2},{10,6},{7,3},{11,7},{20,16},{24,20},... | collective-permute-start | bytes 786440 | tf_op jit(solution)/shard_map/ppermute | solution.py:521
  14.6 3.3 %shard_map.47 = (f32[2,128,256]{2,1,0:T(8,128)S(1)}, bf16[2,128,256]{2,1,0:T(8,128)(2,1)S(1)}) custom-call(s32[1,10]{1,0:T(1,128)S(1)} %bitcast.23, f32[3,8,32,512]{3,2,1,0:T(8,128)S(1)} %get-tuple-element.28.own_rows, bf16[1024,256]{1,0:T(8,128)(2,1)S(1)} %copy-done, bf16[2,8,16,512]{3,2,1,0:T(8,128)(2,1)S(1)} %collective-permute-done.3.part), custom_call_target="tpu_custom_call" | custom-call | tf_op jit(solution)/shard_map/pallas_call | solution.py:304
  17.9 1.3 %collective-permute-start.14 = (bf16[2,8,16,512]{3,2,1,0:T(8,128)(2,1)S(1)}, bf16[2,8,16,512]{3,2,1,0:T(8,128)(2,1)S(1)}, u32[]{:S(2)}, u32[]{:S(2)}) collective-permute-start(bf16[2,8,16,512]{3,2,1,0:T(8,128)(2,1)S(1)} %collective-permute-done.2.part), channel_id=1, source_target_pairs={{4,0},{8,4},{5,1},{9,5},{6,2},{10,6},{7,3},{11,7},{20,16},{24,20},... | collective-permute-start | bytes 786440 | tf_op jit(solution)/shard_map/ppermute | solution.py:521
  19.3 0.5 %collective-permute-start.7 = (bf16[1,128,256]{2,1,0:T(8,128)(2,1)S(1)}, bf16[1,128,256]{2,1,0:T(8,128)(2,1)S(1)}, u32[]{:S(2)}, u32[]{:S(2)}) collective-permute-start(bf16[1,128,256]{2,1,0:T(8,128)(2,1)S(1)} %get-tuple-element.35), channel_id=1, source_target_pairs={{0,1},{1,0},{2,3},{3,2},{4,5},{5,4},{6,7},{7,6},{8,9},{9,8},{10,11... | collective-permute-start | bytes 196616 | tf_op jit(solution)/shard_map/ppermute | solution.py:485
  19.8 3.2 %shard_map.48 = (f32[2,256,256]{2,1,0:T(8,128)S(1)}, bf16[1,128,256]{2,1,0:T(8,128)(2,1)S(1)}, bf16[1,128,256]{2,1,0:T(8,128)(2,1)S(1)}, bf16[1,128,256]{2,1,0:T(8,128)(2,1)S(1)}, bf16[1,128,256]{2,1,0:T(8,128)(2,1)S(1)}) custom-call(s32[1,10]{1,0:T(1,128)S(1)} %bitcast.24, f32[3,8,32,512]{3,2,1,0:T(8,128)S(1)} %get-tuple-element.28.own_rows, ...), custom_call_target="tpu_custom_call" | custom-call | tf_op jit(solution)/shard_map/pallas_call | solution.py:319
  23.0 0.2 collective-permute-start.4
  23.2 0.4 collective-permute-start.5
  23.7 0.6 %collective-permute-done.4.refs_1_ = bf16[1,128,256]{2,1,0:T(8,128)(2,1)S(1)} collective-permute-done((bf16[1,128,256]{2,1,0:T(8,128)(2,1)S(1)}, bf16[1,128,256]{2,1,0:T(8,128)(2,1)S(1)}, u32[]{:S(2)}, u32[]{:S(2)}) %collective-permute-start.4) | collective-permute-done | bytes 65568 | tf_op jit(solution)/shard_map/ppermute | solution.py:485
  24.4 0.2 collective-permute-start.10
  24.6 1.6 %collective-permute-start.8 = (bf16[2,256,256]{2,1,0:T(8,128)(2,1)S(1)}, bf16[2,256,256]{2,1,0:T(8,128)(2,1)S(1)}, u32[]{:S(2)}, u32[]{:S(2)}) collective-permute-start(bf16[2,256,256]{2,1,0:T(8,128)(2,1)S(1)} %shard_map.49.refs_2_), channel_id=1, source_target_pairs={{0,2},{2,0},{1,3},{3,1},{4,6},{6,4},{5,7},{7,5},{8,10},{10,8},{9,1... | collective-permute-start | bytes 786440 | tf_op jit(solution)/shard_map/ppermute | solution.py:490
  26.2 1.3 %collective-permute-start.11 = (bf16[1,256,256]{2,1,0:T(8,128)(2,1)S(1)}, bf16[1,256,256]{2,1,0:T(8,128)(2,1)S(1)}, u32[]{:S(2)}, u32[]{:S(2)}) collective-permute-start(bf16[1,256,256]{2,1,0:T(8,128)(2,1)S(1)} %shard_map.52), channel_id=1, source_target_pairs={{12,0},{14,2},{13,1},{15,3},{28,16},{30,18},{29,17},{31,19}} | collective-permute-start | bytes 393224 | tf_op jit(solution)/shard_map/ppermute | solution.py:496
  27.5 1.3 %collective-permute-start.12 = (bf16[1,256,256]{2,1,0:T(8,128)(2,1)S(1)}, bf16[1,256,256]{2,1,0:T(8,128)(2,1)S(1)}, u32[]{:S(2)}, u32[]{:S(2)}) collective-permute-start(bf16[1,256,256]{2,1,0:T(8,128)(2,1)S(1)} %shard_map.53), channel_id=1, source_target_pairs={{12,2},{14,0},{13,3},{15,1},{28,18},{30,16},{29,19},{31,17}} | collective-permute-start | bytes 393224 | tf_op jit(solution)/shard_map/ppermute | solution.py:496
  29.1 0.4 %collective-permute-start.18 = (bf16[1,128,256]{2,1,0:T(8,128)(2,1)S(1)}, bf16[1,128,256]{2,1,0:T(8,128)(2,1)S(1)}, u32[]{:S(2)}, u32[]{:S(2)}) collective-permute-start(bf16[1,128,256]{2,1,0:T(8,128)(2,1)S(1)} %get-tuple-element.44), channel_id=1, source_target_pairs={{0,1},{1,0},{2,3},{3,2},{4,5},{5,4},{6,7},{7,6},{8,9},{9,8},{10,11... | collective-permute-start | bytes 196616 | tf_op jit(solution)/shard_map/ppermute | solution.py:485
  29.5 0.7 %collective-permute-done.17.refs_1_ = bf16[1,128,256]{2,1,0:T(8,128)(2,1)S(1)} collective-permute-done((bf16[1,128,256]{2,1,0:T(8,128)(2,1)S(1)}, bf16[1,128,256]{2,1,0:T(8,128)(2,1)S(1)}, u32[]{:S(2)}, u32[]{:S(2)}) %collective-permute-start.17) | collective-permute-done | bytes 65568 | tf_op jit(solution)/shard_map/ppermute | solution.py:485
  30.3 0.2 collective-permute-start.1
  30.4 0.4 collective-permute-start
  30.8 5.4 %collective-permute-done.11.refs_0_ = bf16[1,256,256]{2,1,0:T(8,128)(2,1)S(1)} collective-permute-done((bf16[1,256,256]{2,1,0:T(8,128)(2,1)S(1)}, bf16[1,256,256]{2,1,0:T(8,128)(2,1)S(1)}, u32[]{:S(2)}, u32[]{:S(2)}) %collective-permute-start.11) | collective-permute-done | bytes 131104 | tf_op jit(solution)/shard_map/ppermute | solution.py:496
  36.2 1.0 %collective-permute-start.19 = (bf16[1,256,256]{2,1,0:T(8,128)(2,1)S(1)}, bf16[1,256,256]{2,1,0:T(8,128)(2,1)S(1)}, u32[]{:S(2)}, u32[]{:S(2)}) collective-permute-start(bf16[1,256,256]{2,1,0:T(8,128)(2,1)S(1)} %shard_map.56), channel_id=1, source_target_pairs={{0,2},{2,0},{1,3},{3,1},{4,6},{6,4},{5,7},{7,5},{8,10},{10,8},{9,1... | collective-permute-start | bytes 393224 | tf_op jit(solution)/shard_map/ppermute | solution.py:490
  37.2 1.6 %collective-permute-done.12.refs_1_ = bf16[1,256,256]{2,1,0:T(8,128)(2,1)S(1)} collective-permute-done((bf16[1,256,256]{2,1,0:T(8,128)(2,1)S(1)}, bf16[1,256,256]{2,1,0:T(8,128)(2,1)S(1)}, u32[]{:S(2)}, u32[]{:S(2)}) %collective-permute-start.12) | collective-permute-done | bytes 131104 | tf_op jit(solution)/shard_map/ppermute | solution.py:496
  38.8 0.6 %collective-permute-start.21 = (bf16[1,144,256]{2,1,0:T(8,128)(2,1)S(1)}, bf16[1,144,256]{2,1,0:T(8,128)(2,1)S(1)}, u32[]{:S(2)}, u32[]{:S(2)}) collective-permute-start(bf16[1,144,256]{2,1,0:T(8,128)(2,1)S(1)} %slice.17), channel_id=1, source_target_pairs={{0,1},{1,0},{2,3},{3,2},{4,5},{5,4},{6,7},{7,6},{8,9},{9,8},{10,11... | collective-permute-start | bytes 221192 | tf_op jit(solution)/shard_map/ppermute | solution.py:533
  39.4 0.4 %collective-permute-start.16 = (bf16[1,128,256]{2,1,0:T(8,128)(2,1)S(1)}, bf16[1,128,256]{2,1,0:T(8,128)(2,1)S(1)}, u32[]{:S(2)}, u32[]{:S(2)}) collective-permute-start(bf16[1,128,256]{2,1,0:T(8,128)(2,1)S(1)} %get-tuple-element.42), channel_id=1, source_target_pairs={{0,1},{1,0},{2,3},{3,2},{4,5},{5,4},{6,7},{7,6},{8,9},{9,8},{10,11... | collective-permute-start | bytes 196616 | tf_op jit(solution)/shard_map/ppermute | solution.py:485
  39.8 0.2 shard_map.54.refs_2_
  40.0 0.2 shard_map.51.refs_1_
  40.2 0.2 shard_map.50.refs_0_
  40.3 0.2 collective-permute-done.15.refs_4_
  40.6 0.2 collective-permute-done.16.refs_5_
  40.7 0.7 %collective-permute-done.19.refs_6_ = bf16[1,256,256]{2,1,0:T(8,128)(2,1)S(1)} collective-permute-done((bf16[1,256,256]{2,1,0:T(8,128)(2,1)S(1)}, bf16[1,256,256]{2,1,0:T(8,128)(2,1)S(1)}, u32[]{:S(2)}, u32[]{:S(2)}) %collective-permute-start.19) | collective-permute-done | bytes 131104 | tf_op jit(solution)/shard_map/ppermute | solution.py:490
  41.4 1.0 %shard_map.57 = f32[3,8,32,256]{3,2,1,0:T(8,128)} custom-call(s32[1,10]{1,0:T(1,128)S(1)} %bitcast.29, f32[8,32,256]{2,1,0:T(8,128)S(1)} %shard_map.50.refs_0_, f32[8,32,256]{2,1,0:T(8,128)S(1)} %shard_map.51.refs_1_, f32[8,32,256]{2,1,0:T(8,128)S(1)} %shard_map.54.refs_2_, f32[2,256,256]{2,1,0:T(8,128)S(1)} %get-tuple-element.40.refs_0_.refs_3_, ...), custom_call_target="tpu_custom_call" | custom-call | tf_op jit(solution)/shard_map/pallas_call | solution.py:448
  (36 shorter events, 1.0 us)
Async XLA Ops:
  0.0 7.3 %copy-start = (bf16[1024,256]{1,0:T(8,128)(2,1)S(1)}, bf16[1024,256]{1,0:T(8,128)(2,1)}, u32[]{:S(2)}) copy-start(bf16[1024,256]{1,0:T(8,128)(2,1)} %constant.17.clone.table) | copy-start | bytes 1572868
  0.0 7.2 %copy-start.2 = (s32[1,3]{1,0:T(1,128)S(1)}, s32[1,3]{1,0:T(1,128)}, u32[]{:S(2)}) copy-start(s32[1,3]{1,0:T(1,128)} %param.6) | copy-start | bytes 40
  0.0 7.2 %copy-start.1 = (s32[1,3]{1,0:T(1,128)S(1)}, s32[1,3]{1,0:T(1,128)}, u32[]{:S(2)}) copy-start(s32[1,3]{1,0:T(1,128)} %param.5) | copy-start | bytes 40
  1.5 11.8 %collective-permute-start.3 = (bf16[2,8,16,512]{3,2,1,0:T(8,128)(2,1)S(1)}, bf16[2,8,16,512]{3,2,1,0:T(8,128)(2,1)S(1)}, u32[]{:S(2)}, u32[]{:S(2)}) collective-permute-start(bf16[2,8,16,512]{3,2,1,0:T(8,128)(2,1)S(1)} %bitcast.20), channel_id=1, source_target_pairs={{4,0},{8,4},{12,8},{0,12},{5,1},{9,5},{13,9},{1,13},{6,2},{10,6},{... | collective-permute-start | bytes 786440 | tf_op jit(solution)/shard_map/ppermute | solution.py:503
  6.7 11.2 %collective-permute-start.2 = (bf16[2,8,16,512]{3,2,1,0:T(8,128)(2,1)S(1)}, bf16[2,8,16,512]{3,2,1,0:T(8,128)(2,1)S(1)}, u32[]{:S(2)}, u32[]{:S(2)}) collective-permute-start(bf16[2,8,16,512]{3,2,1,0:T(8,128)(2,1)S(1)} %bitcast.18), channel_id=1, source_target_pairs={{4,0},{8,4},{12,8},{0,12},{5,1},{9,5},{13,9},{1,13},{6,2},{10,6},{... | collective-permute-start | bytes 786440 | tf_op jit(solution)/shard_map/ppermute | solution.py:503
  13.3 15.5 %collective-permute-start.13 = (bf16[2,8,16,512]{3,2,1,0:T(8,128)(2,1)S(1)}, bf16[2,8,16,512]{3,2,1,0:T(8,128)(2,1)S(1)}, u32[]{:S(2)}, u32[]{:S(2)}) collective-permute-start(bf16[2,8,16,512]{3,2,1,0:T(8,128)(2,1)S(1)} %collective-permute-done.3.part), channel_id=1, source_target_pairs={{4,0},{8,4},{5,1},{9,5},{6,2},{10,6},{7,3},{11,7},{20,16},{24,20},... | collective-permute-start | bytes 786440 | tf_op jit(solution)/shard_map/ppermute | solution.py:521
  17.9 10.9 %collective-permute-start.14 = (bf16[2,8,16,512]{3,2,1,0:T(8,128)(2,1)S(1)}, bf16[2,8,16,512]{3,2,1,0:T(8,128)(2,1)S(1)}, u32[]{:S(2)}, u32[]{:S(2)}) collective-permute-start(bf16[2,8,16,512]{3,2,1,0:T(8,128)(2,1)S(1)} %collective-permute-done.2.part), channel_id=1, source_target_pairs={{4,0},{8,4},{5,1},{9,5},{6,2},{10,6},{7,3},{11,7},{20,16},{24,20},... | collective-permute-start | bytes 786440 | tf_op jit(solution)/shard_map/ppermute | solution.py:521
  19.2 4.0 %collective-permute-start.6 = (bf16[1,128,256]{2,1,0:T(8,128)(2,1)S(1)}, bf16[1,128,256]{2,1,0:T(8,128)(2,1)S(1)}, u32[]{:S(2)}, u32[]{:S(2)}) collective-permute-start(bf16[1,128,256]{2,1,0:T(8,128)(2,1)S(1)} %get-tuple-element.34), channel_id=1, source_target_pairs={{0,1},{1,0},{2,3},{3,2},{4,5},{5,4},{6,7},{7,6},{8,9},{9,8},{10,11... | collective-permute-start | bytes 196616 | tf_op jit(solution)/shard_map/ppermute | solution.py:485
  19.3 4.3 %collective-permute-start.7 = (bf16[1,128,256]{2,1,0:T(8,128)(2,1)S(1)}, bf16[1,128,256]{2,1,0:T(8,128)(2,1)S(1)}, u32[]{:S(2)}, u32[]{:S(2)}) collective-permute-start(bf16[1,128,256]{2,1,0:T(8,128)(2,1)S(1)} %get-tuple-element.35), channel_id=1, source_target_pairs={{0,1},{1,0},{2,3},{3,2},{4,5},{5,4},{6,7},{7,6},{8,9},{9,8},{10,11... | collective-permute-start | bytes 196616 | tf_op jit(solution)/shard_map/ppermute | solution.py:485
  23.0 1.3 %collective-permute-start.4 = (bf16[1,128,256]{2,1,0:T(8,128)(2,1)S(1)}, bf16[1,128,256]{2,1,0:T(8,128)(2,1)S(1)}, u32[]{:S(2)}, u32[]{:S(2)}) collective-permute-start(bf16[1,128,256]{2,1,0:T(8,128)(2,1)S(1)} %get-tuple-element.32), channel_id=1, source_target_pairs={{0,1},{1,0},{2,3},{3,2},{4,5},{5,4},{6,7},{7,6},{8,9},{9,8},{10,11... | collective-permute-start | bytes 196616 | tf_op jit(solution)/shard_map/ppermute | solution.py:485
  23.2 1.3 %collective-permute-start.5 = (bf16[1,128,256]{2,1,0:T(8,128)(2,1)S(1)}, bf16[1,128,256]{2,1,0:T(8,128)(2,1)S(1)}, u32[]{:S(2)}, u32[]{:S(2)}) collective-permute-start(bf16[1,128,256]{2,1,0:T(8,128)(2,1)S(1)} %get-tuple-element.33), channel_id=1, source_target_pairs={{0,1},{1,0},{2,3},{3,2},{4,5},{5,4},{6,7},{7,6},{8,9},{9,8},{10,11... | collective-permute-start | bytes 196616 | tf_op jit(solution)/shard_map/ppermute | solution.py:485
  23.6 2.5 %collective-permute-start.9 = (bf16[1,128,256]{2,1,0:T(8,128)(2,1)S(1)}, bf16[1,128,256]{2,1,0:T(8,128)(2,1)S(1)}, u32[]{:S(2)}, u32[]{:S(2)}) collective-permute-start(bf16[1,128,256]{2,1,0:T(8,128)(2,1)S(1)} %get-tuple-element.36), channel_id=1, source_target_pairs={{0,1},{1,0},{2,3},{3,2},{4,5},{5,4},{6,7},{7,6},{8,9},{9,8},{10,11... | collective-permute-start | bytes 196616 | tf_op jit(solution)/shard_map/ppermute | solution.py:485
  24.4 1.8 %collective-permute-start.10 = (bf16[1,128,256]{2,1,0:T(8,128)(2,1)S(1)}, bf16[1,128,256]{2,1,0:T(8,128)(2,1)S(1)}, u32[]{:S(2)}, u32[]{:S(2)}) collective-permute-start(bf16[1,128,256]{2,1,0:T(8,128)(2,1)S(1)} %get-tuple-element.37), channel_id=1, source_target_pairs={{0,1},{1,0},{2,3},{3,2},{4,5},{5,4},{6,7},{7,6},{8,9},{9,8},{10,11... | collective-permute-start | bytes 196616 | tf_op jit(solution)/shard_map/ppermute | solution.py:485
  24.6 14.8 %collective-permute-start.8 = (bf16[2,256,256]{2,1,0:T(8,128)(2,1)S(1)}, bf16[2,256,256]{2,1,0:T(8,128)(2,1)S(1)}, u32[]{:S(2)}, u32[]{:S(2)}) collective-permute-start(bf16[2,256,256]{2,1,0:T(8,128)(2,1)S(1)} %shard_map.49.refs_2_), channel_id=1, source_target_pairs={{0,2},{2,0},{1,3},{3,1},{4,6},{6,4},{5,7},{7,5},{8,10},{10,8},{9,1... | collective-permute-start | bytes 786440 | tf_op jit(solution)/shard_map/ppermute | solution.py:490
  26.2 10.0 %collective-permute-start.11 = (bf16[1,256,256]{2,1,0:T(8,128)(2,1)S(1)}, bf16[1,256,256]{2,1,0:T(8,128)(2,1)S(1)}, u32[]{:S(2)}, u32[]{:S(2)}) collective-permute-start(bf16[1,256,256]{2,1,0:T(8,128)(2,1)S(1)} %shard_map.52), channel_id=1, source_target_pairs={{12,0},{14,2},{13,1},{15,3},{28,16},{30,18},{29,17},{31,19}} | collective-permute-start | bytes 393224 | tf_op jit(solution)/shard_map/ppermute | solution.py:496
  27.5 11.2 %collective-permute-start.12 = (bf16[1,256,256]{2,1,0:T(8,128)(2,1)S(1)}, bf16[1,256,256]{2,1,0:T(8,128)(2,1)S(1)}, u32[]{:S(2)}, u32[]{:S(2)}) collective-permute-start(bf16[1,256,256]{2,1,0:T(8,128)(2,1)S(1)} %shard_map.53), channel_id=1, source_target_pairs={{12,2},{14,0},{13,3},{15,1},{28,18},{30,16},{29,19},{31,17}} | collective-permute-start | bytes 393224 | tf_op jit(solution)/shard_map/ppermute | solution.py:496
  28.9 1.3 %collective-permute-start.17 = (bf16[1,128,256]{2,1,0:T(8,128)(2,1)S(1)}, bf16[1,128,256]{2,1,0:T(8,128)(2,1)S(1)}, u32[]{:S(2)}, u32[]{:S(2)}) collective-permute-start(bf16[1,128,256]{2,1,0:T(8,128)(2,1)S(1)} %get-tuple-element.43), channel_id=1, source_target_pairs={{0,1},{1,0},{2,3},{3,2},{4,5},{5,4},{6,7},{7,6},{8,9},{9,8},{10,11... | collective-permute-start | bytes 196616 | tf_op jit(solution)/shard_map/ppermute | solution.py:485
  29.1 1.3 %collective-permute-start.18 = (bf16[1,128,256]{2,1,0:T(8,128)(2,1)S(1)}, bf16[1,128,256]{2,1,0:T(8,128)(2,1)S(1)}, u32[]{:S(2)}, u32[]{:S(2)}) collective-permute-start(bf16[1,128,256]{2,1,0:T(8,128)(2,1)S(1)} %get-tuple-element.44), channel_id=1, source_target_pairs={{0,1},{1,0},{2,3},{3,2},{4,5},{5,4},{6,7},{7,6},{8,9},{9,8},{10,11... | collective-permute-start | bytes 196616 | tf_op jit(solution)/shard_map/ppermute | solution.py:485
  30.3 8.5 %collective-permute-start.1 = (bf16[1,128,256]{2,1,0:T(8,128)(2,1)S(1)}, bf16[1,128,256]{2,1,0:T(8,128)(2,1)S(1)}, u32[]{:S(2)}, u32[]{:S(2)}) collective-permute-start(bf16[1,128,256]{2,1,0:T(8,128)(2,1)S(1)} %get-tuple-element.27), channel_id=1, source_target_pairs={{0,1},{1,0},{2,3},{3,2},{4,5},{5,4},{6,7},{7,6},{8,9},{9,8},{10,11... | collective-permute-start | bytes 196616 | tf_op jit(solution)/shard_map/ppermute | solution.py:485
  30.4 8.9 %collective-permute-start = (bf16[1,128,256]{2,1,0:T(8,128)(2,1)S(1)}, bf16[1,128,256]{2,1,0:T(8,128)(2,1)S(1)}, u32[]{:S(2)}, u32[]{:S(2)}) collective-permute-start(bf16[1,128,256]{2,1,0:T(8,128)(2,1)S(1)} %get-tuple-element.26), channel_id=1, source_target_pairs={{0,1},{1,0},{2,3},{3,2},{4,5},{5,4},{6,7},{7,6},{8,9},{9,8},{10,11... | collective-permute-start | bytes 196616 | tf_op jit(solution)/shard_map/ppermute | solution.py:485
  36.2 5.2 %collective-permute-start.19 = (bf16[1,256,256]{2,1,0:T(8,128)(2,1)S(1)}, bf16[1,256,256]{2,1,0:T(8,128)(2,1)S(1)}, u32[]{:S(2)}, u32[]{:S(2)}) collective-permute-start(bf16[1,256,256]{2,1,0:T(8,128)(2,1)S(1)} %shard_map.56), channel_id=1, source_target_pairs={{0,2},{2,0},{1,3},{3,1},{4,6},{6,4},{5,7},{7,5},{8,10},{10,8},{9,1... | collective-permute-start | bytes 393224 | tf_op jit(solution)/shard_map/ppermute | solution.py:490
  38.7 1.6 %collective-permute-start.20 = (bf16[1,144,256]{2,1,0:T(8,128)(2,1)S(1)}, bf16[1,144,256]{2,1,0:T(8,128)(2,1)S(1)}, u32[]{:S(2)}, u32[]{:S(2)}) collective-permute-start(bf16[1,144,256]{2,1,0:T(8,128)(2,1)S(1)} %slice.16), channel_id=1, source_target_pairs={{0,1},{1,0},{2,3},{3,2},{4,5},{5,4},{6,7},{7,6},{8,9},{9,8},{10,11... | collective-permute-start | bytes 221192 | tf_op jit(solution)/shard_map/ppermute | solution.py:533
  38.8 1.6 %collective-permute-start.21 = (bf16[1,144,256]{2,1,0:T(8,128)(2,1)S(1)}, bf16[1,144,256]{2,1,0:T(8,128)(2,1)S(1)}, u32[]{:S(2)}, u32[]{:S(2)}) collective-permute-start(bf16[1,144,256]{2,1,0:T(8,128)(2,1)S(1)} %slice.17), channel_id=1, source_target_pairs={{0,1},{1,0},{2,3},{3,2},{4,5},{5,4},{6,7},{7,6},{8,9},{9,8},{10,11... | collective-permute-start | bytes 221192 | tf_op jit(solution)/shard_map/ppermute | solution.py:533
  39.3 1.3 %collective-permute-start.15 = (bf16[1,128,256]{2,1,0:T(8,128)(2,1)S(1)}, bf16[1,128,256]{2,1,0:T(8,128)(2,1)S(1)}, u32[]{:S(2)}, u32[]{:S(2)}) collective-permute-start(bf16[1,128,256]{2,1,0:T(8,128)(2,1)S(1)} %get-tuple-element.41), channel_id=1, source_target_pairs={{0,1},{1,0},{2,3},{3,2},{4,5},{5,4},{6,7},{7,6},{8,9},{9,8},{10,11... | collective-permute-start | bytes 196616 | tf_op jit(solution)/shard_map/ppermute | solution.py:485
  39.4 1.3 %collective-permute-start.16 = (bf16[1,128,256]{2,1,0:T(8,128)(2,1)S(1)}, bf16[1,128,256]{2,1,0:T(8,128)(2,1)S(1)}, u32[]{:S(2)}, u32[]{:S(2)}) collective-permute-start(bf16[1,128,256]{2,1,0:T(8,128)(2,1)S(1)} %get-tuple-element.42), channel_id=1, source_target_pairs={{0,1},{1,0},{2,3},{3,2},{4,5},{5,4},{6,7},{7,6},{8,9},{9,8},{10,11... | collective-permute-start | bytes 196616 | tf_op jit(solution)/shard_map/ppermute | solution.py:485

commit v5 on v4

--- a/solution.py
+++ b/solution.py
@@ -79,12 +79,14 @@
     return functools.reduce(lambda x, y: x + y, picked)
 
 
-def cross_tile(rows, cols, cross, reach, first_distance):
-    _, windows, row_count, bins = rows.shape
+def cross_tile(rows, cols, cross, reach, first_distance, begin=0, row_count=None):
+    _, windows, all_rows, bins = rows.shape
+    row_count = row_count or all_rows
     groups = cols.shape[2] // ROWS
 
     def body(step, carry):
-        row_at = pl.multiple_of((step // groups) * 8, 8)
+        row_to = pl.multiple_of((step // groups) * 8, 8)
+        row_at = pl.multiple_of(begin + row_to, 8)
         group = step % groups
         col_at = pl.multiple_of(group * ROWS, ROWS)
         nearest = first_distance + col_at - row_at
@@ -105,7 +107,7 @@
                                 sums[i][k] = product if w == 0 else sums[i][k] + product
                     for i in range(OWN):
                         k1, k2, k3 = sums[i]
-                        at_row = (group * row_count + row_at + first + i) * ROWS
+                        at_row = (group * row_count + row_to + first + i) * ROWS
                         place = pl.ds(pl.multiple_of(at_row, ROWS), ROWS)
                         cross[place, pl.ds(at, LANES)] = (k1 - k3).astype(jnp.bfloat16)
                         cross[place, pl.ds(bins + at, LANES)] = (k1 + k2).astype(jnp.bfloat16)
@@ -158,17 +160,42 @@
     lag_sums(scalars, cross, table, keep, sends)
 
 
-def partner_kernel(part_count, after_count, step, scalars, own_rows, table, *refs):
-    parts = refs[:part_count]
-    keep, *sends, cols, cross = refs[part_count + after_count :]
+def days_kernel(shifts, owners, part_count, after_count, step, scalars, own_rows, table, *refs):
+    parts, refs = refs[:part_count], refs[part_count:]
+    if not parts:
+        cols, *refs = refs
+    keep, *sends, cross = refs[after_count:]
+    if parts:
+        *sends, cols = sends
+    per = len(sends) // len(shifts)
+    width = own_rows.shape[2]
+    count = width // owners
+    size = count * ROWS // 2
+    core, day = scalars[0, 0], scalars[0, 1]
     reach = reach_of(scalars, step)
+
+    def store_at(k, half):
+        def store(kept, sent):
+            keep[k, pl.ds(half * size, size)] = kept
+            begin = 0
+            for send in sends[k * per : (k + 1) * per]:
+                low = max(begin, half * size)
+                high = min(begin + send.shape[1], (half + 1) * size)
+                if low < high:
+                    send[0, pl.ds(low - begin, high - low)] = sent[low - half * size : high - half * size]
+                begin += send.shape[1]
+
+        return store
 
     @pl.when(reach > 0)
     def _():
         for part, begin in zip(parts, begins_of(parts)):
             store_factors(part, cols, begin, col_factors)
-        cross_tile(own_rows, cols, cross, reach, step * own_rows.shape[2])
-        lag_sums(scalars, cross, table, keep, sends)
+        for k, shift in enumerate(shifts):
+            begin = lax.rem(day + shift, owners) * count
+            cross_tile(own_rows, cols, cross, reach, step * width, begin, count)
+            for half in range(HALVES):
+                lag_block(core, cross, half * 2 * size, table, size, store_at(k, half))
 
 
 def half_cross(can_swap, step, half, scalars, own_rows, part, cols, cross, swap_refs, finish):
@@ -252,6 +279,33 @@
     ] * (owners * HALVES)
 
 
+def fetch_kernel(source, *refs):
+    *parts, sems = refs
+    half = parts[0].shape[2]
+    copies = [
+        pltpu.make_async_copy(source.at[:, :, pl.ds(k * half, half)], part, sems.at[k])
+        for k, part in enumerate(parts)
+    ]
+    for copy in copies:
+        copy.start()
+    for copy in copies:
+        copy.wait()
+
+
+def fetch_halves(spectra):
+    days, windows, width, parts, bins = spectra.shape
+    shape = jax.ShapeDtypeStruct((days, windows, width // HALVES, parts, bins), spectra.dtype)
+    return pl.pallas_call(
+        fetch_kernel,
+        out_shape=[shape] * HALVES,
+        in_specs=[ANY],
+        out_specs=[VMEM] * HALVES,
+        scratch_shapes=[pltpu.SemaphoreType.DMA((HALVES,))],
+        compiler_params=PARAMS,
+        cost_estimate=FREE,
+    )(spectra)
+
+
 def own_tile(scalars, parts, table, owners):
     _, windows, _, bins = parts[0].shape
     width = sum(part.shape[2] for part in parts)
@@ -271,21 +325,26 @@
     return keep, sends, rows
 
 
-def partner_tile(scalars, own_rows, parts, table, owners, step, after):
+def days_tile(scalars, own_rows, table, owners, step, shifts, splits, parts=(), cols=None, after=()):
     _, windows, width, bins = own_rows.shape
+    col_shape = (3, windows, width, bins)
+    shapes = [jax.ShapeDtypeStruct((len(shifts), sum(splits), LAGS), jnp.float32)]
+    shapes += [jax.ShapeDtypeStruct((1, rows, LAGS), jnp.bfloat16) for rows in splits] * len(shifts)
+    if cols is None:
+        shapes.append(jax.ShapeDtypeStruct(col_shape, jnp.float32))
+    operands = list(parts) if cols is None else [cols]
     keep, *sends = pl.pallas_call(
-        functools.partial(partner_kernel, len(parts), len(after), step),
-        out_shape=sums_shapes(owners, width),
-        in_specs=[VMEM] + [VMEM] * (2 + len(parts)) + [ANY] * len(after),
-        out_specs=[VMEM] * (owners * HALVES + 1),
-        scratch_shapes=[
-            pltpu.VMEM((3, windows, width, bins), jnp.float32),
-            pltpu.VMEM((width * width, 2 * bins), jnp.bfloat16),
-        ],
-        compiler_params=PARAMS,
-        cost_estimate=FREE,
-    )(scalars, own_rows, table, *parts, *after)
-    return keep, sends
+        functools.partial(days_kernel, shifts, owners, len(parts), len(after), step),
+        out_shape=shapes,
+        in_specs=[VMEM] * (3 + len(operands)) + [ANY] * len(after),
+        out_specs=[VMEM] * len(shapes),
+        scratch_shapes=[pltpu.VMEM((width // owners * width, 2 * bins), jnp.bfloat16)],
+        compiler_params=PARAMS,
+        cost_estimate=FREE,
+    )(scalars, own_rows, table, *operands, *after)
+    if cols is None:
+        *sends, cols = sends
+    return keep, sends, cols
 
 
 def half_scratch(own_rows, can_swap):
@@ -360,7 +419,8 @@
         value = None
         for term in terms:
             if isinstance(term, list):
-                part = term[half][0]
+                whole = jnp.concatenate([part[0].astype(jnp.float32) for part in term], axis=0)
+                part = whole[half * size : (half + 1) * size]
             else:
                 array, at = term
                 part = array[at, pl.ds(half * size, size)]
@@ -474,8 +534,7 @@
 
     half = width // HALVES
     halves = [
-        jnp.transpose(spectra[:, :, at : at + half], (3, 0, 1, 2, 4)).reshape(2, -1, half, bins)
-        for at in range(0, width, half)
+        jnp.transpose(part, (3, 0, 1, 2, 4)).reshape(2, -1, half, bins) for part in fetch_halves(spectra)
     ]
     is_last = (block == blocks - 1).astype(jnp.int32) if wraps else jnp.int32(0)
     scalars = jnp.stack([core, day, is_last, day * cores + core]).astype(jnp.int32)
@@ -483,7 +542,7 @@
 
     def over_cores(sends):
         got = [lax.ppermute(send, "sub", [(k, (k + 1) % cores) for k in range(cores)]) for send in sends]
-        return [got[k * HALVES : (k + 1) * HALVES] for k in range(days)]
+        return [got[k : k + HALVES] for k in range(0, len(got), HALVES)]
 
     def over_days(pieces):
         return [
@@ -521,16 +580,25 @@
             lax.ppermute(lax.optimization_barrier((part, wait))[0], "chan", pairs)
             for part, wait in zip(ahead, waits)
         ]
-        keep, sends2 = partner_tile(scalars, own_rows, ahead, table, days, step, pieces)
-        sums = (keep, over_cores(sends2))
-        last = [add_cores([sums], shift) for shift in range(1, days)]
-        terms = [(keep, 0), sums[1][0]] + [(piece, 0) for piece in over_days(last)]
-        late.append((step, terms))
+        rows = row_count * width
+        arrived, block = [], {"parts": ahead}
+        if days > 1:
+            keep, sends2, cols = days_tile(
+                scalars, own_rows, table, days, step, range(1, days), (rows // 2, rows // 2), ahead, None, pieces
+            )
+            sums = (keep, over_cores(sends2))
+            arrived = over_days([add_cores([sums], k) for k in range(days - 1)])
+            block = {"cols": cols}
+        splits = (rows * 3 // 4, rows // 4)
+        keep, sends2, _ = days_tile(scalars, own_rows, table, days, step, [0], splits, **block)
+        got = [array for arrays in over_cores(sends2) for array in arrays]
+        late.append((step, [(keep, 0), got] + [(piece, 0) for piece in arrived]))
     if wraps:
         terms = [(piece, 0) for piece in back]
-        ready.append((steps, finished_tile(scalars, steps, terms, row_count, width, norm_scale)))
+        hosted = finished_tile(scalars, steps, terms, row_count, width, norm_scale)
+        ready.append((steps, hosted))
         pairs = [(c, (c + 1) % cores) for c in range(cores)]
-        settled = [lax.ppermute(piece[:, :SETTLED], "sub", pairs) for piece in back]
+        settled = [lax.ppermute(hosted[:3, :24], "sub", pairs)]
     return write_output(scalars, ready, late, slots, norm_scale, settled)[None]
 
 

time: 42.9 us -> 41.3 us (0.963)
  Pallas kernels: 14.2 us -> 11.7 us
  waiting for transfers between devices: 9.56 us -> 10.7 us
    slice x3 -> x1, local copies, waits for them, and re-layouts: 1.48 us -> 0.01 us  [on_device(): settled = [lax.ppermute(hosted[:3, :24], 'sub', pairs)]]
    pallas_call x1, Pallas kernels: 3.24 us -> 1.91 us  [second_half_tile(): pl.pallas_call(functools.partial(second_half_kernel, can_swap, step, len(...]
    ppermute x2, waiting for transfers between devices: 0.11 us -> 1.36 us  [on_device(): moving = [lax.ppermute(part, 'chan', pairs) for part in halves]]
    unnamed x8, local copies, waits for them, and re-layouts: 0.07 us -> 1.11 us
    pallas_call x1, Pallas kernels: 5.97 us -> 5.08 us  [own_tile(): pl.pallas_call(functools.partial(own_kernel, len(parts)), out_shape=sums_...]
    ppermute x2, starting transfers between devices: 2.51 us -> 3.28 us  [over_days(): lax.ppermute(piece, 'day', [(k, (k + shift) % days) for k in range(days)])]
    ppermute x2, waiting for transfers between devices: 0.7 us -> 0.01 us  [over_days(): lax.ppermute(piece, 'day', [(k, (k + shift) % days) for k in range(days)])]
    ppermute x2 -> x1, starting transfers between devices: 0.57 us -> 0.07 us  [on_device(): settled = [lax.ppermute(hosted[:3, :24], 'sub', pairs)]]
  transfers between devices with their start and end apart: 22 -> 21, of which waited for: 8 -> 9; matrix products, arithmetic and copies ran while one was open for 0% -> 0% of each run, Pallas kernels for 31% -> 26%
where the time goes in v5:
time: 41.3 us; the launch traced here: 40.7 us
  starting transfers between devices  16.8 us (41%)
  Pallas kernels  11.7 us (28%)
  waiting for transfers between devices  10.7 us (26%)
  local copies, waits for them, and re-layouts  1.26 us (3%)
    ppermute x2, waiting for transfers between devices, to_first(): return lax.ppermute(piece, ('chan', 'day'), pairs)  6.78 us
    ppermute x2, starting transfers between devices, on_device(): moving = [lax.ppermute(part, 'chan', pairs) for part in halves]  5.6 us
    pallas_call x1, Pallas kernels, own_tile(): pl.pallas_call(functools.partial(own_kernel, len(parts)), out_shape=sums_...  5.08 us
    ppermute x2, starting transfers between devices, over_days(): lax.ppermute(piece, 'day', [(k, (k + shift) % days) for k in range(days)])  3.28 us
    pallas_call x1, Pallas kernels, first_half_tile(): pl.pallas_call(functools.partial(first_half_kernel, can_swap, step), out_...  2.81 us
    ppermute x12, starting transfers between devices, over_cores(): lax.ppermute(send, 'sub', [(k, (k + 1) % cores) for k in range(cores)])  2.71 us
    ppermute x2, starting transfers between devices, to_first(): return lax.ppermute(piece, ('chan', 'day'), pairs)  2.58 us
    ppermute x2, starting transfers between devices, on_device(): lax.ppermute(lax.optimization_barrier((part, wait))[0], 'chan', pairs)  2.56 us
  transfers between devices with their start and end apart: 21, of which 9 were waited for; matrix products, arithmetic and copies ran while one was open for 0% of the time, Pallas kernels for 26%

profile of v5, /device:TPU:0, one launch (start us, length us, event | category | flops | bytes accessed | tf_op | source)
XLA Modules:
  0.0 40.7 jit_solution(7496827780261764394)
XLA Ops:
  0.0 1.1 %copy-done.1 = bf16[1,8,32,2,512]{4,3,2,1,0:T(2,128)(2,1)S(1)} copy-done((bf16[1,8,32,2,512]{4,3,2,1,0:T(2,128)(2,1)S(1)}, bf16[1,8,32,2,512]{4,3,2,1,0:T(2,128)(2,1)}, u32[]{:S(2)}) %copy-start.1) | copy-done | bytes 524312
  1.2 5.1 %collective-permute-start.3 = (bf16[2,8,16,512]{3,2,1,0:T(8,128)(2,1)S(1)}, bf16[2,8,16,512]{3,2,1,0:T(8,128)(2,1)S(1)}, u32[]{:S(2)}, u32[]{:S(2)}) collective-permute-start(bf16[2,8,16,512]{3,2,1,0:T(8,128)(2,1)S(1)} %bitcast.20), channel_id=1, source_target_pairs={{4,0},{8,4},{12,8},{0,12},{5,1},{9,5},{13,9},{1,13},{6,2},{10,6},{... | collective-permute-start | bytes 786440 | tf_op jit(solution)/shard_map/ppermute | solution.py:562
  6.3 0.5 %collective-permute-start.2 = (bf16[2,8,16,512]{3,2,1,0:T(8,128)(2,1)S(1)}, bf16[2,8,16,512]{3,2,1,0:T(8,128)(2,1)S(1)}, u32[]{:S(2)}, u32[]{:S(2)}) collective-permute-start(bf16[2,8,16,512]{3,2,1,0:T(8,128)(2,1)S(1)} %bitcast.18), channel_id=1, source_target_pairs={{4,0},{8,4},{12,8},{0,12},{5,1},{9,5},{13,9},{1,13},{6,2},{10,6},{... | collective-permute-start | bytes 786440 | tf_op jit(solution)/shard_map/ppermute | solution.py:562
  6.9 5.1 %shard_map.47 = (f32[2,256,256]{2,1,0:T(8,128)S(1)}, bf16[1,128,256]{2,1,0:T(8,128)(2,1)S(1)}, bf16[1,128,256]{2,1,0:T(8,128)(2,1)S(1)}, bf16[1,128,256]{2,1,0:T...) custom-call(s32[1,10]{1,0:T(1,128)S(1)} %bitcast.22, bf16[1024,256]{1,0:T(8,128)(2,1)S(1)} %copy-done, ...), custom_call_target="tpu_custom_call" | custom-call | tf_op jit(solution)/shard_map/pallas_call | solution.py:313
  12.0 1.0 %collective-permute-done.3.part = bf16[2,8,16,512]{3,2,1,0:T(8,128)(2,1)S(1)} collective-permute-done((bf16[2,8,16,512]{3,2,1,0:T(8,128)(2,1)S(1)}, bf16[2,8,16,512]{3,2,1,0:T(8,128)(2,1)S(1)}, u32[]{:S(2)}, u32[]{:S(2)}) %collective-permute-start.3) | collective-permute-done | bytes 262176 | tf_op jit(solution)/shard_map/ppermute | solution.py:562
  13.0 1.3 %collective-permute-start.13 = (bf16[2,8,16,512]{3,2,1,0:T(8,128)(2,1)S(1)}, bf16[2,8,16,512]{3,2,1,0:T(8,128)(2,1)S(1)}, u32[]{:S(2)}, u32[]{:S(2)}) collective-permute-start(bf16[2,8,16,512]{3,2,1,0:T(8,128)(2,1)S(1)} %collective-permute-done.3.part), channel_id=1, source_target_pairs={{4,0},{8,4},{5,1},{9,5},{6,2},{10,6},{7,3},{11,7},{20,16},{24,20},... | collective-permute-start | bytes 786440 | tf_op jit(solution)/shard_map/ppermute | solution.py:580
  14.3 2.8 %shard_map.48 = (f32[2,128,256]{2,1,0:T(8,128)S(1)}, bf16[2,128,256]{2,1,0:T(8,128)(2,1)S(1)}) custom-call(s32[1,10]{1,0:T(1,128)S(1)} %bitcast.23, f32[3,8,32,512]{3,2,1,0:T(8,128)S(1)} %get-tuple-element.34.own_rows, bf16[1024,256]{1,0:T(8,128)(2,1)S(1)} %copy-done, bf16[2,8,16,512]{3,2,1,0:T(8,128)(2,1)S(1)} %collective-permute-done.3.part), custom_call_target="tpu_custom_call" | custom-call | tf_op jit(solution)/shard_map/pallas_call | solution.py:363
  17.1 0.4 collective-permute-done.2.part
  17.5 1.3 %collective-permute-start.14 = (bf16[2,8,16,512]{3,2,1,0:T(8,128)(2,1)S(1)}, bf16[2,8,16,512]{3,2,1,0:T(8,128)(2,1)S(1)}, u32[]{:S(2)}, u32[]{:S(2)}) collective-permute-start(bf16[2,8,16,512]{3,2,1,0:T(8,128)(2,1)S(1)} %collective-permute-done.2.part), channel_id=1, source_target_pairs={{4,0},{8,4},{5,1},{9,5},{6,2},{10,6},{7,3},{11,7},{20,16},{24,20},... | collective-permute-start | bytes 786440 | tf_op jit(solution)/shard_map/ppermute | solution.py:580
  18.9 0.5 %collective-permute-start.7 = (bf16[1,128,256]{2,1,0:T(8,128)(2,1)S(1)}, bf16[1,128,256]{2,1,0:T(8,128)(2,1)S(1)}, u32[]{:S(2)}, u32[]{:S(2)}) collective-permute-start(bf16[1,128,256]{2,1,0:T(8,128)(2,1)S(1)} %get-tuple-element.41), channel_id=1, source_target_pairs={{0,1},{1,0},{2,3},{3,2},{4,5},{5,4},{6,7},{7,6},{8,9},{9,8},{10,11... | collective-permute-start | bytes 196616 | tf_op jit(solution)/shard_map/ppermute | solution.py:544
  19.4 1.9 %shard_map.49 = (f32[2,256,256]{2,1,0:T(8,128)S(1)}, bf16[1,128,256]{2,1,0:T(8,128)(2,1)S(1)}, bf16[1,128,256]{2,1,0:T(8,128)(2,1)S(1)}, bf16[1,128,256]{2,1,0:T(8,128)(2,1)S(1)}, bf16[1,128,256]{2,1,0:T(8,128)(2,1)S(1)}) custom-call(s32[1,10]{1,0:T(1,128)S(1)} %bitcast.24, f32[3,8,32,512]{3,2,1,0:T(8,128)S(1)} %get-tuple-element.34.own_rows, ...), custom_call_target="tpu_custom_call" | custom-call | tf_op jit(solution)/shard_map/pallas_call | solution.py:378
  21.3 0.2 collective-permute-start.4
  21.4 0.4 %collective-permute-start.5 = (bf16[1,128,256]{2,1,0:T(8,128)(2,1)S(1)}, bf16[1,128,256]{2,1,0:T(8,128)(2,1)S(1)}, u32[]{:S(2)}, u32[]{:S(2)}) collective-permute-start(bf16[1,128,256]{2,1,0:T(8,128)(2,1)S(1)} %get-tuple-element.39), channel_id=1, source_target_pairs={{0,1},{1,0},{2,3},{3,2},{4,5},{5,4},{6,7},{7,6},{8,9},{9,8},{10,11... | collective-permute-start | bytes 196616 | tf_op jit(solution)/shard_map/ppermute | solution.py:544
  22.0 0.6 %collective-permute-done.4.refs_1_ = bf16[1,128,256]{2,1,0:T(8,128)(2,1)S(1)} collective-permute-done((bf16[1,128,256]{2,1,0:T(8,128)(2,1)S(1)}, bf16[1,128,256]{2,1,0:T(8,128)(2,1)S(1)}, u32[]{:S(2)}, u32[]{:S(2)}) %collective-permute-start.4) | collective-permute-done | bytes 65568 | tf_op jit(solution)/shard_map/ppermute | solution.py:544
  22.6 0.2 collective-permute-start.10
  22.8 1.6 %collective-permute-start.8 = (bf16[2,256,256]{2,1,0:T(8,128)(2,1)S(1)}, bf16[2,256,256]{2,1,0:T(8,128)(2,1)S(1)}, u32[]{:S(2)}, u32[]{:S(2)}) collective-permute-start(bf16[2,256,256]{2,1,0:T(8,128)(2,1)S(1)} %shard_map.50.refs_2_), channel_id=1, source_target_pairs={{0,2},{2,0},{1,3},{3,1},{4,6},{6,4},{5,7},{7,5},{8,10},{10,8},{9,1... | collective-permute-start | bytes 786440 | tf_op jit(solution)/shard_map/ppermute | solution.py:549
  24.4 1.3 %collective-permute-start.11 = (bf16[1,256,256]{2,1,0:T(8,128)(2,1)S(1)}, bf16[1,256,256]{2,1,0:T(8,128)(2,1)S(1)}, u32[]{:S(2)}, u32[]{:S(2)}) collective-permute-start(bf16[1,256,256]{2,1,0:T(8,128)(2,1)S(1)} %shard_map.53), channel_id=1, source_target_pairs={{12,0},{14,2},{13,1},{15,3},{28,16},{30,18},{29,17},{31,19}} | collective-permute-start | bytes 393224 | tf_op jit(solution)/shard_map/ppermute | solution.py:555
  25.7 1.3 %collective-permute-start.12 = (bf16[1,256,256]{2,1,0:T(8,128)(2,1)S(1)}, bf16[1,256,256]{2,1,0:T(8,128)(2,1)S(1)}, u32[]{:S(2)}, u32[]{:S(2)}) collective-permute-start(bf16[1,256,256]{2,1,0:T(8,128)(2,1)S(1)} %shard_map.54), channel_id=1, source_target_pairs={{12,2},{14,0},{13,3},{15,1},{28,18},{30,16},{29,19},{31,17}} | collective-permute-start | bytes 393224 | tf_op jit(solution)/shard_map/ppermute | solution.py:555
  27.1 0.4 collective-permute-done.14.refs_1_
  27.6 0.5 %collective-permute-start.18 = (bf16[1,128,256]{2,1,0:T(8,128)(2,1)S(1)}, bf16[1,128,256]{2,1,0:T(8,128)(2,1)S(1)}, u32[]{:S(2)}, u32[]{:S(2)}) collective-permute-start(bf16[1,128,256]{2,1,0:T(8,128)(2,1)S(1)} %get-tuple-element.52), channel_id=1, source_target_pairs={{0,1},{1,0},{2,3},{3,2},{4,5},{5,4},{6,7},{7,6},{8,9},{9,8},{10,11... | collective-permute-start | bytes 196616 | tf_op jit(solution)/shard_map/ppermute | solution.py:544
  28.1 0.7 %collective-permute-done.17.refs_1_ = bf16[1,128,256]{2,1,0:T(8,128)(2,1)S(1)} collective-permute-done((bf16[1,128,256]{2,1,0:T(8,128)(2,1)S(1)}, bf16[1,128,256]{2,1,0:T(8,128)(2,1)S(1)}, u32[]{:S(2)}, u32[]{:S(2)}) %collective-permute-start.17) | collective-permute-done | bytes 65568 | tf_op jit(solution)/shard_map/ppermute | solution.py:544
  28.9 0.2 collective-permute-start
  29.1 1.7 %collective-permute-start.19 = (bf16[1,256,256]{2,1,0:T(8,128)(2,1)S(1)}, bf16[1,256,256]{2,1,0:T(8,128)(2,1)S(1)}, u32[]{:S(2)}, u32[]{:S(2)}) collective-permute-start(bf16[1,256,256]{2,1,0:T(8,128)(2,1)S(1)} %shard_map.58), channel_id=1, source_target_pairs={{0,2},{2,0},{1,3},{3,1},{4,6},{6,4},{5,7},{7,5},{8,10},{10,8},{9,1... | collective-permute-start | bytes 393224 | tf_op jit(solution)/shard_map/ppermute | solution.py:549
  30.9 4.0 %collective-permute-done.11.refs_0_ = bf16[1,256,256]{2,1,0:T(8,128)(2,1)S(1)} collective-permute-done((bf16[1,256,256]{2,1,0:T(8,128)(2,1)S(1)}, bf16[1,256,256]{2,1,0:T(8,128)(2,1)S(1)}, u32[]{:S(2)}, u32[]{:S(2)}) %collective-permute-start.11) | collective-permute-done | bytes 131104 | tf_op jit(solution)/shard_map/ppermute | solution.py:555
  34.9 2.8 %collective-permute-done.12.refs_1_ = bf16[1,256,256]{2,1,0:T(8,128)(2,1)S(1)} collective-permute-done((bf16[1,256,256]{2,1,0:T(8,128)(2,1)S(1)}, bf16[1,256,256]{2,1,0:T(8,128)(2,1)S(1)}, u32[]{:S(2)}, u32[]{:S(2)}) %collective-permute-start.12) | collective-permute-done | bytes 131104 | tf_op jit(solution)/shard_map/ppermute | solution.py:555
  37.7 0.2 shard_map.55.refs_2_
  38.0 0.5 %collective-permute-start.1 = (bf16[1,128,256]{2,1,0:T(8,128)(2,1)S(1)}, bf16[1,128,256]{2,1,0:T(8,128)(2,1)S(1)}, u32[]{:S(2)}, u32[]{:S(2)}) collective-permute-start(bf16[1,128,256]{2,1,0:T(8,128)(2,1)S(1)} %get-tuple-element.33), channel_id=1, source_target_pairs={{0,1},{1,0},{2,3},{3,2},{4,5},{5,4},{6,7},{7,6},{8,9},{9,8},{10,11... | collective-permute-start | bytes 196616 | tf_op jit(solution)/shard_map/ppermute | solution.py:544
  38.6 0.2 shard_map.52.refs_1_
  38.7 0.6 %collective-permute-done.1.refs_2_ = bf16[1,128,256]{2,1,0:T(8,128)(2,1)S(1)} collective-permute-done((bf16[1,128,256]{2,1,0:T(8,128)(2,1)S(1)}, bf16[1,128,256]{2,1,0:T(8,128)(2,1)S(1)}, u32[]{:S(2)}, u32[]{:S(2)}) %collective-permute-start.1) | collective-permute-done | bytes 65568 | tf_op jit(solution)/shard_map/ppermute | solution.py:544
  39.4 0.2 shard_map.51.refs_0_
  39.5 0.1 collective-permute-done.16.refs_5_
  39.7 1.0 %shard_map.59 = f32[3,8,32,256]{3,2,1,0:T(8,128)} custom-call(s32[1,10]{1,0:T(1,128)S(1)} %bitcast.30, f32[8,32,256]{2,1,0:T(8,128)S(1)} %shard_map.51.refs_0_, f32[8,32,256]{2,1,0:T(8,128)S(1)} %shard_map.52.refs_1_, f32[8,32,256]{2,1,0:T(8,128)S(1)} %shard_map.55.refs_2_, f32[1,256,256]{2,1,0:T(8,128)S(1)} %get-tuple-element.47.refs_3_, ...), custom_call_target="tpu_custom_call" | custom-call | tf_op jit(solution)/shard_map/pallas_call | solution.py:508
  (36 shorter events, 1.0 us)
Async XLA Ops:
  0.0 6.9 %copy-start = (bf16[1024,256]{1,0:T(8,128)(2,1)S(1)}, bf16[1024,256]{1,0:T(8,128)(2,1)}, u32[]{:S(2)}) copy-start(bf16[1024,256]{1,0:T(8,128)(2,1)} %constant.17.clone.table) | copy-start | bytes 1572868
  0.0 1.1 %copy-start.1 = (bf16[1,8,32,2,512]{4,3,2,1,0:T(2,128)(2,1)S(1)}, bf16[1,8,32,2,512]{4,3,2,1,0:T(2,128)(2,1)}, u32[]{:S(2)}) copy-start(bf16[1,8,32,2,512]{4,3,2,1,0:T(2,128)(2,1)} %source.1) | copy-start | bytes 1572868
  1.1 5.8 %copy-start.2 = (s32[1,3]{1,0:T(1,128)S(1)}, s32[1,3]{1,0:T(1,128)}, u32[]{:S(2)}) copy-start(s32[1,3]{1,0:T(1,128)} %param.5) | copy-start | bytes 40
  1.1 5.8 %copy-start.3 = (s32[1,3]{1,0:T(1,128)S(1)}, s32[1,3]{1,0:T(1,128)}, u32[]{:S(2)}) copy-start(s32[1,3]{1,0:T(1,128)} %param.6) | copy-start | bytes 40
  1.2 11.8 %collective-permute-start.3 = (bf16[2,8,16,512]{3,2,1,0:T(8,128)(2,1)S(1)}, bf16[2,8,16,512]{3,2,1,0:T(8,128)(2,1)S(1)}, u32[]{:S(2)}, u32[]{:S(2)}) collective-permute-start(bf16[2,8,16,512]{3,2,1,0:T(8,128)(2,1)S(1)} %bitcast.20), channel_id=1, source_target_pairs={{4,0},{8,4},{12,8},{0,12},{5,1},{9,5},{13,9},{1,13},{6,2},{10,6},{... | collective-permute-start | bytes 786440 | tf_op jit(solution)/shard_map/ppermute | solution.py:562
  6.3 11.1 %collective-permute-start.2 = (bf16[2,8,16,512]{3,2,1,0:T(8,128)(2,1)S(1)}, bf16[2,8,16,512]{3,2,1,0:T(8,128)(2,1)S(1)}, u32[]{:S(2)}, u32[]{:S(2)}) collective-permute-start(bf16[2,8,16,512]{3,2,1,0:T(8,128)(2,1)S(1)} %bitcast.18), channel_id=1, source_target_pairs={{4,0},{8,4},{12,8},{0,12},{5,1},{9,5},{13,9},{1,13},{6,2},{10,6},{... | collective-permute-start | bytes 786440 | tf_op jit(solution)/shard_map/ppermute | solution.py:562
  13.0 14.0 %collective-permute-start.13 = (bf16[2,8,16,512]{3,2,1,0:T(8,128)(2,1)S(1)}, bf16[2,8,16,512]{3,2,1,0:T(8,128)(2,1)S(1)}, u32[]{:S(2)}, u32[]{:S(2)}) collective-permute-start(bf16[2,8,16,512]{3,2,1,0:T(8,128)(2,1)S(1)} %collective-permute-done.3.part), channel_id=1, source_target_pairs={{4,0},{8,4},{5,1},{9,5},{6,2},{10,6},{7,3},{11,7},{20,16},{24,20},... | collective-permute-start | bytes 786440 | tf_op jit(solution)/shard_map/ppermute | solution.py:580
  17.5 10.0 %collective-permute-start.14 = (bf16[2,8,16,512]{3,2,1,0:T(8,128)(2,1)S(1)}, bf16[2,8,16,512]{3,2,1,0:T(8,128)(2,1)S(1)}, u32[]{:S(2)}, u32[]{:S(2)}) collective-permute-start(bf16[2,8,16,512]{3,2,1,0:T(8,128)(2,1)S(1)} %collective-permute-done.2.part), channel_id=1, source_target_pairs={{4,0},{8,4},{5,1},{9,5},{6,2},{10,6},{7,3},{11,7},{20,16},{24,20},... | collective-permute-start | bytes 786440 | tf_op jit(solution)/shard_map/ppermute | solution.py:580
  18.8 2.7 %collective-permute-start.6 = (bf16[1,128,256]{2,1,0:T(8,128)(2,1)S(1)}, bf16[1,128,256]{2,1,0:T(8,128)(2,1)S(1)}, u32[]{:S(2)}, u32[]{:S(2)}) collective-permute-start(bf16[1,128,256]{2,1,0:T(8,128)(2,1)S(1)} %get-tuple-element.40), channel_id=1, source_target_pairs={{0,1},{1,0},{2,3},{3,2},{4,5},{5,4},{6,7},{7,6},{8,9},{9,8},{10,11... | collective-permute-start | bytes 196616 | tf_op jit(solution)/shard_map/ppermute | solution.py:544
  18.9 3.0 %collective-permute-start.7 = (bf16[1,128,256]{2,1,0:T(8,128)(2,1)S(1)}, bf16[1,128,256]{2,1,0:T(8,128)(2,1)S(1)}, u32[]{:S(2)}, u32[]{:S(2)}) collective-permute-start(bf16[1,128,256]{2,1,0:T(8,128)(2,1)S(1)} %get-tuple-element.41), channel_id=1, source_target_pairs={{0,1},{1,0},{2,3},{3,2},{4,5},{5,4},{6,7},{7,6},{8,9},{9,8},{10,11... | collective-permute-start | bytes 196616 | tf_op jit(solution)/shard_map/ppermute | solution.py:544
  21.3 1.3 %collective-permute-start.4 = (bf16[1,128,256]{2,1,0:T(8,128)(2,1)S(1)}, bf16[1,128,256]{2,1,0:T(8,128)(2,1)S(1)}, u32[]{:S(2)}, u32[]{:S(2)}) collective-permute-start(bf16[1,128,256]{2,1,0:T(8,128)(2,1)S(1)} %get-tuple-element.38), channel_id=1, source_target_pairs={{0,1},{1,0},{2,3},{3,2},{4,5},{5,4},{6,7},{7,6},{8,9},{9,8},{10,11... | collective-permute-start | bytes 196616 | tf_op jit(solution)/shard_map/ppermute | solution.py:544
  21.4 1.3 %collective-permute-start.5 = (bf16[1,128,256]{2,1,0:T(8,128)(2,1)S(1)}, bf16[1,128,256]{2,1,0:T(8,128)(2,1)S(1)}, u32[]{:S(2)}, u32[]{:S(2)}) collective-permute-start(bf16[1,128,256]{2,1,0:T(8,128)(2,1)S(1)} %get-tuple-element.39), channel_id=1, source_target_pairs={{0,1},{1,0},{2,3},{3,2},{4,5},{5,4},{6,7},{7,6},{8,9},{9,8},{10,11... | collective-permute-start | bytes 196616 | tf_op jit(solution)/shard_map/ppermute | solution.py:544
  21.9 2.5 %collective-permute-start.9 = (bf16[1,128,256]{2,1,0:T(8,128)(2,1)S(1)}, bf16[1,128,256]{2,1,0:T(8,128)(2,1)S(1)}, u32[]{:S(2)}, u32[]{:S(2)}) collective-permute-start(bf16[1,128,256]{2,1,0:T(8,128)(2,1)S(1)} %get-tuple-element.42), channel_id=1, source_target_pairs={{0,1},{1,0},{2,3},{3,2},{4,5},{5,4},{6,7},{7,6},{8,9},{9,8},{10,11... | collective-permute-start | bytes 196616 | tf_op jit(solution)/shard_map/ppermute | solution.py:544
  22.6 1.8 %collective-permute-start.10 = (bf16[1,128,256]{2,1,0:T(8,128)(2,1)S(1)}, bf16[1,128,256]{2,1,0:T(8,128)(2,1)S(1)}, u32[]{:S(2)}, u32[]{:S(2)}) collective-permute-start(bf16[1,128,256]{2,1,0:T(8,128)(2,1)S(1)} %get-tuple-element.43), channel_id=1, source_target_pairs={{0,1},{1,0},{2,3},{3,2},{4,5},{5,4},{6,7},{7,6},{8,9},{9,8},{10,11... | collective-permute-start | bytes 196616 | tf_op jit(solution)/shard_map/ppermute | solution.py:544
  22.8 15.7 %collective-permute-start.8 = (bf16[2,256,256]{2,1,0:T(8,128)(2,1)S(1)}, bf16[2,256,256]{2,1,0:T(8,128)(2,1)S(1)}, u32[]{:S(2)}, u32[]{:S(2)}) collective-permute-start(bf16[2,256,256]{2,1,0:T(8,128)(2,1)S(1)} %shard_map.50.refs_2_), channel_id=1, source_target_pairs={{0,2},{2,0},{1,3},{3,1},{4,6},{6,4},{5,7},{7,5},{8,10},{10,8},{9,1... | collective-permute-start | bytes 786440 | tf_op jit(solution)/shard_map/ppermute | solution.py:549
  24.4 10.5 %collective-permute-start.11 = (bf16[1,256,256]{2,1,0:T(8,128)(2,1)S(1)}, bf16[1,256,256]{2,1,0:T(8,128)(2,1)S(1)}, u32[]{:S(2)}, u32[]{:S(2)}) collective-permute-start(bf16[1,256,256]{2,1,0:T(8,128)(2,1)S(1)} %shard_map.53), channel_id=1, source_target_pairs={{12,0},{14,2},{13,1},{15,3},{28,16},{30,18},{29,17},{31,19}} | collective-permute-start | bytes 393224 | tf_op jit(solution)/shard_map/ppermute | solution.py:555
  25.7 12.0 %collective-permute-start.12 = (bf16[1,256,256]{2,1,0:T(8,128)(2,1)S(1)}, bf16[1,256,256]{2,1,0:T(8,128)(2,1)S(1)}, u32[]{:S(2)}, u32[]{:S(2)}) collective-permute-start(bf16[1,256,256]{2,1,0:T(8,128)(2,1)S(1)} %shard_map.54), channel_id=1, source_target_pairs={{12,2},{14,0},{13,3},{15,1},{28,18},{30,16},{29,19},{31,17}} | collective-permute-start | bytes 393224 | tf_op jit(solution)/shard_map/ppermute | solution.py:555
  27.6 1.3 %collective-permute-start.17 = (bf16[1,128,256]{2,1,0:T(8,128)(2,1)S(1)}, bf16[1,128,256]{2,1,0:T(8,128)(2,1)S(1)}, u32[]{:S(2)}, u32[]{:S(2)}) collective-permute-start(bf16[1,128,256]{2,1,0:T(8,128)(2,1)S(1)} %get-tuple-element.51), channel_id=1, source_target_pairs={{0,1},{1,0},{2,3},{3,2},{4,5},{5,4},{6,7},{7,6},{8,9},{9,8},{10,11... | collective-permute-start | bytes 196616 | tf_op jit(solution)/shard_map/ppermute | solution.py:544
  27.6 1.4 %collective-permute-start.18 = (bf16[1,128,256]{2,1,0:T(8,128)(2,1)S(1)}, bf16[1,128,256]{2,1,0:T(8,128)(2,1)S(1)}, u32[]{:S(2)}, u32[]{:S(2)}) collective-permute-start(bf16[1,128,256]{2,1,0:T(8,128)(2,1)S(1)} %get-tuple-element.52), channel_id=1, source_target_pairs={{0,1},{1,0},{2,3},{3,2},{4,5},{5,4},{6,7},{7,6},{8,9},{9,8},{10,11... | collective-permute-start | bytes 196616 | tf_op jit(solution)/shard_map/ppermute | solution.py:544
  28.9 9.1 %collective-permute-start = (bf16[1,128,256]{2,1,0:T(8,128)(2,1)S(1)}, bf16[1,128,256]{2,1,0:T(8,128)(2,1)S(1)}, u32[]{:S(2)}, u32[]{:S(2)}) collective-permute-start(bf16[1,128,256]{2,1,0:T(8,128)(2,1)S(1)} %get-tuple-element.32), channel_id=1, source_target_pairs={{0,1},{1,0},{2,3},{3,2},{4,5},{5,4},{6,7},{7,6},{8,9},{9,8},{10,11... | collective-permute-start | bytes 196616 | tf_op jit(solution)/shard_map/ppermute | solution.py:544
  29.1 10.6 %collective-permute-start.19 = (bf16[1,256,256]{2,1,0:T(8,128)(2,1)S(1)}, bf16[1,256,256]{2,1,0:T(8,128)(2,1)S(1)}, u32[]{:S(2)}, u32[]{:S(2)}) collective-permute-start(bf16[1,256,256]{2,1,0:T(8,128)(2,1)S(1)} %shard_map.58), channel_id=1, source_target_pairs={{0,2},{2,0},{1,3},{3,1},{4,6},{6,4},{5,7},{7,5},{8,10},{10,8},{9,1... | collective-permute-start | bytes 393224 | tf_op jit(solution)/shard_map/ppermute | solution.py:549
  34.9 4.7 %collective-permute-start.15 = (bf16[1,192,256]{2,1,0:T(8,128)(2,1)S(1)}, bf16[1,192,256]{2,1,0:T(8,128)(2,1)S(1)}, u32[]{:S(2)}, u32[]{:S(2)}) collective-permute-start(bf16[1,192,256]{2,1,0:T(8,128)(2,1)S(1)} %get-tuple-element.48), channel_id=1, source_target_pairs={{0,1},{1,0},{2,3},{3,2},{4,5},{5,4},{6,7},{7,6},{8,9},{9,8},{10,11... | collective-permute-start | bytes 294920 | tf_op jit(solution)/shard_map/ppermute | solution.py:544
  37.9 1.6 %collective-permute-start.20 = (f32[3,24,256]{2,1,0:T(8,128)S(1)}, f32[3,24,256]{2,1,0:T(8,128)S(1)}, u32[]{:S(2)}, u32[]{:S(2)}) collective-permute-start(f32[3,24,256]{2,1,0:T(8,128)S(1)} %slice.4), channel_id=1, source_target_pairs={{0,1},{1,0},{2,3},{3,2},{4,5},{5,4},{6,7},{7,6},{8,9},{9,8},{10,11... | collective-permute-start | bytes 221192 | tf_op jit(solution)/shard_map/ppermute | solution.py:601
  38.0 1.4 %collective-permute-start.1 = (bf16[1,128,256]{2,1,0:T(8,128)(2,1)S(1)}, bf16[1,128,256]{2,1,0:T(8,128)(2,1)S(1)}, u32[]{:S(2)}, u32[]{:S(2)}) collective-permute-start(bf16[1,128,256]{2,1,0:T(8,128)(2,1)S(1)} %get-tuple-element.33), channel_id=1, source_target_pairs={{0,1},{1,0},{2,3},{3,2},{4,5},{5,4},{6,7},{7,6},{8,9},{9,8},{10,11... | collective-permute-start | bytes 196616 | tf_op jit(solution)/shard_map/ppermute | solution.py:544
  38.5 1.2 %collective-permute-start.16 = (bf16[1,64,256]{2,1,0:T(8,128)(2,1)S(1)}, bf16[1,64,256]{2,1,0:T(8,128)(2,1)S(1)}, u32[]{:S(2)}, u32[]{:S(2)}) collective-permute-start(bf16[1,64,256]{2,1,0:T(8,128)(2,1)S(1)} %get-tuple-element.49), channel_id=1, source_target_pairs={{0,1},{1,0},{2,3},{3,2},{4,5},{5,4},{6,7},{7,6},{8,9},{9,8},{10,11... | collective-permute-start | bytes 98312 | tf_op jit(solution)/shard_map/ppermute | solution.py:544

commit v6 on v5

--- a/solution.py
+++ b/solution.py
@@ -125,6 +125,21 @@
     pl.when(core != 0)(lambda: store(high, low.astype(jnp.bfloat16)))
 
 
+def lag_blocks(core, cross, blocks, table, size, store):
+    lags = jnp.dot(cross[: blocks * 2 * size], table[...], preferred_element_type=jnp.float32)
+    parts = [(lags[k * 2 * size :][:size], lags[(k * 2 + 1) * size :][:size]) for k in range(blocks)]
+
+    @pl.when(core == 0)
+    def _():
+        for k, (low, high) in enumerate(parts):
+            store(k, low, high.astype(jnp.bfloat16))
+
+    @pl.when(core != 0)
+    def _():
+        for k, (low, high) in enumerate(parts):
+            store(k, high, low.astype(jnp.bfloat16))
+
+
 def store_at(keep, sends, shift, half):
     def store(kept, sent):
         size = sent.shape[0]
@@ -174,18 +189,15 @@
     core, day = scalars[0, 0], scalars[0, 1]
     reach = reach_of(scalars, step)
 
-    def store_at(k, half):
-        def store(kept, sent):
-            keep[k, pl.ds(half * size, size)] = kept
-            begin = 0
-            for send in sends[k * per : (k + 1) * per]:
-                low = max(begin, half * size)
-                high = min(begin + send.shape[1], (half + 1) * size)
-                if low < high:
-                    send[0, pl.ds(low - begin, high - low)] = sent[low - half * size : high - half * size]
-                begin += send.shape[1]
-
-        return store
+    def store(k, half, kept, sent):
+        keep[k, pl.ds(half * size, size)] = kept
+        begin = 0
+        for send in sends[k * per : (k + 1) * per]:
+            low = max(begin, half * size)
+            high = min(begin + send.shape[1], (half + 1) * size)
+            if low < high:
+                send[0, pl.ds(low - begin, high - low)] = sent[low - half * size : high - half * size]
+            begin += send.shape[1]
 
     @pl.when(reach > 0)
     def _():
@@ -194,8 +206,7 @@
         for k, shift in enumerate(shifts):
             begin = lax.rem(day + shift, owners) * count
             cross_tile(own_rows, cols, cross, reach, step * width, begin, count)
-            for half in range(HALVES):
-                lag_block(core, cross, half * 2 * size, table, size, store_at(k, half))
+            lag_blocks(core, cross, HALVES, table, size, functools.partial(store, k))
 
 
 def half_cross(can_swap, step, half, scalars, own_rows, part, cols, cross, swap_refs, finish):
@@ -227,13 +238,11 @@
     owners, size = keep.shape[0], keep.shape[1]
 
     def finish(swapped):
-        for k in range(owners):
-
-            def store(kept, sent, k=k):
-                keep[k] = kept
-                send[k] = sent
-
-            lag_block(scalars[0, 0], cross, k * 2 * size, table, size, store)
+        def store(k, kept, sent):
+            keep[k] = kept
+            send[k] = sent
+
+        lag_blocks(scalars[0, 0], cross, owners, table, size, store)
 
     half_cross(can_swap, step, 0, scalars, own_rows, part, cols, cross, swap_refs, finish)
 
@@ -248,20 +257,24 @@
     core, day = scalars[0, 0], scalars[0, 1]
 
     def finish(swapped):
+        def store(block, kept, sent):
+            for shift in range(owners):
+                owner = lax.rem(day + shift, owners)
+                half = block if swapped else 1
+                here = owner != 0 if swapped else owner == block
+                pl.when(here)(lambda: store_at(keep, sends, shift, half)(kept, sent))
+
         for shift in range(owners):
             owner = lax.rem(day + shift, owners)
-            if not swapped:
+            if swapped:
+                for half in range(HALVES):
+                    copy = functools.partial(
+                        store_at(keep, sends, shift, half), first_keep[half], first_send[half]
+                    )
+                    pl.when(owner == 0)(copy)
+            else:
                 store_at(keep, sends, shift, 0)(first_keep[owner], first_send[owner])
-                lag_block(core, cross, owner * 2 * size, table, size, store_at(keep, sends, shift, 1))
-                continue
-            for half in range(HALVES):
-                store = store_at(keep, sends, shift, half)
-                pl.when(owner == 0)(lambda store=store, half=half: store(first_keep[half], first_send[half]))
-                pl.when(owner != 0)(
-                    lambda store=store, half=half: lag_block(
-                        core, cross, half * 2 * size, table, size, store
-                    )
-                )
+        lag_blocks(core, cross, HALVES if swapped else owners, table, size, store)
 
     half_cross(can_swap, step, 1, scalars, own_rows, part, cols, cross, swap_refs, finish)
 

time: 41.3 us -> 41 us (level); the launches traced: 40.7 us -> 40.9 us
  Pallas kernels: 11.7 us -> 13.6 us
  waiting for transfers between devices: 10.7 us -> 9.32 us
    pallas_call x1, Pallas kernels: 1.91 us -> 2.9 us  [second_half_tile(): pl.pallas_call(functools.partial(second_half_kernel, can_swap, step, len(...]
    ppermute x2, waiting for transfers between devices: 1.36 us -> 0.43 us  [on_device(): moving = [lax.ppermute(part, 'chan', pairs) for part in halves]]
    pallas_call x1, Pallas kernels: 5.08 us -> 5.97 us  [own_tile(): pl.pallas_call(functools.partial(own_kernel, len(parts)), out_shape=sums_...]
  transfers between devices with their start and end apart: 21 -> 21, of which waited for: 9 -> 8; matrix products, arithmetic and copies ran while one was open for 0% -> 0% of each run, Pallas kernels for 26% -> 31%
where the time goes in v6:
time: 41 us; the launch traced here: 40.9 us
  starting transfers between devices  16.5 us (40%)
  Pallas kernels  13.6 us (33%)
  waiting for transfers between devices  9.32 us (23%)
  local copies, waits for them, and re-layouts  1.26 us (3%)
    ppermute x2, waiting for transfers between devices, to_first(): return lax.ppermute(piece, ('chan', 'day'), pairs)  6.67 us
    pallas_call x1, Pallas kernels, own_tile(): pl.pallas_call(functools.partial(own_kernel, len(parts)), out_shape=sums_...  5.97 us
    ppermute x2, starting transfers between devices, on_device(): moving = [lax.ppermute(part, 'chan', pairs) for part in halves]  5.6 us
    ppermute x2, starting transfers between devices, over_days(): lax.ppermute(piece, 'day', [(k, (k + shift) % days) for k in range(days)])  3.03 us
    pallas_call x1, Pallas kernels, second_half_tile(): pl.pallas_call(functools.partial(second_half_kernel, can_swap, step, len(...  2.9 us
    pallas_call x1, Pallas kernels, first_half_tile(): pl.pallas_call(functools.partial(first_half_kernel, can_swap, step), out_...  2.85 us
    ppermute x12, starting transfers between devices, over_cores(): lax.ppermute(send, 'sub', [(k, (k + 1) % cores) for k in range(cores)])  2.7 us
    ppermute x2, starting transfers between devices, to_first(): return lax.ppermute(piece, ('chan', 'day'), pairs)  2.58 us
  transfers between devices with their start and end apart: 21, of which 8 were waited for; matrix products, arithmetic and copies ran while one was open for 0% of the time, Pallas kernels for 31%

profile of v6, /device:TPU:0, one launch (start us, length us, event | category | flops | bytes accessed | tf_op | source)
XLA Modules:
  0.0 40.9 jit_solution(8817717469256379734)
XLA Ops:
  0.0 1.1 %copy-done.1 = bf16[1,8,32,2,512]{4,3,2,1,0:T(2,128)(2,1)S(1)} copy-done((bf16[1,8,32,2,512]{4,3,2,1,0:T(2,128)(2,1)S(1)}, bf16[1,8,32,2,512]{4,3,2,1,0:T(2,128)(2,1)}, u32[]{:S(2)}) %copy-start.1) | copy-done | bytes 524312
  1.2 5.1 %collective-permute-start.3 = (bf16[2,8,16,512]{3,2,1,0:T(8,128)(2,1)S(1)}, bf16[2,8,16,512]{3,2,1,0:T(8,128)(2,1)S(1)}, u32[]{:S(2)}, u32[]{:S(2)}) collective-permute-start(bf16[2,8,16,512]{3,2,1,0:T(8,128)(2,1)S(1)} %bitcast.20), channel_id=1, source_target_pairs={{4,0},{8,4},{12,8},{0,12},{5,1},{9,5},{13,9},{1,13},{6,2},{10,6},{... | collective-permute-start | bytes 786440 | tf_op jit(solution)/shard_map/ppermute | solution.py:575
  6.3 0.5 %collective-permute-start.2 = (bf16[2,8,16,512]{3,2,1,0:T(8,128)(2,1)S(1)}, bf16[2,8,16,512]{3,2,1,0:T(8,128)(2,1)S(1)}, u32[]{:S(2)}, u32[]{:S(2)}) collective-permute-start(bf16[2,8,16,512]{3,2,1,0:T(8,128)(2,1)S(1)} %bitcast.18), channel_id=1, source_target_pairs={{4,0},{8,4},{12,8},{0,12},{5,1},{9,5},{13,9},{1,13},{6,2},{10,6},{... | collective-permute-start | bytes 786440 | tf_op jit(solution)/shard_map/ppermute | solution.py:575
  6.9 6.0 %shard_map.47 = (f32[2,256,256]{2,1,0:T(8,128)S(1)}, bf16[1,128,256]{2,1,0:T(8,128)(2,1)S(1)}, bf16[1,128,256]{2,1,0:T(8,128)(2,1)S(1)}, bf16[1,128,256]{2,1,0:T...) custom-call(s32[1,10]{1,0:T(1,128)S(1)} %bitcast.22, bf16[1024,256]{1,0:T(8,128)(2,1)S(1)} %copy-done, ...), custom_call_target="tpu_custom_call" | custom-call | tf_op jit(solution)/shard_map/pallas_call | solution.py:326
  13.0 1.3 %collective-permute-start.13 = (bf16[2,8,16,512]{3,2,1,0:T(8,128)(2,1)S(1)}, bf16[2,8,16,512]{3,2,1,0:T(8,128)(2,1)S(1)}, u32[]{:S(2)}, u32[]{:S(2)}) collective-permute-start(bf16[2,8,16,512]{3,2,1,0:T(8,128)(2,1)S(1)} %collective-permute-done.3.part), channel_id=1, source_target_pairs={{4,0},{8,4},{5,1},{9,5},{6,2},{10,6},{7,3},{11,7},{20,16},{24,20},... | collective-permute-start | bytes 786440 | tf_op jit(solution)/shard_map/ppermute | solution.py:593
  14.3 2.8 %shard_map.48 = (f32[2,128,256]{2,1,0:T(8,128)S(1)}, bf16[2,128,256]{2,1,0:T(8,128)(2,1)S(1)}) custom-call(s32[1,10]{1,0:T(1,128)S(1)} %bitcast.23, f32[3,8,32,512]{3,2,1,0:T(8,128)S(1)} %get-tuple-element.34.own_rows, bf16[1024,256]{1,0:T(8,128)(2,1)S(1)} %copy-done, bf16[2,8,16,512]{3,2,1,0:T(8,128)(2,1)S(1)} %collective-permute-done.3.part), custom_call_target="tpu_custom_call" | custom-call | tf_op jit(solution)/shard_map/pallas_call | solution.py:376
  17.2 0.3 collective-permute-done.2.part
  17.5 1.3 %collective-permute-start.14 = (bf16[2,8,16,512]{3,2,1,0:T(8,128)(2,1)S(1)}, bf16[2,8,16,512]{3,2,1,0:T(8,128)(2,1)S(1)}, u32[]{:S(2)}, u32[]{:S(2)}) collective-permute-start(bf16[2,8,16,512]{3,2,1,0:T(8,128)(2,1)S(1)} %collective-permute-done.2.part), channel_id=1, source_target_pairs={{4,0},{8,4},{5,1},{9,5},{6,2},{10,6},{7,3},{11,7},{20,16},{24,20},... | collective-permute-start | bytes 786440 | tf_op jit(solution)/shard_map/ppermute | solution.py:593
  18.9 0.5 %collective-permute-start.7 = (bf16[1,128,256]{2,1,0:T(8,128)(2,1)S(1)}, bf16[1,128,256]{2,1,0:T(8,128)(2,1)S(1)}, u32[]{:S(2)}, u32[]{:S(2)}) collective-permute-start(bf16[1,128,256]{2,1,0:T(8,128)(2,1)S(1)} %get-tuple-element.41), channel_id=1, source_target_pairs={{0,1},{1,0},{2,3},{3,2},{4,5},{5,4},{6,7},{7,6},{8,9},{9,8},{10,11... | collective-permute-start | bytes 196616 | tf_op jit(solution)/shard_map/ppermute | solution.py:557
  19.4 2.9 %shard_map.49 = (f32[2,256,256]{2,1,0:T(8,128)S(1)}, bf16[1,128,256]{2,1,0:T(8,128)(2,1)S(1)}, bf16[1,128,256]{2,1,0:T(8,128)(2,1)S(1)}, bf16[1,128,256]{2,1,0:T(8,128)(2,1)S(1)}, bf16[1,128,256]{2,1,0:T(8,128)(2,1)S(1)}) custom-call(s32[1,10]{1,0:T(1,128)S(1)} %bitcast.24, f32[3,8,32,512]{3,2,1,0:T(8,128)S(1)} %get-tuple-element.34.own_rows, ...), custom_call_target="tpu_custom_call" | custom-call | tf_op jit(solution)/shard_map/pallas_call | solution.py:391
  22.3 0.1 collective-permute-start.4
  22.4 0.4 %collective-permute-start.5 = (bf16[1,128,256]{2,1,0:T(8,128)(2,1)S(1)}, bf16[1,128,256]{2,1,0:T(8,128)(2,1)S(1)}, u32[]{:S(2)}, u32[]{:S(2)}) collective-permute-start(bf16[1,128,256]{2,1,0:T(8,128)(2,1)S(1)} %get-tuple-element.39), channel_id=1, source_target_pairs={{0,1},{1,0},{2,3},{3,2},{4,5},{5,4},{6,7},{7,6},{8,9},{9,8},{10,11... | collective-permute-start | bytes 196616 | tf_op jit(solution)/shard_map/ppermute | solution.py:557
  22.9 0.7 %collective-permute-done.4.refs_1_ = bf16[1,128,256]{2,1,0:T(8,128)(2,1)S(1)} collective-permute-done((bf16[1,128,256]{2,1,0:T(8,128)(2,1)S(1)}, bf16[1,128,256]{2,1,0:T(8,128)(2,1)S(1)}, u32[]{:S(2)}, u32[]{:S(2)}) %collective-permute-start.4) | collective-permute-done | bytes 65568 | tf_op jit(solution)/shard_map/ppermute | solution.py:557
  23.6 0.2 collective-permute-start.10
  23.8 1.6 %collective-permute-start.8 = (bf16[2,256,256]{2,1,0:T(8,128)(2,1)S(1)}, bf16[2,256,256]{2,1,0:T(8,128)(2,1)S(1)}, u32[]{:S(2)}, u32[]{:S(2)}) collective-permute-start(bf16[2,256,256]{2,1,0:T(8,128)(2,1)S(1)} %shard_map.50.refs_2_), channel_id=1, source_target_pairs={{0,2},{2,0},{1,3},{3,1},{4,6},{6,4},{5,7},{7,5},{8,10},{10,8},{9,1... | collective-permute-start | bytes 786440 | tf_op jit(solution)/shard_map/ppermute | solution.py:562
  25.4 1.3 %collective-permute-start.11 = (bf16[1,256,256]{2,1,0:T(8,128)(2,1)S(1)}, bf16[1,256,256]{2,1,0:T(8,128)(2,1)S(1)}, u32[]{:S(2)}, u32[]{:S(2)}) collective-permute-start(bf16[1,256,256]{2,1,0:T(8,128)(2,1)S(1)} %shard_map.53), channel_id=1, source_target_pairs={{12,0},{14,2},{13,1},{15,3},{28,16},{30,18},{29,17},{31,19}} | collective-permute-start | bytes 393224 | tf_op jit(solution)/shard_map/ppermute | solution.py:568
  26.7 1.3 %collective-permute-start.12 = (bf16[1,256,256]{2,1,0:T(8,128)(2,1)S(1)}, bf16[1,256,256]{2,1,0:T(8,128)(2,1)S(1)}, u32[]{:S(2)}, u32[]{:S(2)}) collective-permute-start(bf16[1,256,256]{2,1,0:T(8,128)(2,1)S(1)} %shard_map.54), channel_id=1, source_target_pairs={{12,2},{14,0},{13,3},{15,1},{28,18},{30,16},{29,19},{31,17}} | collective-permute-start | bytes 393224 | tf_op jit(solution)/shard_map/ppermute | solution.py:568
  28.1 0.1 shard_map.56
  28.2 0.1 collective-permute-start.17
  28.3 0.4 %collective-permute-start.18 = (bf16[1,128,256]{2,1,0:T(8,128)(2,1)S(1)}, bf16[1,128,256]{2,1,0:T(8,128)(2,1)S(1)}, u32[]{:S(2)}, u32[]{:S(2)}) collective-permute-start(bf16[1,128,256]{2,1,0:T(8,128)(2,1)S(1)} %get-tuple-element.52), channel_id=1, source_target_pairs={{0,1},{1,0},{2,3},{3,2},{4,5},{5,4},{6,7},{7,6},{8,9},{9,8},{10,11... | collective-permute-start | bytes 196616 | tf_op jit(solution)/shard_map/ppermute | solution.py:557
  28.8 0.7 %collective-permute-done.17.refs_1_ = bf16[1,128,256]{2,1,0:T(8,128)(2,1)S(1)} collective-permute-done((bf16[1,128,256]{2,1,0:T(8,128)(2,1)S(1)}, bf16[1,128,256]{2,1,0:T(8,128)(2,1)S(1)}, u32[]{:S(2)}, u32[]{:S(2)}) %collective-permute-start.17) | collective-permute-done | bytes 65568 | tf_op jit(solution)/shard_map/ppermute | solution.py:557
  29.5 0.2 collective-permute-start
  29.7 1.5 %collective-permute-start.19 = (bf16[1,256,256]{2,1,0:T(8,128)(2,1)S(1)}, bf16[1,256,256]{2,1,0:T(8,128)(2,1)S(1)}, u32[]{:S(2)}, u32[]{:S(2)}) collective-permute-start(bf16[1,256,256]{2,1,0:T(8,128)(2,1)S(1)} %shard_map.58), channel_id=1, source_target_pairs={{0,2},{2,0},{1,3},{3,1},{4,6},{6,4},{5,7},{7,5},{8,10},{10,8},{9,1... | collective-permute-start | bytes 393224 | tf_op jit(solution)/shard_map/ppermute | solution.py:562
  31.3 4.2 %collective-permute-done.11.refs_0_ = bf16[1,256,256]{2,1,0:T(8,128)(2,1)S(1)} collective-permute-done((bf16[1,256,256]{2,1,0:T(8,128)(2,1)S(1)}, bf16[1,256,256]{2,1,0:T(8,128)(2,1)S(1)}, u32[]{:S(2)}, u32[]{:S(2)}) %collective-permute-start.11) | collective-permute-done | bytes 131104 | tf_op jit(solution)/shard_map/ppermute | solution.py:568
  35.4 2.5 %collective-permute-done.12.refs_1_ = bf16[1,256,256]{2,1,0:T(8,128)(2,1)S(1)} collective-permute-done((bf16[1,256,256]{2,1,0:T(8,128)(2,1)S(1)}, bf16[1,256,256]{2,1,0:T(8,128)(2,1)S(1)}, u32[]{:S(2)}, u32[]{:S(2)}) %collective-permute-start.12) | collective-permute-done | bytes 131104 | tf_op jit(solution)/shard_map/ppermute | solution.py:568
  38.0 0.2 shard_map.55.refs_2_
  38.2 0.5 %collective-permute-start.1 = (bf16[1,128,256]{2,1,0:T(8,128)(2,1)S(1)}, bf16[1,128,256]{2,1,0:T(8,128)(2,1)S(1)}, u32[]{:S(2)}, u32[]{:S(2)}) collective-permute-start(bf16[1,128,256]{2,1,0:T(8,128)(2,1)S(1)} %get-tuple-element.33), channel_id=1, source_target_pairs={{0,1},{1,0},{2,3},{3,2},{4,5},{5,4},{6,7},{7,6},{8,9},{9,8},{10,11... | collective-permute-start | bytes 196616 | tf_op jit(solution)/shard_map/ppermute | solution.py:557
  38.8 0.2 shard_map.52.refs_1_
  39.0 0.6 %collective-permute-done.1.refs_2_ = bf16[1,128,256]{2,1,0:T(8,128)(2,1)S(1)} collective-permute-done((bf16[1,128,256]{2,1,0:T(8,128)(2,1)S(1)}, bf16[1,128,256]{2,1,0:T(8,128)(2,1)S(1)}, u32[]{:S(2)}, u32[]{:S(2)}) %collective-permute-start.1) | collective-permute-done | bytes 65568 | tf_op jit(solution)/shard_map/ppermute | solution.py:557
  39.6 0.2 shard_map.51.refs_0_
  39.8 0.1 collective-permute-done.16.refs_5_
  39.9 1.0 %shard_map.59 = f32[3,8,32,256]{3,2,1,0:T(8,128)} custom-call(s32[1,10]{1,0:T(1,128)S(1)} %bitcast.30, f32[8,32,256]{2,1,0:T(8,128)S(1)} %shard_map.51.refs_0_, f32[8,32,256]{2,1,0:T(8,128)S(1)} %shard_map.52.refs_1_, f32[8,32,256]{2,1,0:T(8,128)S(1)} %shard_map.55.refs_2_, f32[1,256,256]{2,1,0:T(8,128)S(1)} %get-tuple-element.47.refs_3_, ...), custom_call_target="tpu_custom_call" | custom-call | tf_op jit(solution)/shard_map/pallas_call | solution.py:521
  (36 shorter events, 0.9 us)
Async XLA Ops:
  0.0 6.9 %copy-start = (bf16[1024,256]{1,0:T(8,128)(2,1)S(1)}, bf16[1024,256]{1,0:T(8,128)(2,1)}, u32[]{:S(2)}) copy-start(bf16[1024,256]{1,0:T(8,128)(2,1)} %constant.17.clone.table) | copy-start | bytes 1572868
  0.0 1.1 %copy-start.1 = (bf16[1,8,32,2,512]{4,3,2,1,0:T(2,128)(2,1)S(1)}, bf16[1,8,32,2,512]{4,3,2,1,0:T(2,128)(2,1)}, u32[]{:S(2)}) copy-start(bf16[1,8,32,2,512]{4,3,2,1,0:T(2,128)(2,1)} %source.1) | copy-start | bytes 1572868
  1.1 5.8 %copy-start.2 = (s32[1,3]{1,0:T(1,128)S(1)}, s32[1,3]{1,0:T(1,128)}, u32[]{:S(2)}) copy-start(s32[1,3]{1,0:T(1,128)} %param.5) | copy-start | bytes 40
  1.1 5.8 %copy-start.3 = (s32[1,3]{1,0:T(1,128)S(1)}, s32[1,3]{1,0:T(1,128)}, u32[]{:S(2)}) copy-start(s32[1,3]{1,0:T(1,128)} %param.6) | copy-start | bytes 40
  1.2 11.8 %collective-permute-start.3 = (bf16[2,8,16,512]{3,2,1,0:T(8,128)(2,1)S(1)}, bf16[2,8,16,512]{3,2,1,0:T(8,128)(2,1)S(1)}, u32[]{:S(2)}, u32[]{:S(2)}) collective-permute-start(bf16[2,8,16,512]{3,2,1,0:T(8,128)(2,1)S(1)} %bitcast.20), channel_id=1, source_target_pairs={{4,0},{8,4},{12,8},{0,12},{5,1},{9,5},{13,9},{1,13},{6,2},{10,6},{... | collective-permute-start | bytes 786440 | tf_op jit(solution)/shard_map/ppermute | solution.py:575
  6.3 11.1 %collective-permute-start.2 = (bf16[2,8,16,512]{3,2,1,0:T(8,128)(2,1)S(1)}, bf16[2,8,16,512]{3,2,1,0:T(8,128)(2,1)S(1)}, u32[]{:S(2)}, u32[]{:S(2)}) collective-permute-start(bf16[2,8,16,512]{3,2,1,0:T(8,128)(2,1)S(1)} %bitcast.18), channel_id=1, source_target_pairs={{4,0},{8,4},{12,8},{0,12},{5,1},{9,5},{13,9},{1,13},{6,2},{10,6},{... | collective-permute-start | bytes 786440 | tf_op jit(solution)/shard_map/ppermute | solution.py:575
  13.0 15.0 %collective-permute-start.13 = (bf16[2,8,16,512]{3,2,1,0:T(8,128)(2,1)S(1)}, bf16[2,8,16,512]{3,2,1,0:T(8,128)(2,1)S(1)}, u32[]{:S(2)}, u32[]{:S(2)}) collective-permute-start(bf16[2,8,16,512]{3,2,1,0:T(8,128)(2,1)S(1)} %collective-permute-done.3.part), channel_id=1, source_target_pairs={{4,0},{8,4},{5,1},{9,5},{6,2},{10,6},{7,3},{11,7},{20,16},{24,20},... | collective-permute-start | bytes 786440 | tf_op jit(solution)/shard_map/ppermute | solution.py:593
  17.5 10.5 %collective-permute-start.14 = (bf16[2,8,16,512]{3,2,1,0:T(8,128)(2,1)S(1)}, bf16[2,8,16,512]{3,2,1,0:T(8,128)(2,1)S(1)}, u32[]{:S(2)}, u32[]{:S(2)}) collective-permute-start(bf16[2,8,16,512]{3,2,1,0:T(8,128)(2,1)S(1)} %collective-permute-done.2.part), channel_id=1, source_target_pairs={{4,0},{8,4},{5,1},{9,5},{6,2},{10,6},{7,3},{11,7},{20,16},{24,20},... | collective-permute-start | bytes 786440 | tf_op jit(solution)/shard_map/ppermute | solution.py:593
  18.8 3.6 %collective-permute-start.6 = (bf16[1,128,256]{2,1,0:T(8,128)(2,1)S(1)}, bf16[1,128,256]{2,1,0:T(8,128)(2,1)S(1)}, u32[]{:S(2)}, u32[]{:S(2)}) collective-permute-start(bf16[1,128,256]{2,1,0:T(8,128)(2,1)S(1)} %get-tuple-element.40), channel_id=1, source_target_pairs={{0,1},{1,0},{2,3},{3,2},{4,5},{5,4},{6,7},{7,6},{8,9},{9,8},{10,11... | collective-permute-start | bytes 196616 | tf_op jit(solution)/shard_map/ppermute | solution.py:557
  18.9 4.0 %collective-permute-start.7 = (bf16[1,128,256]{2,1,0:T(8,128)(2,1)S(1)}, bf16[1,128,256]{2,1,0:T(8,128)(2,1)S(1)}, u32[]{:S(2)}, u32[]{:S(2)}) collective-permute-start(bf16[1,128,256]{2,1,0:T(8,128)(2,1)S(1)} %get-tuple-element.41), channel_id=1, source_target_pairs={{0,1},{1,0},{2,3},{3,2},{4,5},{5,4},{6,7},{7,6},{8,9},{9,8},{10,11... | collective-permute-start | bytes 196616 | tf_op jit(solution)/shard_map/ppermute | solution.py:557
  22.3 1.3 %collective-permute-start.4 = (bf16[1,128,256]{2,1,0:T(8,128)(2,1)S(1)}, bf16[1,128,256]{2,1,0:T(8,128)(2,1)S(1)}, u32[]{:S(2)}, u32[]{:S(2)}) collective-permute-start(bf16[1,128,256]{2,1,0:T(8,128)(2,1)S(1)} %get-tuple-element.38), channel_id=1, source_target_pairs={{0,1},{1,0},{2,3},{3,2},{4,5},{5,4},{6,7},{7,6},{8,9},{9,8},{10,11... | collective-permute-start | bytes 196616 | tf_op jit(solution)/shard_map/ppermute | solution.py:557
  22.4 1.3 %collective-permute-start.5 = (bf16[1,128,256]{2,1,0:T(8,128)(2,1)S(1)}, bf16[1,128,256]{2,1,0:T(8,128)(2,1)S(1)}, u32[]{:S(2)}, u32[]{:S(2)}) collective-permute-start(bf16[1,128,256]{2,1,0:T(8,128)(2,1)S(1)} %get-tuple-element.39), channel_id=1, source_target_pairs={{0,1},{1,0},{2,3},{3,2},{4,5},{5,4},{6,7},{7,6},{8,9},{9,8},{10,11... | collective-permute-start | bytes 196616 | tf_op jit(solution)/shard_map/ppermute | solution.py:557
  22.8 2.5 %collective-permute-start.9 = (bf16[1,128,256]{2,1,0:T(8,128)(2,1)S(1)}, bf16[1,128,256]{2,1,0:T(8,128)(2,1)S(1)}, u32[]{:S(2)}, u32[]{:S(2)}) collective-permute-start(bf16[1,128,256]{2,1,0:T(8,128)(2,1)S(1)} %get-tuple-element.42), channel_id=1, source_target_pairs={{0,1},{1,0},{2,3},{3,2},{4,5},{5,4},{6,7},{7,6},{8,9},{9,8},{10,11... | collective-permute-start | bytes 196616 | tf_op jit(solution)/shard_map/ppermute | solution.py:557
  23.6 1.8 %collective-permute-start.10 = (bf16[1,128,256]{2,1,0:T(8,128)(2,1)S(1)}, bf16[1,128,256]{2,1,0:T(8,128)(2,1)S(1)}, u32[]{:S(2)}, u32[]{:S(2)}) collective-permute-start(bf16[1,128,256]{2,1,0:T(8,128)(2,1)S(1)} %get-tuple-element.43), channel_id=1, source_target_pairs={{0,1},{1,0},{2,3},{3,2},{4,5},{5,4},{6,7},{7,6},{8,9},{9,8},{10,11... | collective-permute-start | bytes 196616 | tf_op jit(solution)/shard_map/ppermute | solution.py:557
  23.8 14.9 %collective-permute-start.8 = (bf16[2,256,256]{2,1,0:T(8,128)(2,1)S(1)}, bf16[2,256,256]{2,1,0:T(8,128)(2,1)S(1)}, u32[]{:S(2)}, u32[]{:S(2)}) collective-permute-start(bf16[2,256,256]{2,1,0:T(8,128)(2,1)S(1)} %shard_map.50.refs_2_), channel_id=1, source_target_pairs={{0,2},{2,0},{1,3},{3,1},{4,6},{6,4},{5,7},{7,5},{8,10},{10,8},{9,1... | collective-permute-start | bytes 786440 | tf_op jit(solution)/shard_map/ppermute | solution.py:562
  25.4 10.0 %collective-permute-start.11 = (bf16[1,256,256]{2,1,0:T(8,128)(2,1)S(1)}, bf16[1,256,256]{2,1,0:T(8,128)(2,1)S(1)}, u32[]{:S(2)}, u32[]{:S(2)}) collective-permute-start(bf16[1,256,256]{2,1,0:T(8,128)(2,1)S(1)} %shard_map.53), channel_id=1, source_target_pairs={{12,0},{14,2},{13,1},{15,3},{28,16},{30,18},{29,17},{31,19}} | collective-permute-start | bytes 393224 | tf_op jit(solution)/shard_map/ppermute | solution.py:568
  26.7 11.2 %collective-permute-start.12 = (bf16[1,256,256]{2,1,0:T(8,128)(2,1)S(1)}, bf16[1,256,256]{2,1,0:T(8,128)(2,1)S(1)}, u32[]{:S(2)}, u32[]{:S(2)}) collective-permute-start(bf16[1,256,256]{2,1,0:T(8,128)(2,1)S(1)} %shard_map.54), channel_id=1, source_target_pairs={{12,2},{14,0},{13,3},{15,1},{28,18},{30,16},{29,19},{31,17}} | collective-permute-start | bytes 393224 | tf_op jit(solution)/shard_map/ppermute | solution.py:568
  28.2 1.3 %collective-permute-start.17 = (bf16[1,128,256]{2,1,0:T(8,128)(2,1)S(1)}, bf16[1,128,256]{2,1,0:T(8,128)(2,1)S(1)}, u32[]{:S(2)}, u32[]{:S(2)}) collective-permute-start(bf16[1,128,256]{2,1,0:T(8,128)(2,1)S(1)} %get-tuple-element.51), channel_id=1, source_target_pairs={{0,1},{1,0},{2,3},{3,2},{4,5},{5,4},{6,7},{7,6},{8,9},{9,8},{10,11... | collective-permute-start | bytes 196616 | tf_op jit(solution)/shard_map/ppermute | solution.py:557
  28.3 1.3 %collective-permute-start.18 = (bf16[1,128,256]{2,1,0:T(8,128)(2,1)S(1)}, bf16[1,128,256]{2,1,0:T(8,128)(2,1)S(1)}, u32[]{:S(2)}, u32[]{:S(2)}) collective-permute-start(bf16[1,128,256]{2,1,0:T(8,128)(2,1)S(1)} %get-tuple-element.52), channel_id=1, source_target_pairs={{0,1},{1,0},{2,3},{3,2},{4,5},{5,4},{6,7},{7,6},{8,9},{9,8},{10,11... | collective-permute-start | bytes 196616 | tf_op jit(solution)/shard_map/ppermute | solution.py:557
  29.5 8.7 %collective-permute-start = (bf16[1,128,256]{2,1,0:T(8,128)(2,1)S(1)}, bf16[1,128,256]{2,1,0:T(8,128)(2,1)S(1)}, u32[]{:S(2)}, u32[]{:S(2)}) collective-permute-start(bf16[1,128,256]{2,1,0:T(8,128)(2,1)S(1)} %get-tuple-element.32), channel_id=1, source_target_pairs={{0,1},{1,0},{2,3},{3,2},{4,5},{5,4},{6,7},{7,6},{8,9},{9,8},{10,11... | collective-permute-start | bytes 196616 | tf_op jit(solution)/shard_map/ppermute | solution.py:557
  29.7 10.2 %collective-permute-start.19 = (bf16[1,256,256]{2,1,0:T(8,128)(2,1)S(1)}, bf16[1,256,256]{2,1,0:T(8,128)(2,1)S(1)}, u32[]{:S(2)}, u32[]{:S(2)}) collective-permute-start(bf16[1,256,256]{2,1,0:T(8,128)(2,1)S(1)} %shard_map.58), channel_id=1, source_target_pairs={{0,2},{2,0},{1,3},{3,1},{4,6},{6,4},{5,7},{7,5},{8,10},{10,8},{9,1... | collective-permute-start | bytes 393224 | tf_op jit(solution)/shard_map/ppermute | solution.py:562
  35.4 4.5 %collective-permute-start.15 = (bf16[1,192,256]{2,1,0:T(8,128)(2,1)S(1)}, bf16[1,192,256]{2,1,0:T(8,128)(2,1)S(1)}, u32[]{:S(2)}, u32[]{:S(2)}) collective-permute-start(bf16[1,192,256]{2,1,0:T(8,128)(2,1)S(1)} %get-tuple-element.48), channel_id=1, source_target_pairs={{0,1},{1,0},{2,3},{3,2},{4,5},{5,4},{6,7},{7,6},{8,9},{9,8},{10,11... | collective-permute-start | bytes 294920 | tf_op jit(solution)/shard_map/ppermute | solution.py:557
  38.1 1.6 %collective-permute-start.20 = (f32[3,24,256]{2,1,0:T(8,128)S(1)}, f32[3,24,256]{2,1,0:T(8,128)S(1)}, u32[]{:S(2)}, u32[]{:S(2)}) collective-permute-start(f32[3,24,256]{2,1,0:T(8,128)S(1)} %slice.4), channel_id=1, source_target_pairs={{0,1},{1,0},{2,3},{3,2},{4,5},{5,4},{6,7},{7,6},{8,9},{9,8},{10,11... | collective-permute-start | bytes 221192 | tf_op jit(solution)/shard_map/ppermute | solution.py:614
  38.2 1.4 %collective-permute-start.1 = (bf16[1,128,256]{2,1,0:T(8,128)(2,1)S(1)}, bf16[1,128,256]{2,1,0:T(8,128)(2,1)S(1)}, u32[]{:S(2)}, u32[]{:S(2)}) collective-permute-start(bf16[1,128,256]{2,1,0:T(8,128)(2,1)S(1)} %get-tuple-element.33), channel_id=1, source_target_pairs={{0,1},{1,0},{2,3},{3,2},{4,5},{5,4},{6,7},{7,6},{8,9},{9,8},{10,11... | collective-permute-start | bytes 196616 | tf_op jit(solution)/shard_map/ppermute | solution.py:557
  38.7 1.2 %collective-permute-start.16 = (bf16[1,64,256]{2,1,0:T(8,128)(2,1)S(1)}, bf16[1,64,256]{2,1,0:T(8,128)(2,1)S(1)}, u32[]{:S(2)}, u32[]{:S(2)}) collective-permute-start(bf16[1,64,256]{2,1,0:T(8,128)(2,1)S(1)} %get-tuple-element.49), channel_id=1, source_target_pairs={{0,1},{1,0},{2,3},{3,2},{4,5},{5,4},{6,7},{7,6},{8,9},{9,8},{10,11... | collective-permute-start | bytes 98312 | tf_op jit(solution)/shard_map/ppermute | solution.py:557

commit v7 on v6

--- a/solution.py
+++ b/solution.py
@@ -165,7 +165,8 @@
 
 def own_kernel(part_count, scalars, table, *refs):
     parts = refs[:part_count]
-    keep, *sends, rows, cols, cross = refs[part_count:]
+    keep, send, rows, cols, cross = refs[part_count:]
+    sends = [send.at[pl.ds(k, 1)] for k in range(send.shape[0])]
     for part, begin in zip(parts, begins_of(parts)):
         for lanes, real, imag in whiten(part):
             for k in range(3):
@@ -323,11 +324,13 @@
     _, windows, _, bins = parts[0].shape
     width = sum(part.shape[2] for part in parts)
     factors = (3, windows, width, bins)
-    keep, *sends, rows = pl.pallas_call(
+    keep_shape, *send_shapes = sums_shapes(owners, width)
+    sent = jax.ShapeDtypeStruct((len(send_shapes),) + send_shapes[0].shape[1:], send_shapes[0].dtype)
+    keep, send, rows = pl.pallas_call(
         functools.partial(own_kernel, len(parts)),
-        out_shape=sums_shapes(owners, width) + [jax.ShapeDtypeStruct(factors, jnp.float32)],
+        out_shape=[keep_shape, sent, jax.ShapeDtypeStruct(factors, jnp.float32)],
         in_specs=[VMEM] + [VMEM] * (1 + len(parts)),
-        out_specs=[VMEM] * (owners * HALVES + 2),
+        out_specs=[VMEM] * 3,
         scratch_shapes=[
             pltpu.VMEM(factors, jnp.float32),
             pltpu.VMEM((width * width, 2 * bins), jnp.bfloat16),
@@ -335,7 +338,7 @@
         compiler_params=PARAMS,
         cost_estimate=FREE,
     )(scalars, table, *parts)
-    return keep, sends, rows
+    return keep, [send], rows
 
 
 def days_tile(scalars, own_rows, table, owners, step, shifts, splits, parts=(), cols=None, after=()):
@@ -402,18 +405,19 @@
 
 def add_kernel(tiles, shift, *refs):
     out = refs[-1]
-    for tile in range(tiles):
+    for tile, places in enumerate(tiles):
         keep, *got = refs[tile * (1 + HALVES) : (tile + 1) * (1 + HALVES)]
-        for half, sent in enumerate(got):
+        for half, (sent, at) in enumerate(zip(got, places)):
             place = pl.ds(half * sent.shape[1], sent.shape[1])
-            out[tile, place] = (keep[shift, place] + sent[0].astype(jnp.float32)).astype(out.dtype)
+            out[tile, place] = (keep[shift, place] + sent[at].astype(jnp.float32)).astype(out.dtype)
 
 
 def add_cores(tiles, shift, after=()):
-    operands = [term for keep, got in tiles for term in [keep] + got[shift]]
+    operands = [term for keep, got in tiles for term in [keep] + [array for array, _ in got[shift]]]
+    places = [[at for _, at in got[shift]] for _, got in tiles]
     rows = tiles[0][0].shape[1]
     return pl.pallas_call(
-        functools.partial(add_kernel, len(tiles), shift),
+        functools.partial(add_kernel, places, shift),
         out_shape=jax.ShapeDtypeStruct((len(tiles), rows, LAGS), jnp.bfloat16),
         in_specs=[VMEM] * len(operands) + [ANY] * len(after),
         out_specs=VMEM,
@@ -432,7 +436,7 @@
         value = None
         for term in terms:
             if isinstance(term, list):
-                whole = jnp.concatenate([part[0].astype(jnp.float32) for part in term], axis=0)
+                whole = jnp.concatenate([array[at].astype(jnp.float32) for array, at in term], axis=0)
                 part = whole[half * size : (half + 1) * size]
             else:
                 array, at = term
@@ -447,13 +451,13 @@
         tile[:, pl.ds(half * half_width, half_width), :] = jnp.where(kept, value * norm_scale, 0.0)
 
 
-def grouped(refs, counts):
+def grouped(refs, places):
     terms = []
-    for at, count in counts:
-        if at is not None:
-            terms.append((refs.pop(0), at))
+    for place in places:
+        if isinstance(place, list):
+            terms.append([(refs.pop(0), at) for at in place])
         else:
-            terms.append([refs.pop(0) for _ in range(count)])
+            terms.append((refs.pop(0), place))
     return terms
 
 
@@ -463,12 +467,12 @@
 
 
 def flat(terms):
-    operands, counts = [], []
+    operands, places = [], []
     for term in terms:
         listed = isinstance(term, list)
-        operands += term if listed else [term[0]]
-        counts.append((None, len(term)) if listed else (term[1], 1))
-    return operands, counts
+        operands += [array for array, _ in term] if listed else [term[0]]
+        places.append([at for _, at in term] if listed else term[1])
+    return operands, places
 
 
 def finished_tile(scalars, step, terms, row_count, width, norm_scale):
@@ -555,6 +559,7 @@
 
     def over_cores(sends):
         got = [lax.ppermute(send, "sub", [(k, (k + 1) % cores) for k in range(cores)]) for send in sends]
+        got = [(array, at) for array in got for at in range(array.shape[0])]
         return [got[k : k + HALVES] for k in range(0, len(got), HALVES)]
 
     def over_days(pieces):
@@ -604,7 +609,7 @@
             block = {"cols": cols}
         splits = (rows * 3 // 4, rows // 4)
         keep, sends2, _ = days_tile(scalars, own_rows, table, days, step, [0], splits, **block)
-        got = [array for arrays in over_cores(sends2) for array in arrays]
+        got = [part for parts in over_cores(sends2) for part in parts]
         late.append((step, [(keep, 0), got] + [(piece, 0) for piece in arrived]))
     if wraps:
         terms = [(piece, 0) for piece in back]

time: 41 us -> 40.4 us (0.985)
  Pallas kernels: 13.6 us -> 10.5 us
  waiting for transfers between devices: 9.32 us -> 12.4 us
  starting transfers between devices: 16.5 us -> 16 us
    ppermute x2, waiting for transfers between devices: 0.01 us -> 3.52 us  [on_device(): lax.ppermute(lax.optimization_barrier((part, wait))[0], 'chan', pairs)]
    ppermute x2, waiting for transfers between devices: 6.67 us -> 4.41 us  [to_first(): return lax.ppermute(piece, ('chan', 'day'), pairs)]
    pallas_call x1, Pallas kernels: 2.9 us -> 1.13 us  [second_half_tile(): pl.pallas_call(functools.partial(second_half_kernel, can_swap, step, len(...]
    pallas_call x1, Pallas kernels: 2.85 us -> 1.52 us  [first_half_tile(): pl.pallas_call(functools.partial(first_half_kernel, can_swap, step), out_...]
    ppermute x2, waiting for transfers between devices: 0.43 us -> 1.68 us  [on_device(): moving = [lax.ppermute(part, 'chan', pairs) for part in halves]]
    ppermute x2, waiting for transfers between devices: 0.01 us -> 0.71 us  [over_days(): lax.ppermute(piece, 'day', [(k, (k + shift) % days) for k in range(days)])]
    ppermute x12 -> x9, starting transfers between devices: 2.7 us -> 2.08 us  [over_cores(): lax.ppermute(send, 'sub', [(k, (k + 1) % cores) for k in range(cores)])]
    ppermute x12 -> x9, waiting for transfers between devices: 2.2 us -> 1.68 us  [over_cores(): lax.ppermute(send, 'sub', [(k, (k + 1) % cores) for k in range(cores)])]
  transfers between devices with their start and end apart: 21 -> 18, of which waited for: 8 -> 10; matrix products, arithmetic and copies ran while one was open for 0% -> 0% of each run, Pallas kernels for 31% -> 23%
where the time goes in v7:
time: 40.4 us
  starting transfers between devices  16 us (40%)
  waiting for transfers between devices  12.4 us (31%)
  Pallas kernels  10.5 us (26%)
  local copies, waits for them, and re-layouts  1.26 us (3%)
    pallas_call x1, Pallas kernels, own_tile(): pl.pallas_call(functools.partial(own_kernel, len(parts)), out_shape=[keep...  5.97 us
    ppermute x2, starting transfers between devices, on_device(): moving = [lax.ppermute(part, 'chan', pairs) for part in halves]  5.6 us
    ppermute x2, waiting for transfers between devices, to_first(): return lax.ppermute(piece, ('chan', 'day'), pairs)  4.41 us
    ppermute x2, waiting for transfers between devices, on_device(): lax.ppermute(lax.optimization_barrier((part, wait))[0], 'chan', pairs)  3.52 us
    ppermute x2, starting transfers between devices, over_days(): lax.ppermute(piece, 'day', [(k, (k + shift) % days) for k in range(days)])  3.11 us
    ppermute x2, starting transfers between devices, to_first(): return lax.ppermute(piece, ('chan', 'day'), pairs)  2.58 us
    ppermute x2, starting transfers between devices, on_device(): lax.ppermute(lax.optimization_barrier((part, wait))[0], 'chan', pairs)  2.56 us
    ppermute x9, starting transfers between devices, over_cores(): lax.ppermute(send, 'sub', [(k, (k + 1) % cores) for k in range(cores)])  2.08 us
  transfers between devices with their start and end apart: 18, of which 10 were waited for; matrix products, arithmetic and copies ran while one was open for 0% of the time, Pallas kernels for 23%

profile of v7, /device:TPU:0, one launch (start us, length us, event | category | flops | bytes accessed | tf_op | source)
XLA Modules:
  0.0 40.4 jit_solution(2177108527094467830)
XLA Ops:
  0.0 1.1 %copy-done.1 = bf16[1,8,32,2,512]{4,3,2,1,0:T(2,128)(2,1)S(1)} copy-done((bf16[1,8,32,2,512]{4,3,2,1,0:T(2,128)(2,1)S(1)}, bf16[1,8,32,2,512]{4,3,2,1,0:T(2,128)(2,1)}, u32[]{:S(2)}) %copy-start.1) | copy-done | bytes 524312
  1.2 5.1 %collective-permute-start.2 = (bf16[2,8,16,512]{3,2,1,0:T(8,128)(2,1)S(1)}, bf16[2,8,16,512]{3,2,1,0:T(8,128)(2,1)S(1)}, u32[]{:S(2)}, u32[]{:S(2)}) collective-permute-start(bf16[2,8,16,512]{3,2,1,0:T(8,128)(2,1)S(1)} %bitcast.20), channel_id=1, source_target_pairs={{4,0},{8,4},{12,8},{0,12},{5,1},{9,5},{13,9},{1,13},{6,2},{10,6},{... | collective-permute-start | bytes 786440 | tf_op jit(solution)/shard_map/ppermute | solution.py:580
  6.3 0.5 %collective-permute-start.1 = (bf16[2,8,16,512]{3,2,1,0:T(8,128)(2,1)S(1)}, bf16[2,8,16,512]{3,2,1,0:T(8,128)(2,1)S(1)}, u32[]{:S(2)}, u32[]{:S(2)}) collective-permute-start(bf16[2,8,16,512]{3,2,1,0:T(8,128)(2,1)S(1)} %bitcast.18), channel_id=1, source_target_pairs={{4,0},{8,4},{12,8},{0,12},{5,1},{9,5},{13,9},{1,13},{6,2},{10,6},{... | collective-permute-start | bytes 786440 | tf_op jit(solution)/shard_map/ppermute | solution.py:580
  6.9 6.0 %shard_map.47 = (f32[2,256,256]{2,1,0:T(8,128)S(1)}, bf16[4,128,256]{2,1,0:T(8,128)(2,1)S(1)}, f32[3,8,32,512]{3,2,1,0:T(8,128)S(1)}) custom-call(s32[1,10]{1,0:T(1,128)S(1)} %bitcast.22, bf16[1024,256]{1,0:T(8,128)(2,1)S(1)} %copy-done, bf16[2,8,16,512]{3,2,1,0:T(8,128)(2,1)S(1)} %bitcast.21, bf16[2,8,16,512]{3,2,1,0:T(8,128)(2,1)S(1)} %bitcast.19), custom_call_target="tpu_custom_call" | custom-call | tf_op jit(solution)/shard_map/pallas_call | solution.py:329
  13.0 1.3 %collective-permute-start.10 = (bf16[2,8,16,512]{3,2,1,0:T(8,128)(2,1)S(1)}, bf16[2,8,16,512]{3,2,1,0:T(8,128)(2,1)S(1)}, u32[]{:S(2)}, u32[]{:S(2)}) collective-permute-start(bf16[2,8,16,512]{3,2,1,0:T(8,128)(2,1)S(1)} %collective-permute-done.2.part), channel_id=1, source_target_pairs={{4,0},{8,4},{5,1},{9,5},{6,2},{10,6},{7,3},{11,7},{20,16},{24,20},... | collective-permute-start | bytes 786440 | tf_op jit(solution)/shard_map/ppermute | solution.py:598
  14.3 1.5 %shard_map.48 = (f32[2,128,256]{2,1,0:T(8,128)S(1)}, bf16[2,128,256]{2,1,0:T(8,128)(2,1)S(1)}) custom-call(s32[1,10]{1,0:T(1,128)S(1)} %bitcast.23, f32[3,8,32,512]{3,2,1,0:T(8,128)S(1)} %get-tuple-element.30.own_rows, bf16[1024,256]{1,0:T(8,128)(2,1)S(1)} %copy-done, bf16[2,8,16,512]{3,2,1,0:T(8,128)(2,1)S(1)} %collective-permute-done.2.part), custom_call_target="tpu_custom_call" | custom-call | tf_op jit(solution)/shard_map/pallas_call | solution.py:379
  15.8 1.7 %collective-permute-done.1.part = bf16[2,8,16,512]{3,2,1,0:T(8,128)(2,1)S(1)} collective-permute-done((bf16[2,8,16,512]{3,2,1,0:T(8,128)(2,1)S(1)}, bf16[2,8,16,512]{3,2,1,0:T(8,128)(2,1)S(1)}, u32[]{:S(2)}, u32[]{:S(2)}) %collective-permute-start.1) | collective-permute-done | bytes 262176 | tf_op jit(solution)/shard_map/ppermute | solution.py:580
  17.5 1.3 %collective-permute-start.11 = (bf16[2,8,16,512]{3,2,1,0:T(8,128)(2,1)S(1)}, bf16[2,8,16,512]{3,2,1,0:T(8,128)(2,1)S(1)}, u32[]{:S(2)}, u32[]{:S(2)}) collective-permute-start(bf16[2,8,16,512]{3,2,1,0:T(8,128)(2,1)S(1)} %collective-permute-done.1.part), channel_id=1, source_target_pairs={{4,0},{8,4},{5,1},{9,5},{6,2},{10,6},{7,3},{11,7},{20,16},{24,20},... | collective-permute-start | bytes 786440 | tf_op jit(solution)/shard_map/ppermute | solution.py:598
  18.8 1.1 %shard_map.49 = (f32[2,256,256]{2,1,0:T(8,128)S(1)}, bf16[1,128,256]{2,1,0:T(8,128)(2,1)S(1)}, bf16[1,128,256]{2,1,0:T(8,128)(2,1)S(1)}, bf16[1,128,256]{2,1,0:T(8,128)(2,1)S(1)}, bf16[1,128,256]{2,1,0:T(8,128)(2,1)S(1)}) custom-call(s32[1,10]{1,0:T(1,128)S(1)} %bitcast.24, f32[3,8,32,512]{3,2,1,0:T(8,128)S(1)} %get-tuple-element.30.own_rows, ...), custom_call_target="tpu_custom_call" | custom-call | tf_op jit(solution)/shard_map/pallas_call | solution.py:394
  20.0 0.5 %collective-permute-start.4 = (bf16[1,128,256]{2,1,0:T(8,128)(2,1)S(1)}, bf16[1,128,256]{2,1,0:T(8,128)(2,1)S(1)}, u32[]{:S(2)}, u32[]{:S(2)}) collective-permute-start(bf16[1,128,256]{2,1,0:T(8,128)(2,1)S(1)} %get-tuple-element.35), channel_id=1, source_target_pairs={{0,1},{1,0},{2,3},{3,2},{4,5},{5,4},{6,7},{7,6},{8,9},{9,8},{10,11... | collective-permute-start | bytes 196616 | tf_op jit(solution)/shard_map/ppermute | solution.py:561
  20.6 0.7 %collective-permute-done.3.refs_1_ = bf16[1,128,256]{2,1,0:T(8,128)(2,1)S(1)} collective-permute-done((bf16[1,128,256]{2,1,0:T(8,128)(2,1)S(1)}, bf16[1,128,256]{2,1,0:T(8,128)(2,1)S(1)}, u32[]{:S(2)}, u32[]{:S(2)}) %collective-permute-start.3) | collective-permute-done | bytes 65568 | tf_op jit(solution)/shard_map/ppermute | solution.py:561
  21.2 0.2 collective-permute-start.7
  21.5 1.6 %collective-permute-start.5 = (bf16[2,256,256]{2,1,0:T(8,128)(2,1)S(1)}, bf16[2,256,256]{2,1,0:T(8,128)(2,1)S(1)}, u32[]{:S(2)}, u32[]{:S(2)}) collective-permute-start(bf16[2,256,256]{2,1,0:T(8,128)(2,1)S(1)} %shard_map.50.refs_2_), channel_id=1, source_target_pairs={{0,2},{2,0},{1,3},{3,1},{4,6},{6,4},{5,7},{7,5},{8,10},{10,8},{9,1... | collective-permute-start | bytes 786440 | tf_op jit(solution)/shard_map/ppermute | solution.py:567
  23.0 1.3 %collective-permute-start.8 = (bf16[1,256,256]{2,1,0:T(8,128)(2,1)S(1)}, bf16[1,256,256]{2,1,0:T(8,128)(2,1)S(1)}, u32[]{:S(2)}, u32[]{:S(2)}) collective-permute-start(bf16[1,256,256]{2,1,0:T(8,128)(2,1)S(1)} %shard_map.53), channel_id=1, source_target_pairs={{12,0},{14,2},{13,1},{15,3},{28,16},{30,18},{29,17},{31,19}} | collective-permute-start | bytes 393224 | tf_op jit(solution)/shard_map/ppermute | solution.py:573
  24.4 1.3 %collective-permute-start.9 = (bf16[1,256,256]{2,1,0:T(8,128)(2,1)S(1)}, bf16[1,256,256]{2,1,0:T(8,128)(2,1)S(1)}, u32[]{:S(2)}, u32[]{:S(2)}) collective-permute-start(bf16[1,256,256]{2,1,0:T(8,128)(2,1)S(1)} %shard_map.54), channel_id=1, source_target_pairs={{12,2},{14,0},{13,3},{15,1},{28,18},{30,16},{29,19},{31,17}} | collective-permute-start | bytes 393224 | tf_op jit(solution)/shard_map/ppermute | solution.py:573
  25.7 3.5 %collective-permute-done.11.refs_1_ = bf16[2,8,16,512]{3,2,1,0:T(8,128)(2,1)S(1)} collective-permute-done((bf16[2,8,16,512]{3,2,1,0:T(8,128)(2,1)S(1)}, bf16[2,8,16,512]{3,2,1,0:T(8,128)(2,1)S(1)}, u32[]{:S(2)}, u32[]{:S(2)}) %collective-permute-start.11) | collective-permute-done | bytes 262176 | tf_op jit(solution)/shard_map/ppermute | solution.py:598
  29.2 0.1 shard_map.56
  29.4 0.5 %collective-permute-start.15 = (bf16[1,128,256]{2,1,0:T(8,128)(2,1)S(1)}, bf16[1,128,256]{2,1,0:T(8,128)(2,1)S(1)}, u32[]{:S(2)}, u32[]{:S(2)}) collective-permute-start(bf16[1,128,256]{2,1,0:T(8,128)(2,1)S(1)} %get-tuple-element.46), channel_id=1, source_target_pairs={{0,1},{1,0},{2,3},{3,2},{4,5},{5,4},{6,7},{7,6},{8,9},{9,8},{10,11... | collective-permute-start | bytes 196616 | tf_op jit(solution)/shard_map/ppermute | solution.py:561
  29.9 0.7 %collective-permute-done.14.refs_1_ = bf16[1,128,256]{2,1,0:T(8,128)(2,1)S(1)} collective-permute-done((bf16[1,128,256]{2,1,0:T(8,128)(2,1)S(1)}, bf16[1,128,256]{2,1,0:T(8,128)(2,1)S(1)}, u32[]{:S(2)}, u32[]{:S(2)}) %collective-permute-start.14) | collective-permute-done | bytes 65568 | tf_op jit(solution)/shard_map/ppermute | solution.py:561
  30.7 0.2 collective-permute-done.15.refs_2_
  30.8 1.6 %collective-permute-start.16 = (bf16[1,256,256]{2,1,0:T(8,128)(2,1)S(1)}, bf16[1,256,256]{2,1,0:T(8,128)(2,1)S(1)}, u32[]{:S(2)}, u32[]{:S(2)}) collective-permute-start(bf16[1,256,256]{2,1,0:T(8,128)(2,1)S(1)} %shard_map.58), channel_id=1, source_target_pairs={{0,2},{2,0},{1,3},{3,1},{4,6},{6,4},{5,7},{7,5},{8,10},{10,8},{9,1... | collective-permute-start | bytes 393224 | tf_op jit(solution)/shard_map/ppermute | solution.py:567
  32.4 0.1 shard_map.57
  32.5 0.1 collective-permute-start.12
  32.7 1.6 %collective-permute-done.8.refs_0_ = bf16[1,256,256]{2,1,0:T(8,128)(2,1)S(1)} collective-permute-done((bf16[1,256,256]{2,1,0:T(8,128)(2,1)S(1)}, bf16[1,256,256]{2,1,0:T(8,128)(2,1)S(1)}, u32[]{:S(2)}, u32[]{:S(2)}) %collective-permute-start.8) | collective-permute-done | bytes 131104 | tf_op jit(solution)/shard_map/ppermute | solution.py:573
  34.2 2.8 %collective-permute-done.9.refs_1_ = bf16[1,256,256]{2,1,0:T(8,128)(2,1)S(1)} collective-permute-done((bf16[1,256,256]{2,1,0:T(8,128)(2,1)S(1)}, bf16[1,256,256]{2,1,0:T(8,128)(2,1)S(1)}, u32[]{:S(2)}, u32[]{:S(2)}) %collective-permute-start.9) | collective-permute-done | bytes 131104 | tf_op jit(solution)/shard_map/ppermute | solution.py:573
  37.1 0.2 shard_map.55.refs_2_
  37.3 0.5 %collective-permute-start.13 = (bf16[1,64,256]{2,1,0:T(8,128)(2,1)S(1)}, bf16[1,64,256]{2,1,0:T(8,128)(2,1)S(1)}, u32[]{:S(2)}, u32[]{:S(2)}) collective-permute-start(bf16[1,64,256]{2,1,0:T(8,128)(2,1)S(1)} %get-tuple-element.43), channel_id=1, source_target_pairs={{0,1},{1,0},{2,3},{3,2},{4,5},{5,4},{6,7},{7,6},{8,9},{9,8},{10,11... | collective-permute-start | bytes 98312 | tf_op jit(solution)/shard_map/ppermute | solution.py:561
  37.8 0.2 shard_map.51.refs_0_
  38.0 0.2 shard_map.52.refs_1_
  38.2 0.4 %collective-permute-done.17.refs_7_ = f32[3,24,256]{2,1,0:T(8,128)S(1)} collective-permute-done((f32[3,24,256]{2,1,0:T(8,128)S(1)}, f32[3,24,256]{2,1,0:T(8,128)S(1)}, u32[]{:S(2)}, u32[]{:S(2)}) %collective-permute-start.17) | collective-permute-done | bytes 73760 | tf_op jit(solution)/shard_map/ppermute | solution.py:619
  38.7 0.7 %collective-permute-done.16.refs_6_ = bf16[1,256,256]{2,1,0:T(8,128)(2,1)S(1)} collective-permute-done((bf16[1,256,256]{2,1,0:T(8,128)(2,1)S(1)}, bf16[1,256,256]{2,1,0:T(8,128)(2,1)S(1)}, u32[]{:S(2)}, u32[]{:S(2)}) %collective-permute-start.16) | collective-permute-done | bytes 131104 | tf_op jit(solution)/shard_map/ppermute | solution.py:567
  39.4 1.0 %shard_map.59 = f32[3,8,32,256]{3,2,1,0:T(8,128)} custom-call(s32[1,10]{1,0:T(1,128)S(1)} %bitcast.30, f32[8,32,256]{2,1,0:T(8,128)S(1)} %shard_map.51.refs_0_, f32[8,32,256]{2,1,0:T(8,128)S(1)} %shard_map.52.refs_1_, f32[8,32,256]{2,1,0:T(8,128)S(1)} %shard_map.55.refs_2_, f32[1,256,256]{2,1,0:T(8,128)S(1)} %get-tuple-element.41.refs_3_, ...), custom_call_target="tpu_custom_call" | custom-call | tf_op jit(solution)/shard_map/pallas_call | solution.py:525
  (30 shorter events, 0.9 us)
Async XLA Ops:
  0.0 6.9 %copy-start = (bf16[1024,256]{1,0:T(8,128)(2,1)S(1)}, bf16[1024,256]{1,0:T(8,128)(2,1)}, u32[]{:S(2)}) copy-start(bf16[1024,256]{1,0:T(8,128)(2,1)} %constant.17.clone.table) | copy-start | bytes 1572868
  0.0 1.1 %copy-start.1 = (bf16[1,8,32,2,512]{4,3,2,1,0:T(2,128)(2,1)S(1)}, bf16[1,8,32,2,512]{4,3,2,1,0:T(2,128)(2,1)}, u32[]{:S(2)}) copy-start(bf16[1,8,32,2,512]{4,3,2,1,0:T(2,128)(2,1)} %source.1) | copy-start | bytes 1572868
  1.1 5.8 %copy-start.2 = (s32[1,3]{1,0:T(1,128)S(1)}, s32[1,3]{1,0:T(1,128)}, u32[]{:S(2)}) copy-start(s32[1,3]{1,0:T(1,128)} %param.5) | copy-start | bytes 40
  1.1 5.8 %copy-start.3 = (s32[1,3]{1,0:T(1,128)S(1)}, s32[1,3]{1,0:T(1,128)}, u32[]{:S(2)}) copy-start(s32[1,3]{1,0:T(1,128)} %param.6) | copy-start | bytes 40
  1.2 11.8 %collective-permute-start.2 = (bf16[2,8,16,512]{3,2,1,0:T(8,128)(2,1)S(1)}, bf16[2,8,16,512]{3,2,1,0:T(8,128)(2,1)S(1)}, u32[]{:S(2)}, u32[]{:S(2)}) collective-permute-start(bf16[2,8,16,512]{3,2,1,0:T(8,128)(2,1)S(1)} %bitcast.20), channel_id=1, source_target_pairs={{4,0},{8,4},{12,8},{0,12},{5,1},{9,5},{13,9},{1,13},{6,2},{10,6},{... | collective-permute-start | bytes 786440 | tf_op jit(solution)/shard_map/ppermute | solution.py:580
  6.3 11.1 %collective-permute-start.1 = (bf16[2,8,16,512]{3,2,1,0:T(8,128)(2,1)S(1)}, bf16[2,8,16,512]{3,2,1,0:T(8,128)(2,1)S(1)}, u32[]{:S(2)}, u32[]{:S(2)}) collective-permute-start(bf16[2,8,16,512]{3,2,1,0:T(8,128)(2,1)S(1)} %bitcast.18), channel_id=1, source_target_pairs={{4,0},{8,4},{12,8},{0,12},{5,1},{9,5},{13,9},{1,13},{6,2},{10,6},{... | collective-permute-start | bytes 786440 | tf_op jit(solution)/shard_map/ppermute | solution.py:580
  12.9 7.6 %collective-permute-start = (bf16[4,128,256]{2,1,0:T(8,128)(2,1)S(1)}, bf16[4,128,256]{2,1,0:T(8,128)(2,1)S(1)}, u32[]{:S(2)}, u32[]{:S(2)}) collective-permute-start(bf16[4,128,256]{2,1,0:T(8,128)(2,1)S(1)} %get-tuple-element.29), channel_id=1, source_target_pairs={{0,1},{1,0},{2,3},{3,2},{4,5},{5,4},{6,7},{7,6},{8,9},{9,8},{10,11... | collective-permute-start | bytes 786440 | tf_op jit(solution)/shard_map/ppermute | solution.py:561
  13.0 12.7 %collective-permute-start.10 = (bf16[2,8,16,512]{3,2,1,0:T(8,128)(2,1)S(1)}, bf16[2,8,16,512]{3,2,1,0:T(8,128)(2,1)S(1)}, u32[]{:S(2)}, u32[]{:S(2)}) collective-permute-start(bf16[2,8,16,512]{3,2,1,0:T(8,128)(2,1)S(1)} %collective-permute-done.2.part), channel_id=1, source_target_pairs={{4,0},{8,4},{5,1},{9,5},{6,2},{10,6},{7,3},{11,7},{20,16},{24,20},... | collective-permute-start | bytes 786440 | tf_op jit(solution)/shard_map/ppermute | solution.py:598
  17.5 11.7 %collective-permute-start.11 = (bf16[2,8,16,512]{3,2,1,0:T(8,128)(2,1)S(1)}, bf16[2,8,16,512]{3,2,1,0:T(8,128)(2,1)S(1)}, u32[]{:S(2)}, u32[]{:S(2)}) collective-permute-start(bf16[2,8,16,512]{3,2,1,0:T(8,128)(2,1)S(1)} %collective-permute-done.1.part), channel_id=1, source_target_pairs={{4,0},{8,4},{5,1},{9,5},{6,2},{10,6},{7,3},{11,7},{20,16},{24,20},... | collective-permute-start | bytes 786440 | tf_op jit(solution)/shard_map/ppermute | solution.py:598
  19.9 1.3 %collective-permute-start.3 = (bf16[1,128,256]{2,1,0:T(8,128)(2,1)S(1)}, bf16[1,128,256]{2,1,0:T(8,128)(2,1)S(1)}, u32[]{:S(2)}, u32[]{:S(2)}) collective-permute-start(bf16[1,128,256]{2,1,0:T(8,128)(2,1)S(1)} %get-tuple-element.34), channel_id=1, source_target_pairs={{0,1},{1,0},{2,3},{3,2},{4,5},{5,4},{6,7},{7,6},{8,9},{9,8},{10,11... | collective-permute-start | bytes 196616 | tf_op jit(solution)/shard_map/ppermute | solution.py:561
  20.0 1.4 %collective-permute-start.4 = (bf16[1,128,256]{2,1,0:T(8,128)(2,1)S(1)}, bf16[1,128,256]{2,1,0:T(8,128)(2,1)S(1)}, u32[]{:S(2)}, u32[]{:S(2)}) collective-permute-start(bf16[1,128,256]{2,1,0:T(8,128)(2,1)S(1)} %get-tuple-element.35), channel_id=1, source_target_pairs={{0,1},{1,0},{2,3},{3,2},{4,5},{5,4},{6,7},{7,6},{8,9},{9,8},{10,11... | collective-permute-start | bytes 196616 | tf_op jit(solution)/shard_map/ppermute | solution.py:561
  20.5 2.5 %collective-permute-start.6 = (bf16[1,128,256]{2,1,0:T(8,128)(2,1)S(1)}, bf16[1,128,256]{2,1,0:T(8,128)(2,1)S(1)}, u32[]{:S(2)}, u32[]{:S(2)}) collective-permute-start(bf16[1,128,256]{2,1,0:T(8,128)(2,1)S(1)} %get-tuple-element.36), channel_id=1, source_target_pairs={{0,1},{1,0},{2,3},{3,2},{4,5},{5,4},{6,7},{7,6},{8,9},{9,8},{10,11... | collective-permute-start | bytes 196616 | tf_op jit(solution)/shard_map/ppermute | solution.py:561
  21.2 1.8 %collective-permute-start.7 = (bf16[1,128,256]{2,1,0:T(8,128)(2,1)S(1)}, bf16[1,128,256]{2,1,0:T(8,128)(2,1)S(1)}, u32[]{:S(2)}, u32[]{:S(2)}) collective-permute-start(bf16[1,128,256]{2,1,0:T(8,128)(2,1)S(1)} %get-tuple-element.37), channel_id=1, source_target_pairs={{0,1},{1,0},{2,3},{3,2},{4,5},{5,4},{6,7},{7,6},{8,9},{9,8},{10,11... | collective-permute-start | bytes 196616 | tf_op jit(solution)/shard_map/ppermute | solution.py:561
  21.5 16.4 %collective-permute-start.5 = (bf16[2,256,256]{2,1,0:T(8,128)(2,1)S(1)}, bf16[2,256,256]{2,1,0:T(8,128)(2,1)S(1)}, u32[]{:S(2)}, u32[]{:S(2)}) collective-permute-start(bf16[2,256,256]{2,1,0:T(8,128)(2,1)S(1)} %shard_map.50.refs_2_), channel_id=1, source_target_pairs={{0,2},{2,0},{1,3},{3,1},{4,6},{6,4},{5,7},{7,5},{8,10},{10,8},{9,1... | collective-permute-start | bytes 786440 | tf_op jit(solution)/shard_map/ppermute | solution.py:567
  23.0 11.2 %collective-permute-start.8 = (bf16[1,256,256]{2,1,0:T(8,128)(2,1)S(1)}, bf16[1,256,256]{2,1,0:T(8,128)(2,1)S(1)}, u32[]{:S(2)}, u32[]{:S(2)}) collective-permute-start(bf16[1,256,256]{2,1,0:T(8,128)(2,1)S(1)} %shard_map.53), channel_id=1, source_target_pairs={{12,0},{14,2},{13,1},{15,3},{28,16},{30,18},{29,17},{31,19}} | collective-permute-start | bytes 393224 | tf_op jit(solution)/shard_map/ppermute | solution.py:573
  24.4 12.7 %collective-permute-start.9 = (bf16[1,256,256]{2,1,0:T(8,128)(2,1)S(1)}, bf16[1,256,256]{2,1,0:T(8,128)(2,1)S(1)}, u32[]{:S(2)}, u32[]{:S(2)}) collective-permute-start(bf16[1,256,256]{2,1,0:T(8,128)(2,1)S(1)} %shard_map.54), channel_id=1, source_target_pairs={{12,2},{14,0},{13,3},{15,1},{28,18},{30,16},{29,19},{31,17}} | collective-permute-start | bytes 393224 | tf_op jit(solution)/shard_map/ppermute | solution.py:573
  29.3 1.3 %collective-permute-start.14 = (bf16[1,128,256]{2,1,0:T(8,128)(2,1)S(1)}, bf16[1,128,256]{2,1,0:T(8,128)(2,1)S(1)}, u32[]{:S(2)}, u32[]{:S(2)}) collective-permute-start(bf16[1,128,256]{2,1,0:T(8,128)(2,1)S(1)} %get-tuple-element.45), channel_id=1, source_target_pairs={{0,1},{1,0},{2,3},{3,2},{4,5},{5,4},{6,7},{7,6},{8,9},{9,8},{10,11... | collective-permute-start | bytes 196616 | tf_op jit(solution)/shard_map/ppermute | solution.py:561
  29.4 1.4 %collective-permute-start.15 = (bf16[1,128,256]{2,1,0:T(8,128)(2,1)S(1)}, bf16[1,128,256]{2,1,0:T(8,128)(2,1)S(1)}, u32[]{:S(2)}, u32[]{:S(2)}) collective-permute-start(bf16[1,128,256]{2,1,0:T(8,128)(2,1)S(1)} %get-tuple-element.46), channel_id=1, source_target_pairs={{0,1},{1,0},{2,3},{3,2},{4,5},{5,4},{6,7},{7,6},{8,9},{9,8},{10,11... | collective-permute-start | bytes 196616 | tf_op jit(solution)/shard_map/ppermute | solution.py:561
  30.8 8.5 %collective-permute-start.16 = (bf16[1,256,256]{2,1,0:T(8,128)(2,1)S(1)}, bf16[1,256,256]{2,1,0:T(8,128)(2,1)S(1)}, u32[]{:S(2)}, u32[]{:S(2)}) collective-permute-start(bf16[1,256,256]{2,1,0:T(8,128)(2,1)S(1)} %shard_map.58), channel_id=1, source_target_pairs={{0,2},{2,0},{1,3},{3,1},{4,6},{6,4},{5,7},{7,5},{8,10},{10,8},{9,1... | collective-permute-start | bytes 393224 | tf_op jit(solution)/shard_map/ppermute | solution.py:567
  32.5 6.2 %collective-permute-start.12 = (bf16[1,192,256]{2,1,0:T(8,128)(2,1)S(1)}, bf16[1,192,256]{2,1,0:T(8,128)(2,1)S(1)}, u32[]{:S(2)}, u32[]{:S(2)}) collective-permute-start(bf16[1,192,256]{2,1,0:T(8,128)(2,1)S(1)} %get-tuple-element.42), channel_id=1, source_target_pairs={{0,1},{1,0},{2,3},{3,2},{4,5},{5,4},{6,7},{7,6},{8,9},{9,8},{10,11... | collective-permute-start | bytes 294920 | tf_op jit(solution)/shard_map/ppermute | solution.py:561
  37.2 1.3 %collective-permute-start.17 = (f32[3,24,256]{2,1,0:T(8,128)S(1)}, f32[3,24,256]{2,1,0:T(8,128)S(1)}, u32[]{:S(2)}, u32[]{:S(2)}) collective-permute-start(f32[3,24,256]{2,1,0:T(8,128)S(1)} %slice.4), channel_id=1, source_target_pairs={{0,1},{1,0},{2,3},{3,2},{4,5},{5,4},{6,7},{7,6},{8,9},{9,8},{10,11... | collective-permute-start | bytes 221192 | tf_op jit(solution)/shard_map/ppermute | solution.py:619
  37.3 1.4 %collective-permute-start.13 = (bf16[1,64,256]{2,1,0:T(8,128)(2,1)S(1)}, bf16[1,64,256]{2,1,0:T(8,128)(2,1)S(1)}, u32[]{:S(2)}, u32[]{:S(2)}) collective-permute-start(bf16[1,64,256]{2,1,0:T(8,128)(2,1)S(1)} %get-tuple-element.43), channel_id=1, source_target_pairs={{0,1},{1,0},{2,3},{3,2},{4,5},{5,4},{6,7},{7,6},{8,9},{9,8},{10,11... | collective-permute-start | bytes 98312 | tf_op jit(solution)/shard_map/ppermute | solution.py:561

commit v8 on v7

--- a/solution.py
+++ b/solution.py
@@ -585,7 +585,7 @@
     sums = (keep, over_cores(sends1))
     pieces = [add_cores([sums, own_sums], shift) for shift in range(1, days)]
     if wraps:
-        back = [to_first(add_cores([sums], shift), shift) for shift in range(days)]
+        back = [to_first(add_cores([sums], shift), shift) for shift in reversed(range(days))]
     moved = over_days(pieces)
     for step, (keep, got) in enumerate([own_sums, sums]):
         terms = [(keep, 0), got[0]] + [(piece, 1 - step) for piece in moved]

time: 40.4 us -> 39.7 us (0.983)
  waiting for transfers between devices: 12.4 us -> 4.76 us
  Pallas kernels: 10.5 us -> 17.2 us
    pallas_call x2, Pallas kernels: 0.23 us -> 5.47 us  [days_tile(): pl.pallas_call(functools.partial(days_kernel, shifts, owners, len(parts),...]
    ppermute x2, waiting for transfers between devices: 4.41 us -> 0.51 us  [to_first(): return lax.ppermute(piece, ('chan', 'day'), pairs)]
    ppermute x2, waiting for transfers between devices: 3.52 us -> 0.01 us  [on_device(): lax.ppermute(lax.optimization_barrier((part, wait))[0], 'chan', pairs)]
    pallas_call x1, Pallas kernels: 5.97 us -> 4.19 us  [own_tile(): pl.pallas_call(functools.partial(own_kernel, len(parts)), out_shape=[keep...]
    pallas_call x1, Pallas kernels: 1.13 us -> 2.9 us  [second_half_tile(): pl.pallas_call(functools.partial(second_half_kernel, can_swap, step, len(...]
    pallas_call x1, Pallas kernels: 1.52 us -> 2.85 us  [first_half_tile(): pl.pallas_call(functools.partial(first_half_kernel, can_swap, step), out_...]
    ppermute x2, waiting for transfers between devices: 0.71 us -> 0.01 us  [over_days(): lax.ppermute(piece, 'day', [(k, (k + shift) % days) for k in range(days)])]
    ppermute x2, waiting for transfers between devices: 1.68 us -> 2.13 us  [on_device(): moving = [lax.ppermute(part, 'chan', pairs) for part in halves]]
  transfers between devices with their start and end apart: 18 -> 18, of which waited for: 10 -> 8; matrix products, arithmetic and copies ran while one was open for 0% -> 0% of each run, Pallas kernels for 23% -> 41%
where the time goes in v8:
time: 39.7 us; the launch traced here: 39.5 us
  Pallas kernels  17.2 us (43%)
  starting transfers between devices  16.1 us (41%)
  waiting for transfers between devices  4.76 us (12%)
  local copies, waits for them, and re-layouts  1.26 us (3%)
    ppermute x2, starting transfers between devices, on_device(): moving = [lax.ppermute(part, 'chan', pairs) for part in halves]  5.6 us
    pallas_call x2, Pallas kernels, days_tile(): pl.pallas_call(functools.partial(days_kernel, shifts, owners, len(parts),...  5.47 us
    pallas_call x1, Pallas kernels, own_tile(): pl.pallas_call(functools.partial(own_kernel, len(parts)), out_shape=[keep...  4.19 us
    ppermute x2, starting transfers between devices, over_days(): lax.ppermute(piece, 'day', [(k, (k + shift) % days) for k in range(days)])  3.23 us
    pallas_call x1, Pallas kernels, second_half_tile(): pl.pallas_call(functools.partial(second_half_kernel, can_swap, step, len(...  2.9 us
    pallas_call x1, Pallas kernels, first_half_tile(): pl.pallas_call(functools.partial(first_half_kernel, can_swap, step), out_...  2.85 us
    ppermute x2, starting transfers between devices, to_first(): return lax.ppermute(piece, ('chan', 'day'), pairs)  2.58 us
    ppermute x2, starting transfers between devices, on_device(): lax.ppermute(lax.optimization_barrier((part, wait))[0], 'chan', pairs)  2.56 us
  transfers between devices with their start and end apart: 18, of which 8 were waited for; matrix products, arithmetic and copies ran while one was open for 0% of the time, Pallas kernels for 41%

profile of v8, /device:TPU:0, one launch (start us, length us, event | category | flops | bytes accessed | tf_op | source)
XLA Modules:
  0.0 39.5 jit_solution(6115815399771906313)
XLA Ops:
  0.0 1.1 %copy-done.1 = bf16[1,8,32,2,512]{4,3,2,1,0:T(2,128)(2,1)S(1)} copy-done((bf16[1,8,32,2,512]{4,3,2,1,0:T(2,128)(2,1)S(1)}, bf16[1,8,32,2,512]{4,3,2,1,0:T(2,128)(2,1)}, u32[]{:S(2)}) %copy-start.1) | copy-done | bytes 524312
  1.2 5.1 %collective-permute-start.2 = (bf16[2,8,16,512]{3,2,1,0:T(8,128)(2,1)S(1)}, bf16[2,8,16,512]{3,2,1,0:T(8,128)(2,1)S(1)}, u32[]{:S(2)}, u32[]{:S(2)}) collective-permute-start(bf16[2,8,16,512]{3,2,1,0:T(8,128)(2,1)S(1)} %bitcast.20), channel_id=1, source_target_pairs={{4,0},{8,4},{12,8},{0,12},{5,1},{9,5},{13,9},{1,13},{6,2},{10,6},{... | collective-permute-start | bytes 786440 | tf_op jit(solution)/shard_map/ppermute | solution.py:580
  6.3 0.5 %collective-permute-start.1 = (bf16[2,8,16,512]{3,2,1,0:T(8,128)(2,1)S(1)}, bf16[2,8,16,512]{3,2,1,0:T(8,128)(2,1)S(1)}, u32[]{:S(2)}, u32[]{:S(2)}) collective-permute-start(bf16[2,8,16,512]{3,2,1,0:T(8,128)(2,1)S(1)} %bitcast.18), channel_id=1, source_target_pairs={{4,0},{8,4},{12,8},{0,12},{5,1},{9,5},{13,9},{1,13},{6,2},{10,6},{... | collective-permute-start | bytes 786440 | tf_op jit(solution)/shard_map/ppermute | solution.py:580
  6.9 4.2 %shard_map.47 = (f32[2,256,256]{2,1,0:T(8,128)S(1)}, bf16[4,128,256]{2,1,0:T(8,128)(2,1)S(1)}, f32[3,8,32,512]{3,2,1,0:T(8,128)S(1)}) custom-call(s32[1,10]{1,0:T(1,128)S(1)} %bitcast.22, bf16[1024,256]{1,0:T(8,128)(2,1)S(1)} %copy-done, bf16[2,8,16,512]{3,2,1,0:T(8,128)(2,1)S(1)} %bitcast.21, bf16[2,8,16,512]{3,2,1,0:T(8,128)(2,1)S(1)} %bitcast.19), custom_call_target="tpu_custom_call" | custom-call | tf_op jit(solution)/shard_map/pallas_call | solution.py:329
  11.2 1.8 %collective-permute-done.2.part = bf16[2,8,16,512]{3,2,1,0:T(8,128)(2,1)S(1)} collective-permute-done((bf16[2,8,16,512]{3,2,1,0:T(8,128)(2,1)S(1)}, bf16[2,8,16,512]{3,2,1,0:T(8,128)(2,1)S(1)}, u32[]{:S(2)}, u32[]{:S(2)}) %collective-permute-start.2) | collective-permute-done | bytes 262176 | tf_op jit(solution)/shard_map/ppermute | solution.py:580
  13.0 1.3 %collective-permute-start.10 = (bf16[2,8,16,512]{3,2,1,0:T(8,128)(2,1)S(1)}, bf16[2,8,16,512]{3,2,1,0:T(8,128)(2,1)S(1)}, u32[]{:S(2)}, u32[]{:S(2)}) collective-permute-start(bf16[2,8,16,512]{3,2,1,0:T(8,128)(2,1)S(1)} %collective-permute-done.2.part), channel_id=1, source_target_pairs={{4,0},{8,4},{5,1},{9,5},{6,2},{10,6},{7,3},{11,7},{20,16},{24,20},... | collective-permute-start | bytes 786440 | tf_op jit(solution)/shard_map/ppermute | solution.py:598
  14.3 2.8 %shard_map.48 = (f32[2,128,256]{2,1,0:T(8,128)S(1)}, bf16[2,128,256]{2,1,0:T(8,128)(2,1)S(1)}) custom-call(s32[1,10]{1,0:T(1,128)S(1)} %bitcast.23, f32[3,8,32,512]{3,2,1,0:T(8,128)S(1)} %get-tuple-element.30.own_rows, bf16[1024,256]{1,0:T(8,128)(2,1)S(1)} %copy-done, bf16[2,8,16,512]{3,2,1,0:T(8,128)(2,1)S(1)} %collective-permute-done.2.part), custom_call_target="tpu_custom_call" | custom-call | tf_op jit(solution)/shard_map/pallas_call | solution.py:379
  17.2 0.3 collective-permute-done.1.part
  17.5 1.3 %collective-permute-start.11 = (bf16[2,8,16,512]{3,2,1,0:T(8,128)(2,1)S(1)}, bf16[2,8,16,512]{3,2,1,0:T(8,128)(2,1)S(1)}, u32[]{:S(2)}, u32[]{:S(2)}) collective-permute-start(bf16[2,8,16,512]{3,2,1,0:T(8,128)(2,1)S(1)} %collective-permute-done.1.part), channel_id=1, source_target_pairs={{4,0},{8,4},{5,1},{9,5},{6,2},{10,6},{7,3},{11,7},{20,16},{24,20},... | collective-permute-start | bytes 786440 | tf_op jit(solution)/shard_map/ppermute | solution.py:598
  18.8 2.9 %shard_map.49 = (f32[2,256,256]{2,1,0:T(8,128)S(1)}, bf16[1,128,256]{2,1,0:T(8,128)(2,1)S(1)}, bf16[1,128,256]{2,1,0:T(8,128)(2,1)S(1)}, bf16[1,128,256]{2,1,0:T(8,128)(2,1)S(1)}, bf16[1,128,256]{2,1,0:T(8,128)(2,1)S(1)}) custom-call(s32[1,10]{1,0:T(1,128)S(1)} %bitcast.24, f32[3,8,32,512]{3,2,1,0:T(8,128)S(1)} %get-tuple-element.30.own_rows, ...), custom_call_target="tpu_custom_call" | custom-call | tf_op jit(solution)/shard_map/pallas_call | solution.py:394
  21.8 0.5 %collective-permute-start.4 = (bf16[1,128,256]{2,1,0:T(8,128)(2,1)S(1)}, bf16[1,128,256]{2,1,0:T(8,128)(2,1)S(1)}, u32[]{:S(2)}, u32[]{:S(2)}) collective-permute-start(bf16[1,128,256]{2,1,0:T(8,128)(2,1)S(1)} %get-tuple-element.35), channel_id=1, source_target_pairs={{0,1},{1,0},{2,3},{3,2},{4,5},{5,4},{6,7},{7,6},{8,9},{9,8},{10,11... | collective-permute-start | bytes 196616 | tf_op jit(solution)/shard_map/ppermute | solution.py:561
  22.4 0.7 %collective-permute-done.3.refs_1_ = bf16[1,128,256]{2,1,0:T(8,128)(2,1)S(1)} collective-permute-done((bf16[1,128,256]{2,1,0:T(8,128)(2,1)S(1)}, bf16[1,128,256]{2,1,0:T(8,128)(2,1)S(1)}, u32[]{:S(2)}, u32[]{:S(2)}) %collective-permute-start.3) | collective-permute-done | bytes 65568 | tf_op jit(solution)/shard_map/ppermute | solution.py:561
  23.0 0.2 collective-permute-start.7
  23.2 1.5 %collective-permute-start.5 = (bf16[2,256,256]{2,1,0:T(8,128)(2,1)S(1)}, bf16[2,256,256]{2,1,0:T(8,128)(2,1)S(1)}, u32[]{:S(2)}, u32[]{:S(2)}) collective-permute-start(bf16[2,256,256]{2,1,0:T(8,128)(2,1)S(1)} %shard_map.50.refs_2_), channel_id=1, source_target_pairs={{0,2},{2,0},{1,3},{3,1},{4,6},{6,4},{5,7},{7,5},{8,10},{10,8},{9,1... | collective-permute-start | bytes 786440 | tf_op jit(solution)/shard_map/ppermute | solution.py:567
  24.8 1.3 %collective-permute-start.8 = (bf16[1,256,256]{2,1,0:T(8,128)(2,1)S(1)}, bf16[1,256,256]{2,1,0:T(8,128)(2,1)S(1)}, u32[]{:S(2)}, u32[]{:S(2)}) collective-permute-start(bf16[1,256,256]{2,1,0:T(8,128)(2,1)S(1)} %shard_map.53), channel_id=1, source_target_pairs={{12,2},{14,0},{13,3},{15,1},{28,18},{30,16},{29,19},{31,17}} | collective-permute-start | bytes 393224 | tf_op jit(solution)/shard_map/ppermute | solution.py:573
  26.2 1.3 %collective-permute-start.9 = (bf16[1,256,256]{2,1,0:T(8,128)(2,1)S(1)}, bf16[1,256,256]{2,1,0:T(8,128)(2,1)S(1)}, u32[]{:S(2)}, u32[]{:S(2)}) collective-permute-start(bf16[1,256,256]{2,1,0:T(8,128)(2,1)S(1)} %shard_map.54), channel_id=1, source_target_pairs={{12,0},{14,2},{13,1},{15,3},{28,16},{30,18},{29,17},{31,19}} | collective-permute-start | bytes 393224 | tf_op jit(solution)/shard_map/ppermute | solution.py:573
  27.5 3.0 %shard_map.56 = (f32[1,256,256]{2,1,0:T(8,128)S(1)}, bf16[1,128,256]{2,1,0:T(8,128)(2,1)S(1)}, bf16[1,128,256]{2,1,0:T(8,128)(2,1)S(1)}, f32[3,8,32,512]{3,2,1,0:T(8,128)S(1)}) custom-call(s32[1,10]{1,0:T(1,128)S(1)} %bitcast.25, f32[3,8,32,512]{3,2,1,0:T(8,128)S(1)} %get-tuple-element.30.own_rows, bf16[1024,256]{1,0:T(8,128)(2,1)S(1)} %copy-done, ...), custom_call_target="tpu_custom_call" | custom-call | tf_op jit(solution)/shard_map/pallas_call | solution.py:352
  30.5 0.1 collective-permute-start.14
  30.6 0.4 %collective-permute-start.15 = (bf16[1,128,256]{2,1,0:T(8,128)(2,1)S(1)}, bf16[1,128,256]{2,1,0:T(8,128)(2,1)S(1)}, u32[]{:S(2)}, u32[]{:S(2)}) collective-permute-start(bf16[1,128,256]{2,1,0:T(8,128)(2,1)S(1)} %get-tuple-element.46), channel_id=1, source_target_pairs={{0,1},{1,0},{2,3},{3,2},{4,5},{5,4},{6,7},{7,6},{8,9},{9,8},{10,11... | collective-permute-start | bytes 196616 | tf_op jit(solution)/shard_map/ppermute | solution.py:561
  31.1 0.7 %collective-permute-done.14.refs_1_ = bf16[1,128,256]{2,1,0:T(8,128)(2,1)S(1)} collective-permute-done((bf16[1,128,256]{2,1,0:T(8,128)(2,1)S(1)}, bf16[1,128,256]{2,1,0:T(8,128)(2,1)S(1)}, u32[]{:S(2)}, u32[]{:S(2)}) %collective-permute-start.14) | collective-permute-done | bytes 65568 | tf_op jit(solution)/shard_map/ppermute | solution.py:561
  31.8 0.2 collective-permute-done.15.refs_2_
  32.0 1.7 %collective-permute-start.16 = (bf16[1,256,256]{2,1,0:T(8,128)(2,1)S(1)}, bf16[1,256,256]{2,1,0:T(8,128)(2,1)S(1)}, u32[]{:S(2)}, u32[]{:S(2)}) collective-permute-start(bf16[1,256,256]{2,1,0:T(8,128)(2,1)S(1)} %shard_map.58), channel_id=1, source_target_pairs={{0,2},{2,0},{1,3},{3,1},{4,6},{6,4},{5,7},{7,5},{8,10},{10,8},{9,1... | collective-permute-start | bytes 393224 | tf_op jit(solution)/shard_map/ppermute | solution.py:567
  33.7 2.5 %shard_map.57 = (f32[1,256,256]{2,1,0:T(8,128)S(1)}, bf16[1,192,256]{2,1,0:T(8,128)(2,1)S(1)}, bf16[1,64,256]{2,1,0:T(8,128)(2,1)S(1)}) custom-call(s32[1,10]{1,0:T(1,128)S(1)} %bitcast.26, f32[3,8,32,512]{3,2,1,0:T(8,128)S(1)} %get-tuple-element.30.own_rows, bf16[1024,256]{1,0:T(8,128)(2,1)S(1)} %copy-done, f32[3,8,32,512]{3,2,1,0:T(8,128)S(1)} %get-tuple-element.40.refs_0_), custom_call_target="tpu_custom_call" | custom-call | tf_op jit(solution)/shard_map/pallas_call | solution.py:352
  36.2 0.1 collective-permute-start.12
  36.3 0.5 %collective-permute-done.9.refs_1_ = bf16[1,256,256]{2,1,0:T(8,128)(2,1)S(1)} collective-permute-done((bf16[1,256,256]{2,1,0:T(8,128)(2,1)S(1)}, bf16[1,256,256]{2,1,0:T(8,128)(2,1)S(1)}, u32[]{:S(2)}, u32[]{:S(2)}) %collective-permute-start.9) | collective-permute-done | bytes 131104 | tf_op jit(solution)/shard_map/ppermute | solution.py:573
  36.8 0.2 shard_map.55.refs_2_
  37.1 0.5 %collective-permute-start.13 = (bf16[1,64,256]{2,1,0:T(8,128)(2,1)S(1)}, bf16[1,64,256]{2,1,0:T(8,128)(2,1)S(1)}, u32[]{:S(2)}, u32[]{:S(2)}) collective-permute-start(bf16[1,64,256]{2,1,0:T(8,128)(2,1)S(1)} %get-tuple-element.43), channel_id=1, source_target_pairs={{0,1},{1,0},{2,3},{3,2},{4,5},{5,4},{6,7},{7,6},{8,9},{9,8},{10,11... | collective-permute-start | bytes 98312 | tf_op jit(solution)/shard_map/ppermute | solution.py:561
  37.6 0.2 shard_map.51.refs_0_
  37.7 0.2 shard_map.52.refs_1_
  37.9 0.4 %collective-permute-done.17.refs_7_ = f32[3,24,256]{2,1,0:T(8,128)S(1)} collective-permute-done((f32[3,24,256]{2,1,0:T(8,128)S(1)}, f32[3,24,256]{2,1,0:T(8,128)S(1)}, u32[]{:S(2)}, u32[]{:S(2)}) %collective-permute-start.17) | collective-permute-done | bytes 73760 | tf_op jit(solution)/shard_map/ppermute | solution.py:619
  38.3 0.1 collective-permute-done.13.refs_5_
  38.4 1.1 %shard_map.59 = f32[3,8,32,256]{3,2,1,0:T(8,128)} custom-call(s32[1,10]{1,0:T(1,128)S(1)} %bitcast.30, f32[8,32,256]{2,1,0:T(8,128)S(1)} %shard_map.51.refs_0_, f32[8,32,256]{2,1,0:T(8,128)S(1)} %shard_map.52.refs_1_, f32[8,32,256]{2,1,0:T(8,128)S(1)} %shard_map.55.refs_2_, f32[1,256,256]{2,1,0:T(8,128)S(1)} %get-tuple-element.41.refs_3_, ...), custom_call_target="tpu_custom_call" | custom-call | tf_op jit(solution)/shard_map/pallas_call | solution.py:525
  (30 shorter events, 0.7 us)
Async XLA Ops:
  0.0 6.9 %copy-start = (bf16[1024,256]{1,0:T(8,128)(2,1)S(1)}, bf16[1024,256]{1,0:T(8,128)(2,1)}, u32[]{:S(2)}) copy-start(bf16[1024,256]{1,0:T(8,128)(2,1)} %constant.17.clone.table) | copy-start | bytes 1572868
  0.0 1.1 %copy-start.1 = (bf16[1,8,32,2,512]{4,3,2,1,0:T(2,128)(2,1)S(1)}, bf16[1,8,32,2,512]{4,3,2,1,0:T(2,128)(2,1)}, u32[]{:S(2)}) copy-start(bf16[1,8,32,2,512]{4,3,2,1,0:T(2,128)(2,1)} %source.1) | copy-start | bytes 1572868
  1.1 5.8 %copy-start.2 = (s32[1,3]{1,0:T(1,128)S(1)}, s32[1,3]{1,0:T(1,128)}, u32[]{:S(2)}) copy-start(s32[1,3]{1,0:T(1,128)} %param.5) | copy-start | bytes 40
  1.1 5.8 %copy-start.3 = (s32[1,3]{1,0:T(1,128)S(1)}, s32[1,3]{1,0:T(1,128)}, u32[]{:S(2)}) copy-start(s32[1,3]{1,0:T(1,128)} %param.6) | copy-start | bytes 40
  1.2 11.8 %collective-permute-start.2 = (bf16[2,8,16,512]{3,2,1,0:T(8,128)(2,1)S(1)}, bf16[2,8,16,512]{3,2,1,0:T(8,128)(2,1)S(1)}, u32[]{:S(2)}, u32[]{:S(2)}) collective-permute-start(bf16[2,8,16,512]{3,2,1,0:T(8,128)(2,1)S(1)} %bitcast.20), channel_id=1, source_target_pairs={{4,0},{8,4},{12,8},{0,12},{5,1},{9,5},{13,9},{1,13},{6,2},{10,6},{... | collective-permute-start | bytes 786440 | tf_op jit(solution)/shard_map/ppermute | solution.py:580
  6.3 11.1 %collective-permute-start.1 = (bf16[2,8,16,512]{3,2,1,0:T(8,128)(2,1)S(1)}, bf16[2,8,16,512]{3,2,1,0:T(8,128)(2,1)S(1)}, u32[]{:S(2)}, u32[]{:S(2)}) collective-permute-start(bf16[2,8,16,512]{3,2,1,0:T(8,128)(2,1)S(1)} %bitcast.18), channel_id=1, source_target_pairs={{4,0},{8,4},{12,8},{0,12},{5,1},{9,5},{13,9},{1,13},{6,2},{10,6},{... | collective-permute-start | bytes 786440 | tf_op jit(solution)/shard_map/ppermute | solution.py:580
  11.1 11.1 %collective-permute-start = (bf16[4,128,256]{2,1,0:T(8,128)(2,1)S(1)}, bf16[4,128,256]{2,1,0:T(8,128)(2,1)S(1)}, u32[]{:S(2)}, u32[]{:S(2)}) collective-permute-start(bf16[4,128,256]{2,1,0:T(8,128)(2,1)S(1)} %get-tuple-element.29), channel_id=1, source_target_pairs={{0,1},{1,0},{2,3},{3,2},{4,5},{5,4},{6,7},{7,6},{8,9},{9,8},{10,11... | collective-permute-start | bytes 786440 | tf_op jit(solution)/shard_map/ppermute | solution.py:561
  13.0 14.4 %collective-permute-start.10 = (bf16[2,8,16,512]{3,2,1,0:T(8,128)(2,1)S(1)}, bf16[2,8,16,512]{3,2,1,0:T(8,128)(2,1)S(1)}, u32[]{:S(2)}, u32[]{:S(2)}) collective-permute-start(bf16[2,8,16,512]{3,2,1,0:T(8,128)(2,1)S(1)} %collective-permute-done.2.part), channel_id=1, source_target_pairs={{4,0},{8,4},{5,1},{9,5},{6,2},{10,6},{7,3},{11,7},{20,16},{24,20},... | collective-permute-start | bytes 786440 | tf_op jit(solution)/shard_map/ppermute | solution.py:598
  17.5 10.0 %collective-permute-start.11 = (bf16[2,8,16,512]{3,2,1,0:T(8,128)(2,1)S(1)}, bf16[2,8,16,512]{3,2,1,0:T(8,128)(2,1)S(1)}, u32[]{:S(2)}, u32[]{:S(2)}) collective-permute-start(bf16[2,8,16,512]{3,2,1,0:T(8,128)(2,1)S(1)} %collective-permute-done.1.part), channel_id=1, source_target_pairs={{4,0},{8,4},{5,1},{9,5},{6,2},{10,6},{7,3},{11,7},{20,16},{24,20},... | collective-permute-start | bytes 786440 | tf_op jit(solution)/shard_map/ppermute | solution.py:598
  21.7 1.3 %collective-permute-start.3 = (bf16[1,128,256]{2,1,0:T(8,128)(2,1)S(1)}, bf16[1,128,256]{2,1,0:T(8,128)(2,1)S(1)}, u32[]{:S(2)}, u32[]{:S(2)}) collective-permute-start(bf16[1,128,256]{2,1,0:T(8,128)(2,1)S(1)} %get-tuple-element.34), channel_id=1, source_target_pairs={{0,1},{1,0},{2,3},{3,2},{4,5},{5,4},{6,7},{7,6},{8,9},{9,8},{10,11... | collective-permute-start | bytes 196616 | tf_op jit(solution)/shard_map/ppermute | solution.py:561
  21.8 1.4 %collective-permute-start.4 = (bf16[1,128,256]{2,1,0:T(8,128)(2,1)S(1)}, bf16[1,128,256]{2,1,0:T(8,128)(2,1)S(1)}, u32[]{:S(2)}, u32[]{:S(2)}) collective-permute-start(bf16[1,128,256]{2,1,0:T(8,128)(2,1)S(1)} %get-tuple-element.35), channel_id=1, source_target_pairs={{0,1},{1,0},{2,3},{3,2},{4,5},{5,4},{6,7},{7,6},{8,9},{9,8},{10,11... | collective-permute-start | bytes 196616 | tf_op jit(solution)/shard_map/ppermute | solution.py:561
  22.3 2.5 %collective-permute-start.6 = (bf16[1,128,256]{2,1,0:T(8,128)(2,1)S(1)}, bf16[1,128,256]{2,1,0:T(8,128)(2,1)S(1)}, u32[]{:S(2)}, u32[]{:S(2)}) collective-permute-start(bf16[1,128,256]{2,1,0:T(8,128)(2,1)S(1)} %get-tuple-element.36), channel_id=1, source_target_pairs={{0,1},{1,0},{2,3},{3,2},{4,5},{5,4},{6,7},{7,6},{8,9},{9,8},{10,11... | collective-permute-start | bytes 196616 | tf_op jit(solution)/shard_map/ppermute | solution.py:561
  23.0 3.1 %collective-permute-start.7 = (bf16[1,128,256]{2,1,0:T(8,128)(2,1)S(1)}, bf16[1,128,256]{2,1,0:T(8,128)(2,1)S(1)}, u32[]{:S(2)}, u32[]{:S(2)}) collective-permute-start(bf16[1,128,256]{2,1,0:T(8,128)(2,1)S(1)} %get-tuple-element.37), channel_id=1, source_target_pairs={{0,1},{1,0},{2,3},{3,2},{4,5},{5,4},{6,7},{7,6},{8,9},{9,8},{10,11... | collective-permute-start | bytes 196616 | tf_op jit(solution)/shard_map/ppermute | solution.py:561
  23.2 14.3 %collective-permute-start.5 = (bf16[2,256,256]{2,1,0:T(8,128)(2,1)S(1)}, bf16[2,256,256]{2,1,0:T(8,128)(2,1)S(1)}, u32[]{:S(2)}, u32[]{:S(2)}) collective-permute-start(bf16[2,256,256]{2,1,0:T(8,128)(2,1)S(1)} %shard_map.50.refs_2_), channel_id=1, source_target_pairs={{0,2},{2,0},{1,3},{3,1},{4,6},{6,4},{5,7},{7,5},{8,10},{10,8},{9,1... | collective-permute-start | bytes 786440 | tf_op jit(solution)/shard_map/ppermute | solution.py:567
  24.8 11.5 %collective-permute-start.8 = (bf16[1,256,256]{2,1,0:T(8,128)(2,1)S(1)}, bf16[1,256,256]{2,1,0:T(8,128)(2,1)S(1)}, u32[]{:S(2)}, u32[]{:S(2)}) collective-permute-start(bf16[1,256,256]{2,1,0:T(8,128)(2,1)S(1)} %shard_map.53), channel_id=1, source_target_pairs={{12,2},{14,0},{13,3},{15,1},{28,18},{30,16},{29,19},{31,17}} | collective-permute-start | bytes 393224 | tf_op jit(solution)/shard_map/ppermute | solution.py:573
  26.2 10.7 %collective-permute-start.9 = (bf16[1,256,256]{2,1,0:T(8,128)(2,1)S(1)}, bf16[1,256,256]{2,1,0:T(8,128)(2,1)S(1)}, u32[]{:S(2)}, u32[]{:S(2)}) collective-permute-start(bf16[1,256,256]{2,1,0:T(8,128)(2,1)S(1)} %shard_map.54), channel_id=1, source_target_pairs={{12,0},{14,2},{13,1},{15,3},{28,16},{30,18},{29,17},{31,19}} | collective-permute-start | bytes 393224 | tf_op jit(solution)/shard_map/ppermute | solution.py:573
  30.5 1.3 %collective-permute-start.14 = (bf16[1,128,256]{2,1,0:T(8,128)(2,1)S(1)}, bf16[1,128,256]{2,1,0:T(8,128)(2,1)S(1)}, u32[]{:S(2)}, u32[]{:S(2)}) collective-permute-start(bf16[1,128,256]{2,1,0:T(8,128)(2,1)S(1)} %get-tuple-element.45), channel_id=1, source_target_pairs={{0,1},{1,0},{2,3},{3,2},{4,5},{5,4},{6,7},{7,6},{8,9},{9,8},{10,11... | collective-permute-start | bytes 196616 | tf_op jit(solution)/shard_map/ppermute | solution.py:561
  30.6 1.3 %collective-permute-start.15 = (bf16[1,128,256]{2,1,0:T(8,128)(2,1)S(1)}, bf16[1,128,256]{2,1,0:T(8,128)(2,1)S(1)}, u32[]{:S(2)}, u32[]{:S(2)}) collective-permute-start(bf16[1,128,256]{2,1,0:T(8,128)(2,1)S(1)} %get-tuple-element.46), channel_id=1, source_target_pairs={{0,1},{1,0},{2,3},{3,2},{4,5},{5,4},{6,7},{7,6},{8,9},{9,8},{10,11... | collective-permute-start | bytes 196616 | tf_op jit(solution)/shard_map/ppermute | solution.py:561
  32.0 6.4 %collective-permute-start.16 = (bf16[1,256,256]{2,1,0:T(8,128)(2,1)S(1)}, bf16[1,256,256]{2,1,0:T(8,128)(2,1)S(1)}, u32[]{:S(2)}, u32[]{:S(2)}) collective-permute-start(bf16[1,256,256]{2,1,0:T(8,128)(2,1)S(1)} %shard_map.58), channel_id=1, source_target_pairs={{0,2},{2,0},{1,3},{3,1},{4,6},{6,4},{5,7},{7,5},{8,10},{10,8},{9,1... | collective-permute-start | bytes 393224 | tf_op jit(solution)/shard_map/ppermute | solution.py:567
  36.2 2.3 %collective-permute-start.12 = (bf16[1,192,256]{2,1,0:T(8,128)(2,1)S(1)}, bf16[1,192,256]{2,1,0:T(8,128)(2,1)S(1)}, u32[]{:S(2)}, u32[]{:S(2)}) collective-permute-start(bf16[1,192,256]{2,1,0:T(8,128)(2,1)S(1)} %get-tuple-element.42), channel_id=1, source_target_pairs={{0,1},{1,0},{2,3},{3,2},{4,5},{5,4},{6,7},{7,6},{8,9},{9,8},{10,11... | collective-permute-start | bytes 294920 | tf_op jit(solution)/shard_map/ppermute | solution.py:561
  37.0 1.3 %collective-permute-start.17 = (f32[3,24,256]{2,1,0:T(8,128)S(1)}, f32[3,24,256]{2,1,0:T(8,128)S(1)}, u32[]{:S(2)}, u32[]{:S(2)}) collective-permute-start(f32[3,24,256]{2,1,0:T(8,128)S(1)} %slice.4), channel_id=1, source_target_pairs={{0,1},{1,0},{2,3},{3,2},{4,5},{5,4},{6,7},{7,6},{8,9},{9,8},{10,11... | collective-permute-start | bytes 221192 | tf_op jit(solution)/shard_map/ppermute | solution.py:619
  37.1 1.4 %collective-permute-start.13 = (bf16[1,64,256]{2,1,0:T(8,128)(2,1)S(1)}, bf16[1,64,256]{2,1,0:T(8,128)(2,1)S(1)}, u32[]{:S(2)}, u32[]{:S(2)}) collective-permute-start(bf16[1,64,256]{2,1,0:T(8,128)(2,1)S(1)} %get-tuple-element.43), channel_id=1, source_target_pairs={{0,1},{1,0},{2,3},{3,2},{4,5},{5,4},{6,7},{7,6},{8,9},{9,8},{10,11... | collective-permute-start | bytes 98312 | tf_op jit(solution)/shard_map/ppermute | solution.py:561

commit v9 on v8

--- a/solution.py
+++ b/solution.py
@@ -461,9 +461,10 @@
     return terms
 
 
-def tile_kernel(step, counts, norm_scale, scalars, *refs):
-    *terms, tile = refs
-    write_tile(scalars, step, grouped(terms, counts), tile, norm_scale)
+def tile_kernel(listed, norm_scale, scalars, *refs):
+    rest, tiles = list(refs[: -len(listed)]), refs[-len(listed) :]
+    for (step, places), tile in zip(listed, tiles):
+        write_tile(scalars, step, grouped(rest, places), tile, norm_scale)
 
 
 def flat(terms):
@@ -475,16 +476,22 @@
     return operands, places
 
 
-def finished_tile(scalars, step, terms, row_count, width, norm_scale):
-    operands, counts = flat(terms)
-    return pl.pallas_call(
-        functools.partial(tile_kernel, step, counts, norm_scale),
-        out_shape=jax.ShapeDtypeStruct((row_count, width, LAGS), jnp.float32),
+def finished_tiles(scalars, summed, row_count, width, norm_scale):
+    operands, listed = [], []
+    for step, terms in summed:
+        more, places = flat(terms)
+        operands += more
+        listed.append((step, places))
+    tile = jax.ShapeDtypeStruct((row_count, width, LAGS), jnp.float32)
+    tiles = pl.pallas_call(
+        functools.partial(tile_kernel, listed, norm_scale),
+        out_shape=[tile] * len(listed),
         in_specs=[VMEM] + [VMEM] * len(operands),
-        out_specs=VMEM,
+        out_specs=[VMEM] * len(listed),
         compiler_params=PARAMS,
         cost_estimate=FREE,
     )(scalars, *operands)
+    return [(step, tile) for (step, _), tile in zip(summed, tiles)]
 
 
 def output_kernel(ready_steps, late, after_count, norm_scale, scalars, *refs):
@@ -587,9 +594,11 @@
     if wraps:
         back = [to_first(add_cores([sums], shift), shift) for shift in reversed(range(days))]
     moved = over_days(pieces)
-    for step, (keep, got) in enumerate([own_sums, sums]):
-        terms = [(keep, 0), got[0]] + [(piece, 1 - step) for piece in moved]
-        ready.append((step, finished_tile(scalars, step, terms, row_count, width, norm_scale)))
+    summed = [
+        (step, [(keep, 0), got[0]] + [(piece, 1 - step) for piece in moved])
+        for step, (keep, got) in enumerate([own_sums, sums])
+    ]
+    ready += finished_tiles(scalars, summed, row_count, width, norm_scale)
 
     waits = [sends[0], first[0]]
     for step in range(2, steps + 1 - wraps):
@@ -613,7 +622,7 @@
         late.append((step, [(keep, 0), got] + [(piece, 0) for piece in arrived]))
     if wraps:
         terms = [(piece, 0) for piece in back]
-        hosted = finished_tile(scalars, steps, terms, row_count, width, norm_scale)
+        ((_, hosted),) = finished_tiles(scalars, [(steps, terms)], row_count, width, norm_scale)
         ready.append((steps, hosted))
         pairs = [(c, (c + 1) % cores) for c in range(cores)]
         settled = [lax.ppermute(hosted[:3, :24], "sub", pairs)]

time: 39.7 us -> 39.6 us (level)
  waiting for transfers between devices: 4.76 us -> 5.79 us
  Pallas kernels: 17.2 us -> 16.6 us
  starting transfers between devices: 16.1 us -> 15.7 us
    ppermute x2, waiting for transfers between devices: 0.51 us -> 1.44 us  [to_first(): return lax.ppermute(piece, ('chan', 'day'), pairs)]
    ppermute x2, starting transfers between devices: 3.23 us -> 2.76 us  [over_days(): lax.ppermute(piece, 'day', [(k, (k + shift) % days) for k in range(days)])]
    pallas_call x2, Pallas kernels: 5.47 us -> 5.01 us  [days_tile(): pl.pallas_call(functools.partial(days_kernel, shifts, owners, len(parts),...]
  transfers between devices with their start and end apart: 18 -> 18, of which waited for: 8 -> 9; matrix products, arithmetic and copies ran while one was open for 0% -> 0% of each run, Pallas kernels for 41% -> 39%
where the time goes in v9:
time: 39.6 us; the launch traced here: 39.5 us
  Pallas kernels  16.6 us (42%)
  starting transfers between devices  15.7 us (40%)
  waiting for transfers between devices  5.79 us (15%)
  local copies, waits for them, and re-layouts  1.26 us (3%)
    ppermute x2, starting transfers between devices, on_device(): moving = [lax.ppermute(part, 'chan', pairs) for part in halves]  5.6 us
    pallas_call x2, Pallas kernels, days_tile(): pl.pallas_call(functools.partial(days_kernel, shifts, owners, len(parts),...  5.01 us
    pallas_call x1, Pallas kernels, own_tile(): pl.pallas_call(functools.partial(own_kernel, len(parts)), out_shape=[keep...  4.19 us
    pallas_call x1, Pallas kernels, second_half_tile(): pl.pallas_call(functools.partial(second_half_kernel, can_swap, step, len(...  2.9 us
    pallas_call x1, Pallas kernels, first_half_tile(): pl.pallas_call(functools.partial(first_half_kernel, can_swap, step), out_...  2.85 us
    ppermute x2, starting transfers between devices, over_days(): lax.ppermute(piece, 'day', [(k, (k + shift) % days) for k in range(days)])  2.76 us
    ppermute x2, starting transfers between devices, to_first(): return lax.ppermute(piece, ('chan', 'day'), pairs)  2.58 us
    ppermute x2, starting transfers between devices, on_device(): lax.ppermute(lax.optimization_barrier((part, wait))[0], 'chan', pairs)  2.56 us
  transfers between devices with their start and end apart: 18, of which 9 were waited for; matrix products, arithmetic and copies ran while one was open for 0% of the time, Pallas kernels for 39%

profile of v9, /device:TPU:0, one launch (start us, length us, event | category | flops | bytes accessed | tf_op | source)
XLA Modules:
  0.0 39.5 jit_solution(362354097118903964)
XLA Ops:
  0.0 1.1 %copy-done.1 = bf16[1,8,32,2,512]{4,3,2,1,0:T(2,128)(2,1)S(1)} copy-done((bf16[1,8,32,2,512]{4,3,2,1,0:T(2,128)(2,1)S(1)}, bf16[1,8,32,2,512]{4,3,2,1,0:T(2,128)(2,1)}, u32[]{:S(2)}) %copy-start.1) | copy-done | bytes 524312
  1.2 5.1 %collective-permute-start.2 = (bf16[2,8,16,512]{3,2,1,0:T(8,128)(2,1)S(1)}, bf16[2,8,16,512]{3,2,1,0:T(8,128)(2,1)S(1)}, u32[]{:S(2)}, u32[]{:S(2)}) collective-permute-start(bf16[2,8,16,512]{3,2,1,0:T(8,128)(2,1)S(1)} %bitcast.20), channel_id=1, source_target_pairs={{4,0},{8,4},{12,8},{0,12},{5,1},{9,5},{13,9},{1,13},{6,2},{10,6},{... | collective-permute-start | bytes 786440 | tf_op jit(solution)/shard_map/ppermute | solution.py:587
  6.3 0.5 %collective-permute-start.1 = (bf16[2,8,16,512]{3,2,1,0:T(8,128)(2,1)S(1)}, bf16[2,8,16,512]{3,2,1,0:T(8,128)(2,1)S(1)}, u32[]{:S(2)}, u32[]{:S(2)}) collective-permute-start(bf16[2,8,16,512]{3,2,1,0:T(8,128)(2,1)S(1)} %bitcast.18), channel_id=1, source_target_pairs={{4,0},{8,4},{12,8},{0,12},{5,1},{9,5},{13,9},{1,13},{6,2},{10,6},{... | collective-permute-start | bytes 786440 | tf_op jit(solution)/shard_map/ppermute | solution.py:587
  6.9 4.2 %shard_map.47 = (f32[2,256,256]{2,1,0:T(8,128)S(1)}, bf16[4,128,256]{2,1,0:T(8,128)(2,1)S(1)}, f32[3,8,32,512]{3,2,1,0:T(8,128)S(1)}) custom-call(s32[1,10]{1,0:T(1,128)S(1)} %bitcast.22, bf16[1024,256]{1,0:T(8,128)(2,1)S(1)} %copy-done, bf16[2,8,16,512]{3,2,1,0:T(8,128)(2,1)S(1)} %bitcast.21, bf16[2,8,16,512]{3,2,1,0:T(8,128)(2,1)S(1)} %bitcast.19), custom_call_target="tpu_custom_call" | custom-call | tf_op jit(solution)/shard_map/pallas_call | solution.py:329
  11.2 1.8 %collective-permute-done.2.part = bf16[2,8,16,512]{3,2,1,0:T(8,128)(2,1)S(1)} collective-permute-done((bf16[2,8,16,512]{3,2,1,0:T(8,128)(2,1)S(1)}, bf16[2,8,16,512]{3,2,1,0:T(8,128)(2,1)S(1)}, u32[]{:S(2)}, u32[]{:S(2)}) %collective-permute-start.2) | collective-permute-done | bytes 262176 | tf_op jit(solution)/shard_map/ppermute | solution.py:587
  13.0 1.3 %collective-permute-start.10 = (bf16[2,8,16,512]{3,2,1,0:T(8,128)(2,1)S(1)}, bf16[2,8,16,512]{3,2,1,0:T(8,128)(2,1)S(1)}, u32[]{:S(2)}, u32[]{:S(2)}) collective-permute-start(bf16[2,8,16,512]{3,2,1,0:T(8,128)(2,1)S(1)} %collective-permute-done.2.part), channel_id=1, source_target_pairs={{4,0},{8,4},{5,1},{9,5},{6,2},{10,6},{7,3},{11,7},{20,16},{24,20},... | collective-permute-start | bytes 786440 | tf_op jit(solution)/shard_map/ppermute | solution.py:607
  14.3 2.8 %shard_map.48 = (f32[2,128,256]{2,1,0:T(8,128)S(1)}, bf16[2,128,256]{2,1,0:T(8,128)(2,1)S(1)}) custom-call(s32[1,10]{1,0:T(1,128)S(1)} %bitcast.23, f32[3,8,32,512]{3,2,1,0:T(8,128)S(1)} %get-tuple-element.32.own_rows, bf16[1024,256]{1,0:T(8,128)(2,1)S(1)} %copy-done, bf16[2,8,16,512]{3,2,1,0:T(8,128)(2,1)S(1)} %collective-permute-done.2.part), custom_call_target="tpu_custom_call" | custom-call | tf_op jit(solution)/shard_map/pallas_call | solution.py:379
  17.2 0.3 collective-permute-done.1.part
  17.5 1.3 %collective-permute-start.11 = (bf16[2,8,16,512]{3,2,1,0:T(8,128)(2,1)S(1)}, bf16[2,8,16,512]{3,2,1,0:T(8,128)(2,1)S(1)}, u32[]{:S(2)}, u32[]{:S(2)}) collective-permute-start(bf16[2,8,16,512]{3,2,1,0:T(8,128)(2,1)S(1)} %collective-permute-done.1.part), channel_id=1, source_target_pairs={{4,0},{8,4},{5,1},{9,5},{6,2},{10,6},{7,3},{11,7},{20,16},{24,20},... | collective-permute-start | bytes 786440 | tf_op jit(solution)/shard_map/ppermute | solution.py:607
  18.8 2.9 %shard_map.49 = (f32[2,256,256]{2,1,0:T(8,128)S(1)}, bf16[1,128,256]{2,1,0:T(8,128)(2,1)S(1)}, bf16[1,128,256]{2,1,0:T(8,128)(2,1)S(1)}, bf16[1,128,256]{2,1,0:T(8,128)(2,1)S(1)}, bf16[1,128,256]{2,1,0:T(8,128)(2,1)S(1)}) custom-call(s32[1,10]{1,0:T(1,128)S(1)} %bitcast.24, f32[3,8,32,512]{3,2,1,0:T(8,128)S(1)} %get-tuple-element.32.own_rows, ...), custom_call_target="tpu_custom_call" | custom-call | tf_op jit(solution)/shard_map/pallas_call | solution.py:394
  21.8 0.5 %collective-permute-start.4 = (bf16[1,128,256]{2,1,0:T(8,128)(2,1)S(1)}, bf16[1,128,256]{2,1,0:T(8,128)(2,1)S(1)}, u32[]{:S(2)}, u32[]{:S(2)}) collective-permute-start(bf16[1,128,256]{2,1,0:T(8,128)(2,1)S(1)} %get-tuple-element.37), channel_id=1, source_target_pairs={{0,1},{1,0},{2,3},{3,2},{4,5},{5,4},{6,7},{7,6},{8,9},{9,8},{10,11... | collective-permute-start | bytes 196616 | tf_op jit(solution)/shard_map/ppermute | solution.py:568
  22.4 0.7 %collective-permute-done.3.refs_1_ = bf16[1,128,256]{2,1,0:T(8,128)(2,1)S(1)} collective-permute-done((bf16[1,128,256]{2,1,0:T(8,128)(2,1)S(1)}, bf16[1,128,256]{2,1,0:T(8,128)(2,1)S(1)}, u32[]{:S(2)}, u32[]{:S(2)}) %collective-permute-start.3) | collective-permute-done | bytes 65568 | tf_op jit(solution)/shard_map/ppermute | solution.py:568
  23.0 0.2 collective-permute-start.7
  23.2 1.5 %collective-permute-start.5 = (bf16[2,256,256]{2,1,0:T(8,128)(2,1)S(1)}, bf16[2,256,256]{2,1,0:T(8,128)(2,1)S(1)}, u32[]{:S(2)}, u32[]{:S(2)}) collective-permute-start(bf16[2,256,256]{2,1,0:T(8,128)(2,1)S(1)} %shard_map.50.refs_2_), channel_id=1, source_target_pairs={{0,2},{2,0},{1,3},{3,1},{4,6},{6,4},{5,7},{7,5},{8,10},{10,8},{9,1... | collective-permute-start | bytes 786440 | tf_op jit(solution)/shard_map/ppermute | solution.py:574
  24.8 1.3 %collective-permute-start.8 = (bf16[1,256,256]{2,1,0:T(8,128)(2,1)S(1)}, bf16[1,256,256]{2,1,0:T(8,128)(2,1)S(1)}, u32[]{:S(2)}, u32[]{:S(2)}) collective-permute-start(bf16[1,256,256]{2,1,0:T(8,128)(2,1)S(1)} %shard_map.52), channel_id=1, source_target_pairs={{12,2},{14,0},{13,3},{15,1},{28,18},{30,16},{29,19},{31,17}} | collective-permute-start | bytes 393224 | tf_op jit(solution)/shard_map/ppermute | solution.py:580
  26.2 1.3 %collective-permute-start.9 = (bf16[1,256,256]{2,1,0:T(8,128)(2,1)S(1)}, bf16[1,256,256]{2,1,0:T(8,128)(2,1)S(1)}, u32[]{:S(2)}, u32[]{:S(2)}) collective-permute-start(bf16[1,256,256]{2,1,0:T(8,128)(2,1)S(1)} %shard_map.53), channel_id=1, source_target_pairs={{12,0},{14,2},{13,1},{15,3},{28,16},{30,18},{29,17},{31,19}} | collective-permute-start | bytes 393224 | tf_op jit(solution)/shard_map/ppermute | solution.py:580
  27.5 3.0 %shard_map.55 = (f32[1,256,256]{2,1,0:T(8,128)S(1)}, bf16[1,128,256]{2,1,0:T(8,128)(2,1)S(1)}, bf16[1,128,256]{2,1,0:T(8,128)(2,1)S(1)}, f32[3,8,32,512]{3,2,1,0:T(8,128)S(1)}) custom-call(s32[1,10]{1,0:T(1,128)S(1)} %bitcast.25, f32[3,8,32,512]{3,2,1,0:T(8,128)S(1)} %get-tuple-element.32.own_rows, bf16[1024,256]{1,0:T(8,128)(2,1)S(1)} %copy-done, ...), custom_call_target="tpu_custom_call" | custom-call | tf_op jit(solution)/shard_map/pallas_call | solution.py:352
  30.5 0.1 collective-permute-start.14
  30.6 0.4 %collective-permute-start.15 = (bf16[1,128,256]{2,1,0:T(8,128)(2,1)S(1)}, bf16[1,128,256]{2,1,0:T(8,128)(2,1)S(1)}, u32[]{:S(2)}, u32[]{:S(2)}) collective-permute-start(bf16[1,128,256]{2,1,0:T(8,128)(2,1)S(1)} %get-tuple-element.50), channel_id=1, source_target_pairs={{0,1},{1,0},{2,3},{3,2},{4,5},{5,4},{6,7},{7,6},{8,9},{9,8},{10,11... | collective-permute-start | bytes 196616 | tf_op jit(solution)/shard_map/ppermute | solution.py:568
  31.1 0.7 %collective-permute-done.14.refs_1_ = bf16[1,128,256]{2,1,0:T(8,128)(2,1)S(1)} collective-permute-done((bf16[1,128,256]{2,1,0:T(8,128)(2,1)S(1)}, bf16[1,128,256]{2,1,0:T(8,128)(2,1)S(1)}, u32[]{:S(2)}, u32[]{:S(2)}) %collective-permute-start.14) | collective-permute-done | bytes 65568 | tf_op jit(solution)/shard_map/ppermute | solution.py:568
  31.8 0.2 collective-permute-done.15.refs_2_
  32.0 1.2 %collective-permute-start.16 = (bf16[1,256,256]{2,1,0:T(8,128)(2,1)S(1)}, bf16[1,256,256]{2,1,0:T(8,128)(2,1)S(1)}, u32[]{:S(2)}, u32[]{:S(2)}) collective-permute-start(bf16[1,256,256]{2,1,0:T(8,128)(2,1)S(1)} %shard_map.57), channel_id=1, source_target_pairs={{0,2},{2,0},{1,3},{3,1},{4,6},{6,4},{5,7},{7,5},{8,10},{10,8},{9,1... | collective-permute-start | bytes 393224 | tf_op jit(solution)/shard_map/ppermute | solution.py:574
  33.2 2.0 %shard_map.56 = (f32[1,256,256]{2,1,0:T(8,128)S(1)}, bf16[1,192,256]{2,1,0:T(8,128)(2,1)S(1)}, bf16[1,64,256]{2,1,0:T(8,128)(2,1)S(1)}) custom-call(s32[1,10]{1,0:T(1,128)S(1)} %bitcast.26, f32[3,8,32,512]{3,2,1,0:T(8,128)S(1)} %get-tuple-element.32.own_rows, bf16[1024,256]{1,0:T(8,128)(2,1)S(1)} %copy-done, f32[3,8,32,512]{3,2,1,0:T(8,128)S(1)} %get-tuple-element.44.refs_0_), custom_call_target="tpu_custom_call" | custom-call | tf_op jit(solution)/shard_map/pallas_call | solution.py:352
  35.2 0.1 collective-permute-start.12
  35.4 0.4 collective-permute-done.8.refs_0_
  35.8 1.1 %collective-permute-done.9.refs_1_ = bf16[1,256,256]{2,1,0:T(8,128)(2,1)S(1)} collective-permute-done((bf16[1,256,256]{2,1,0:T(8,128)(2,1)S(1)}, bf16[1,256,256]{2,1,0:T(8,128)(2,1)S(1)}, u32[]{:S(2)}, u32[]{:S(2)}) %collective-permute-start.9) | collective-permute-done | bytes 131104 | tf_op jit(solution)/shard_map/ppermute | solution.py:580
  36.8 0.2 shard_map.54.refs_2_
  37.1 0.5 %collective-permute-start.13 = (bf16[1,64,256]{2,1,0:T(8,128)(2,1)S(1)}, bf16[1,64,256]{2,1,0:T(8,128)(2,1)S(1)}, u32[]{:S(2)}, u32[]{:S(2)}) collective-permute-start(bf16[1,64,256]{2,1,0:T(8,128)(2,1)S(1)} %get-tuple-element.47), channel_id=1, source_target_pairs={{0,1},{1,0},{2,3},{3,2},{4,5},{5,4},{6,7},{7,6},{8,9},{9,8},{10,11... | collective-permute-start | bytes 98312 | tf_op jit(solution)/shard_map/ppermute | solution.py:568
  37.6 0.2 shard_map.51
  37.8 0.5 %collective-permute-done.17.refs_7_ = f32[3,24,256]{2,1,0:T(8,128)S(1)} collective-permute-done((f32[3,24,256]{2,1,0:T(8,128)S(1)}, f32[3,24,256]{2,1,0:T(8,128)S(1)}, u32[]{:S(2)}, u32[]{:S(2)}) %collective-permute-start.17) | collective-permute-done | bytes 73760 | tf_op jit(solution)/shard_map/ppermute | solution.py:628
  38.3 0.1 collective-permute-done.13.refs_5_
  38.4 1.1 %shard_map.58 = f32[3,8,32,256]{3,2,1,0:T(8,128)} custom-call(s32[1,10]{1,0:T(1,128)S(1)} %bitcast.29, f32[8,32,256]{2,1,0:T(8,128)S(1)} %get-tuple-element.40.refs_0_, f32[8,32,256]{2,1,0:T(8,128)S(1)} %get-tuple-element.41.refs_1_, f32[8,32,256]{2,1,0:T(8,128)S(1)} %shard_map.54.refs_2_, f32[1,256,256]{2,1,0:T(8,128)S(1)} %get-tuple-element.45.refs_3_, ...), custom_call_target="tpu_custom_call" | custom-call | tf_op jit(solution)/shard_map/pallas_call | solution.py:532
  (29 shorter events, 0.7 us)
Async XLA Ops:
  0.0 6.9 %copy-start = (bf16[1024,256]{1,0:T(8,128)(2,1)S(1)}, bf16[1024,256]{1,0:T(8,128)(2,1)}, u32[]{:S(2)}) copy-start(bf16[1024,256]{1,0:T(8,128)(2,1)} %constant.17.clone.table) | copy-start | bytes 1572868
  0.0 1.1 %copy-start.1 = (bf16[1,8,32,2,512]{4,3,2,1,0:T(2,128)(2,1)S(1)}, bf16[1,8,32,2,512]{4,3,2,1,0:T(2,128)(2,1)}, u32[]{:S(2)}) copy-start(bf16[1,8,32,2,512]{4,3,2,1,0:T(2,128)(2,1)} %source.1) | copy-start | bytes 1572868
  1.1 5.8 %copy-start.2 = (s32[1,3]{1,0:T(1,128)S(1)}, s32[1,3]{1,0:T(1,128)}, u32[]{:S(2)}) copy-start(s32[1,3]{1,0:T(1,128)} %param.5) | copy-start | bytes 40
  1.1 5.8 %copy-start.3 = (s32[1,3]{1,0:T(1,128)S(1)}, s32[1,3]{1,0:T(1,128)}, u32[]{:S(2)}) copy-start(s32[1,3]{1,0:T(1,128)} %param.6) | copy-start | bytes 40
  1.2 11.8 %collective-permute-start.2 = (bf16[2,8,16,512]{3,2,1,0:T(8,128)(2,1)S(1)}, bf16[2,8,16,512]{3,2,1,0:T(8,128)(2,1)S(1)}, u32[]{:S(2)}, u32[]{:S(2)}) collective-permute-start(bf16[2,8,16,512]{3,2,1,0:T(8,128)(2,1)S(1)} %bitcast.20), channel_id=1, source_target_pairs={{4,0},{8,4},{12,8},{0,12},{5,1},{9,5},{13,9},{1,13},{6,2},{10,6},{... | collective-permute-start | bytes 786440 | tf_op jit(solution)/shard_map/ppermute | solution.py:587
  6.3 11.1 %collective-permute-start.1 = (bf16[2,8,16,512]{3,2,1,0:T(8,128)(2,1)S(1)}, bf16[2,8,16,512]{3,2,1,0:T(8,128)(2,1)S(1)}, u32[]{:S(2)}, u32[]{:S(2)}) collective-permute-start(bf16[2,8,16,512]{3,2,1,0:T(8,128)(2,1)S(1)} %bitcast.18), channel_id=1, source_target_pairs={{4,0},{8,4},{12,8},{0,12},{5,1},{9,5},{13,9},{1,13},{6,2},{10,6},{... | collective-permute-start | bytes 786440 | tf_op jit(solution)/shard_map/ppermute | solution.py:587
  11.1 11.1 %collective-permute-start = (bf16[4,128,256]{2,1,0:T(8,128)(2,1)S(1)}, bf16[4,128,256]{2,1,0:T(8,128)(2,1)S(1)}, u32[]{:S(2)}, u32[]{:S(2)}) collective-permute-start(bf16[4,128,256]{2,1,0:T(8,128)(2,1)S(1)} %get-tuple-element.31), channel_id=1, source_target_pairs={{0,1},{1,0},{2,3},{3,2},{4,5},{5,4},{6,7},{7,6},{8,9},{9,8},{10,11... | collective-permute-start | bytes 786440 | tf_op jit(solution)/shard_map/ppermute | solution.py:568
  13.0 14.4 %collective-permute-start.10 = (bf16[2,8,16,512]{3,2,1,0:T(8,128)(2,1)S(1)}, bf16[2,8,16,512]{3,2,1,0:T(8,128)(2,1)S(1)}, u32[]{:S(2)}, u32[]{:S(2)}) collective-permute-start(bf16[2,8,16,512]{3,2,1,0:T(8,128)(2,1)S(1)} %collective-permute-done.2.part), channel_id=1, source_target_pairs={{4,0},{8,4},{5,1},{9,5},{6,2},{10,6},{7,3},{11,7},{20,16},{24,20},... | collective-permute-start | bytes 786440 | tf_op jit(solution)/shard_map/ppermute | solution.py:607
  17.5 10.0 %collective-permute-start.11 = (bf16[2,8,16,512]{3,2,1,0:T(8,128)(2,1)S(1)}, bf16[2,8,16,512]{3,2,1,0:T(8,128)(2,1)S(1)}, u32[]{:S(2)}, u32[]{:S(2)}) collective-permute-start(bf16[2,8,16,512]{3,2,1,0:T(8,128)(2,1)S(1)} %collective-permute-done.1.part), channel_id=1, source_target_pairs={{4,0},{8,4},{5,1},{9,5},{6,2},{10,6},{7,3},{11,7},{20,16},{24,20},... | collective-permute-start | bytes 786440 | tf_op jit(solution)/shard_map/ppermute | solution.py:607
  21.7 1.3 %collective-permute-start.3 = (bf16[1,128,256]{2,1,0:T(8,128)(2,1)S(1)}, bf16[1,128,256]{2,1,0:T(8,128)(2,1)S(1)}, u32[]{:S(2)}, u32[]{:S(2)}) collective-permute-start(bf16[1,128,256]{2,1,0:T(8,128)(2,1)S(1)} %get-tuple-element.36), channel_id=1, source_target_pairs={{0,1},{1,0},{2,3},{3,2},{4,5},{5,4},{6,7},{7,6},{8,9},{9,8},{10,11... | collective-permute-start | bytes 196616 | tf_op jit(solution)/shard_map/ppermute | solution.py:568
  21.8 1.4 %collective-permute-start.4 = (bf16[1,128,256]{2,1,0:T(8,128)(2,1)S(1)}, bf16[1,128,256]{2,1,0:T(8,128)(2,1)S(1)}, u32[]{:S(2)}, u32[]{:S(2)}) collective-permute-start(bf16[1,128,256]{2,1,0:T(8,128)(2,1)S(1)} %get-tuple-element.37), channel_id=1, source_target_pairs={{0,1},{1,0},{2,3},{3,2},{4,5},{5,4},{6,7},{7,6},{8,9},{9,8},{10,11... | collective-permute-start | bytes 196616 | tf_op jit(solution)/shard_map/ppermute | solution.py:568
  22.3 2.5 %collective-permute-start.6 = (bf16[1,128,256]{2,1,0:T(8,128)(2,1)S(1)}, bf16[1,128,256]{2,1,0:T(8,128)(2,1)S(1)}, u32[]{:S(2)}, u32[]{:S(2)}) collective-permute-start(bf16[1,128,256]{2,1,0:T(8,128)(2,1)S(1)} %get-tuple-element.38), channel_id=1, source_target_pairs={{0,1},{1,0},{2,3},{3,2},{4,5},{5,4},{6,7},{7,6},{8,9},{9,8},{10,11... | collective-permute-start | bytes 196616 | tf_op jit(solution)/shard_map/ppermute | solution.py:568
  23.0 3.1 %collective-permute-start.7 = (bf16[1,128,256]{2,1,0:T(8,128)(2,1)S(1)}, bf16[1,128,256]{2,1,0:T(8,128)(2,1)S(1)}, u32[]{:S(2)}, u32[]{:S(2)}) collective-permute-start(bf16[1,128,256]{2,1,0:T(8,128)(2,1)S(1)} %get-tuple-element.39), channel_id=1, source_target_pairs={{0,1},{1,0},{2,3},{3,2},{4,5},{5,4},{6,7},{7,6},{8,9},{9,8},{10,11... | collective-permute-start | bytes 196616 | tf_op jit(solution)/shard_map/ppermute | solution.py:568
  23.2 14.3 %collective-permute-start.5 = (bf16[2,256,256]{2,1,0:T(8,128)(2,1)S(1)}, bf16[2,256,256]{2,1,0:T(8,128)(2,1)S(1)}, u32[]{:S(2)}, u32[]{:S(2)}) collective-permute-start(bf16[2,256,256]{2,1,0:T(8,128)(2,1)S(1)} %shard_map.50.refs_2_), channel_id=1, source_target_pairs={{0,2},{2,0},{1,3},{3,1},{4,6},{6,4},{5,7},{7,5},{8,10},{10,8},{9,1... | collective-permute-start | bytes 786440 | tf_op jit(solution)/shard_map/ppermute | solution.py:574
  24.8 10.9 %collective-permute-start.8 = (bf16[1,256,256]{2,1,0:T(8,128)(2,1)S(1)}, bf16[1,256,256]{2,1,0:T(8,128)(2,1)S(1)}, u32[]{:S(2)}, u32[]{:S(2)}) collective-permute-start(bf16[1,256,256]{2,1,0:T(8,128)(2,1)S(1)} %shard_map.52), channel_id=1, source_target_pairs={{12,2},{14,0},{13,3},{15,1},{28,18},{30,16},{29,19},{31,17}} | collective-permute-start | bytes 393224 | tf_op jit(solution)/shard_map/ppermute | solution.py:580
  26.2 10.7 %collective-permute-start.9 = (bf16[1,256,256]{2,1,0:T(8,128)(2,1)S(1)}, bf16[1,256,256]{2,1,0:T(8,128)(2,1)S(1)}, u32[]{:S(2)}, u32[]{:S(2)}) collective-permute-start(bf16[1,256,256]{2,1,0:T(8,128)(2,1)S(1)} %shard_map.53), channel_id=1, source_target_pairs={{12,0},{14,2},{13,1},{15,3},{28,16},{30,18},{29,17},{31,19}} | collective-permute-start | bytes 393224 | tf_op jit(solution)/shard_map/ppermute | solution.py:580
  30.5 1.3 %collective-permute-start.14 = (bf16[1,128,256]{2,1,0:T(8,128)(2,1)S(1)}, bf16[1,128,256]{2,1,0:T(8,128)(2,1)S(1)}, u32[]{:S(2)}, u32[]{:S(2)}) collective-permute-start(bf16[1,128,256]{2,1,0:T(8,128)(2,1)S(1)} %get-tuple-element.49), channel_id=1, source_target_pairs={{0,1},{1,0},{2,3},{3,2},{4,5},{5,4},{6,7},{7,6},{8,9},{9,8},{10,11... | collective-permute-start | bytes 196616 | tf_op jit(solution)/shard_map/ppermute | solution.py:568
  30.6 1.3 %collective-permute-start.15 = (bf16[1,128,256]{2,1,0:T(8,128)(2,1)S(1)}, bf16[1,128,256]{2,1,0:T(8,128)(2,1)S(1)}, u32[]{:S(2)}, u32[]{:S(2)}) collective-permute-start(bf16[1,128,256]{2,1,0:T(8,128)(2,1)S(1)} %get-tuple-element.50), channel_id=1, source_target_pairs={{0,1},{1,0},{2,3},{3,2},{4,5},{5,4},{6,7},{7,6},{8,9},{9,8},{10,11... | collective-permute-start | bytes 196616 | tf_op jit(solution)/shard_map/ppermute | solution.py:568
  32.0 6.4 %collective-permute-start.16 = (bf16[1,256,256]{2,1,0:T(8,128)(2,1)S(1)}, bf16[1,256,256]{2,1,0:T(8,128)(2,1)S(1)}, u32[]{:S(2)}, u32[]{:S(2)}) collective-permute-start(bf16[1,256,256]{2,1,0:T(8,128)(2,1)S(1)} %shard_map.57), channel_id=1, source_target_pairs={{0,2},{2,0},{1,3},{3,1},{4,6},{6,4},{5,7},{7,5},{8,10},{10,8},{9,1... | collective-permute-start | bytes 393224 | tf_op jit(solution)/shard_map/ppermute | solution.py:574
  35.2 3.2 %collective-permute-start.12 = (bf16[1,192,256]{2,1,0:T(8,128)(2,1)S(1)}, bf16[1,192,256]{2,1,0:T(8,128)(2,1)S(1)}, u32[]{:S(2)}, u32[]{:S(2)}) collective-permute-start(bf16[1,192,256]{2,1,0:T(8,128)(2,1)S(1)} %get-tuple-element.46), channel_id=1, source_target_pairs={{0,1},{1,0},{2,3},{3,2},{4,5},{5,4},{6,7},{7,6},{8,9},{9,8},{10,11... | collective-permute-start | bytes 294920 | tf_op jit(solution)/shard_map/ppermute | solution.py:568
  37.0 1.3 %collective-permute-start.17 = (f32[3,24,256]{2,1,0:T(8,128)S(1)}, f32[3,24,256]{2,1,0:T(8,128)S(1)}, u32[]{:S(2)}, u32[]{:S(2)}) collective-permute-start(f32[3,24,256]{2,1,0:T(8,128)S(1)} %slice.4), channel_id=1, source_target_pairs={{0,1},{1,0},{2,3},{3,2},{4,5},{5,4},{6,7},{7,6},{8,9},{9,8},{10,11... | collective-permute-start | bytes 221192 | tf_op jit(solution)/shard_map/ppermute | solution.py:628
  37.1 1.4 %collective-permute-start.13 = (bf16[1,64,256]{2,1,0:T(8,128)(2,1)S(1)}, bf16[1,64,256]{2,1,0:T(8,128)(2,1)S(1)}, u32[]{:S(2)}, u32[]{:S(2)}) collective-permute-start(bf16[1,64,256]{2,1,0:T(8,128)(2,1)S(1)} %get-tuple-element.47), channel_id=1, source_target_pairs={{0,1},{1,0},{2,3},{3,2},{4,5},{5,4},{6,7},{7,6},{8,9},{9,8},{10,11... | collective-permute-start | bytes 98312 | tf_op jit(solution)/shard_map/ppermute | solution.py:568
